TPU v7x, 32 devices: a whole 2x2x4 slice. The times are simulated.
32 devices in a mesh: grp: 4 (over y, x), tok: 8 (over z, core).
Axes of the slice: x: 2, y: 2, z: 4, core: 2. Of those that a mesh axis runs over, the one named last changes fastest.
Arguments:
- hidden_in: bfloat16 [4096, 960], P(('grp', 'tok')), may hold values from -6 to 6
- cotangent: bfloat16 [4096, 960], P(('grp', 'tok')), may hold values from -6 to 6
- lengths: int32 [4, 3], P('grp'), may hold values from 1 to 512, 1024 in all within a row
- active: int32 [3, 4096], P(None, ('grp', 'tok')), may hold values from 0 to 1, as said below
- norm_attn: bfloat16 [960], P('tok'), may hold values from 0.5 to 1.5
- w_query: bfloat16 [960, 960], P('tok'), may hold values from -0.1875 to 0.1875
- w_key: bfloat16 [960, 320], P('tok'), may hold values from -0.1875 to 0.1875
- w_value: bfloat16 [960, 320], P('tok'), may hold values from -0.1875 to 0.1875
- w_out: bfloat16 [960, 960], P('tok'), may hold values from -0.75 to 0.75
- norm_mlp: bfloat16 [960], P('tok'), may hold values from 0.5 to 1.5
- w_gate: bfloat16 [960, 2560], P('tok'), may hold values from -0.1875 to 0.1875
- w_up: bfloat16 [960, 2560], P('tok'), may hold values from -0.1875 to 0.1875
- w_down: bfloat16 [2560, 960], P('tok'), may hold values from -0.125 to 0.125
- w_router: bfloat16 [960], P('tok'), may hold values from -0.1875 to 0.1875
Outputs:
- output: bfloat16 [4096, 960], P(('grp', 'tok'))
- grad_hidden: float32 [4096, 960], P(('grp', 'tok'))
- grad_norm_attn: float32 [960], replicated
- grad_w_query: float32 [960, 960], replicated
- grad_w_key: float32 [960, 320], replicated
- grad_w_value: float32 [960, 320], replicated
- grad_w_out: float32 [960, 960], replicated
- grad_norm_mlp: float32 [960], replicated
- grad_w_gate: float32 [960, 2560], replicated
- grad_w_up: float32 [960, 2560], replicated
- grad_w_down: float32 [2560, 960], replicated
- grad_w_router: float32 [960], replicated
Inputs may be any that keep to these rules, and one draw needn't show every extreme that they name: `active`: at recursion r exactly (3 - r) * 256 tokens of each group are 1, and a token that is 1 at recursion r is 1 at every earlier recursion. `lengths`: each row sums to 1024 and its largest entry is exactly 512.
All inputs are finite; a program needn't handle non-finite values.
Results may differ from a plain program's by a relative error of at most 0.024.
Values may be sent and summed in bfloat16 or wider, within the bound.
A program may use at most 320 MiB of HBM per device.

v0:
```python
import jax
import jax.numpy as jnp
from jax import lax
from jax.sharding import PartitionSpec as P

H = 15
KVH = 5
HD = 64
RECUR = 3
SPAN = 16


epsilon = 1e-05
theta = 10000.0
masked = -1000000000.0
highest = lax.Precision.HIGHEST


def from_behind(block, axis, distance):
    devices = range(lax.axis_size(axis))
    route = [(i - distance, i) for i in devices if i - distance in devices]
    return lax.ppermute(block, axis, route)


def matmul(left, right):
    return jnp.dot(left, right, preferred_element_type=jnp.float32)


def matmul_tn(left, right):
    return lax.dot_general(
        left, right, (((0,), (0,)), ((), ())), preferred_element_type=jnp.float32
    )


def matmul_nt(left, right):
    return lax.dot_general(
        left, right, (((1,), (1,)), ((), ())), preferred_element_type=jnp.float32
    )


def norm_forward(values_in, gain_vec):
    inverse_rms = lax.rsqrt(jnp.mean(values_in * values_in, axis=-1, keepdims=True) + epsilon)
    scaled = values_in * inverse_rms
    return (scaled * gain_vec, scaled, inverse_rms)


def norm_backward(grad_in, scaled, inverse_rms, gain_vec):
    grad_scaled = grad_in * gain_vec
    inner = jnp.mean(grad_scaled * scaled, axis=-1, keepdims=True)
    return (inverse_rms * (grad_scaled - scaled * inner), jnp.sum(grad_in * scaled, axis=0))


def segment_of(lengths_row, global_rows):
    ends_at = jnp.cumsum(lengths_row)
    return jnp.sum((global_rows[:, None] >= ends_at[None, :]).astype(jnp.int32), axis=1)


def position_of(lengths_row, global_rows, segments):
    ends_at = jnp.cumsum(lengths_row)
    starts_at = ends_at - lengths_row
    picked = segments[:, None] == jnp.arange(lengths_row.shape[0], dtype=jnp.int32)[None, :]
    return global_rows - jnp.sum(jnp.where(picked, starts_at[None, :], 0), axis=1)


def rotary_tables(positions):
    half_dim = HD // 2
    inverse = jnp.power(theta, -jnp.arange(half_dim, dtype=jnp.float32) * (2.0 / HD))
    angle = positions.astype(jnp.float32)[..., None] * inverse
    return (jnp.cos(angle), jnp.sin(angle))


def rotate(tensor, cosine_table, sine_table):
    half_dim = tensor.shape[-1] // 2
    first_half = tensor[..., :half_dim]
    second_half = tensor[..., half_dim:]
    cos_b = cosine_table[..., None, :]
    sin_b = sine_table[..., None, :]
    return jnp.concatenate(
        [first_half * cos_b - second_half * sin_b, second_half * cos_b + first_half * sin_b],
        axis=-1,
    )


def rotate_back(gradient, cosine_table, sine_table):
    half_dim = gradient.shape[-1] // 2
    first_half = gradient[..., :half_dim]
    second_half = gradient[..., half_dim:]
    cos_b = cosine_table[..., None, :]
    sin_b = sine_table[..., None, :]
    return jnp.concatenate(
        [first_half * cos_b + second_half * sin_b, second_half * cos_b - first_half * sin_b],
        axis=-1,
    )


def head_layout(queries, keys_all, values_all):
    row_count = queries.shape[0]
    key_count = keys_all.shape[0]
    per_group = H // KVH
    query_heads = jnp.transpose(queries.reshape(row_count, KVH, per_group, HD), (1, 0, 2, 3))
    key_heads = jnp.transpose(keys_all.reshape(key_count, KVH, HD), (1, 0, 2))
    value_heads = jnp.transpose(values_all.reshape(key_count, KVH, HD), (1, 0, 2))
    return (query_heads, key_heads, value_heads)


def attend(queries, keys_all, values_all, allowed):
    row_count = queries.shape[0]
    score_scale = HD ** (-0.5)
    query_heads, key_heads, value_heads = head_layout(queries, keys_all, values_all)

    def one_head(operands):
        query_h, key_h, value_h = operands
        scores = (
            jnp.einsum("rgd,kd->grk", query_h, key_h, preferred_element_type=jnp.float32)
            * score_scale
        )
        scores = jnp.where(allowed[None], scores, masked)
        largest = jnp.max(scores, axis=-1, keepdims=True)
        exponent = jnp.exp(scores - largest)
        totals = jnp.sum(exponent, axis=-1, keepdims=True)
        probs_low = (exponent / totals).astype(jnp.bfloat16)
        mixed_h = jnp.einsum("grk,kd->rgd", probs_low, value_h, preferred_element_type=jnp.float32)
        return (mixed_h.astype(jnp.bfloat16), (largest + jnp.log(totals))[..., 0])

    mixed_heads, log_totals = lax.map(one_head, (query_heads, key_heads, value_heads))
    mixed_rows = jnp.transpose(mixed_heads, (1, 0, 2, 3)).reshape(row_count, H * HD)
    return (mixed_rows, log_totals)


def attend_back(queries, keys_all, values_all, allowed, log_totals, grad_mixed):
    row_count = queries.shape[0]
    key_count = keys_all.shape[0]
    per_group = H // KVH
    score_scale = HD ** (-0.5)
    query_heads, key_heads, value_heads = head_layout(queries, keys_all, values_all)
    grad_heads = jnp.transpose(grad_mixed.reshape(row_count, KVH, per_group, HD), (1, 0, 2, 3))

    def one_head(operands):
        query_h, key_h, value_h, grad_h, log_h = operands
        scores = (
            jnp.einsum("rgd,kd->grk", query_h, key_h, preferred_element_type=jnp.float32)
            * score_scale
        )
        scores = jnp.where(allowed[None], scores, masked)
        probs = jnp.exp(scores - log_h[..., None])
        grad_value_h = jnp.einsum(
            "grk,rgd->kd", probs.astype(jnp.bfloat16), grad_h, preferred_element_type=jnp.float32
        )
        grad_probs = jnp.einsum("rgd,kd->grk", grad_h, value_h, preferred_element_type=jnp.float32)
        grad_scores = (
            probs * (grad_probs - jnp.sum(probs * grad_probs, axis=-1, keepdims=True))
        ).astype(jnp.bfloat16)
        grad_query_h = (
            jnp.einsum("grk,kd->rgd", grad_scores, key_h, preferred_element_type=jnp.float32)
            * score_scale
        )
        grad_key_h = (
            jnp.einsum("grk,rgd->kd", grad_scores, query_h, preferred_element_type=jnp.float32)
            * score_scale
        )
        return (grad_query_h, grad_key_h, grad_value_h)

    grad_q_heads, grad_k_heads, grad_v_heads = lax.map(
        one_head, (query_heads, key_heads, value_heads, grad_heads, log_totals)
    )
    grad_queries = jnp.transpose(grad_q_heads, (1, 0, 2, 3)).reshape(row_count, H * HD)
    grad_keys = jnp.transpose(grad_k_heads, (1, 0, 2)).reshape(key_count, KVH * HD)
    grad_values = jnp.transpose(grad_v_heads, (1, 0, 2)).reshape(key_count, KVH * HD)
    return (grad_queries, grad_keys, grad_values)


def attention_front(hidden_state, live_int, weights, context, pieces):
    lengths_row, global_rows, cosine_table, sine_table, segment_rows, tok_dev, nback = context
    normed, scaled_one, inverse_one = norm_forward(hidden_state, weights[0].astype(jnp.float32))
    normed_low = normed.astype(jnp.bfloat16)
    row_count = hidden_state.shape[0]
    queries = rotate(
        matmul(normed_low, weights[1]).reshape(row_count, H, HD), cosine_table, sine_table
    )
    queries = queries.astype(jnp.bfloat16).reshape(row_count, H * HD)
    keys_own = rotate(
        matmul(normed_low, weights[2]).reshape(row_count, KVH, HD), cosine_table, sine_table
    )
    keys_own = keys_own.astype(jnp.bfloat16).reshape(row_count, KVH * HD)
    values_own = matmul(normed_low, weights[3]).astype(jnp.bfloat16)
    live_low = live_int.astype(jnp.bfloat16)
    pieces = [
        from_behind((keys_own, values_own, live_low), "tok", distance)
        for distance in range(1, nback + 1)
    ]
    keys_all = jnp.concatenate([keys_own] + [one_piece[0] for one_piece in pieces], axis=0)
    values_all = jnp.concatenate([values_own] + [one_piece[1] for one_piece in pieces], axis=0)
    live_all = jnp.concatenate([live_low] + [one_piece[2] for one_piece in pieces], axis=0)
    global_keys = jnp.concatenate(
        [global_rows - distance * tok_dev for distance in range(nback + 1)]
    )
    segment_keys = segment_of(lengths_row, global_keys)
    allowed = (
        (segment_rows[:, None] == segment_keys[None, :])
        & (global_keys[None, :] <= global_rows[:, None])
        & (live_all[None, :] > 0)
    )
    mixed_rows, log_totals = attend(queries, keys_all, values_all, allowed)
    attn_out = matmul(mixed_rows, weights[4])
    middle = hidden_state + attn_out
    normed_two, scaled_two, inverse_two = norm_forward(middle, weights[5].astype(jnp.float32))
    return (
        normed_low,
        scaled_one,
        inverse_one,
        queries,
        keys_all,
        values_all,
        allowed,
        mixed_rows,
        log_totals,
        attn_out,
        normed_two.astype(jnp.bfloat16),
        scaled_two,
        inverse_two,
        pieces,
    )


def ffn_forward(rows_in, w_gate, w_up, w_down):
    gate_pre = matmul(rows_in, w_gate)
    up_pre = matmul(rows_in, w_up)
    hidden_low = (jax.nn.silu(gate_pre) * up_pre).astype(jnp.bfloat16)
    return matmul(hidden_low, w_down).astype(jnp.bfloat16)


def ffn_backward(rows_in, grad_rows, w_gate, w_up, w_down):
    gate_pre = matmul(rows_in, w_gate)
    up_pre = matmul(rows_in, w_up)
    sigmoid_gate = jax.nn.sigmoid(gate_pre)
    silu_gate = jax.nn.silu(gate_pre)
    hidden_low = (silu_gate * up_pre).astype(jnp.bfloat16)
    grad_down = matmul_tn(hidden_low, grad_rows)
    grad_hidden = matmul_nt(grad_rows, w_down)
    grad_up_low = (grad_hidden * silu_gate).astype(jnp.bfloat16)
    grad_gate_low = (
        grad_hidden * up_pre * (sigmoid_gate * (1.0 + gate_pre * (1.0 - sigmoid_gate)))
    ).astype(jnp.bfloat16)
    grad_gate = matmul_tn(rows_in, grad_gate_low)
    grad_up = matmul_tn(rows_in, grad_up_low)
    grad_input = (matmul_nt(grad_gate_low, w_gate) + matmul_nt(grad_up_low, w_up)).astype(
        jnp.bfloat16
    )
    return (grad_input, grad_gate, grad_up, grad_down)


def feed_forward(normed_two, weights):
    mlp_low = ffn_forward(normed_two, weights[6], weights[7], weights[8])
    return mlp_low


def feed_back(normed_two, grad_mlp, weights):
    grad_normed, grad_gate, grad_up, grad_down = ffn_backward(
        normed_two, grad_mlp, weights[6], weights[7], weights[8]
    )
    return (grad_normed, grad_gate, grad_up, grad_down)


def recursion_forward(hidden_state, live_int, weights, context):
    front = attention_front(hidden_state, live_int, weights, context, None)
    mlp_low = feed_forward(front[10], weights)
    router_gate = jax.nn.sigmoid(
        jnp.dot(hidden_state, weights[9].astype(jnp.float32), precision=highest)
    )
    factor = live_int.astype(jnp.float32) * router_gate
    updated = hidden_state + factor[:, None] * (front[9] + mlp_low.astype(jnp.float32))
    return (updated, front[13], mlp_low)


def recursion_backward(
    hidden_state, live_int, weights, context, pieces, mlp_low, grad_after, grads
):
    (
        normed_low,
        scaled_one,
        inverse_one,
        queries,
        keys_all,
        values_all,
        allowed,
        mixed_rows,
        log_totals,
        attn_out,
        normed_two,
        scaled_two,
        inverse_two,
        pieces,
    ) = attention_front(hidden_state, live_int, weights, context, pieces)
    lengths_row, global_rows, cosine_table, sine_table, segment_rows, tok_dev, nback = context
    live_f = live_int.astype(jnp.float32)
    router_vec = weights[9].astype(jnp.float32)
    router_gate = jax.nn.sigmoid(jnp.dot(hidden_state, router_vec, precision=highest))
    branch_sum = attn_out + mlp_low.astype(jnp.float32)
    grad_branch = (live_f * router_gate)[:, None] * grad_after
    grad_logit = (
        live_f * jnp.sum(branch_sum * grad_after, axis=1) * router_gate * (1.0 - router_gate)
    )
    grad_router = jnp.dot(grad_logit, hidden_state, precision=highest)
    grad_state = grad_after + grad_logit[:, None] * router_vec[None, :]
    grad_normed_two, grad_gate, grad_up, grad_down = feed_back(
        normed_two, grad_branch.astype(jnp.bfloat16), weights
    )
    grad_middle, grad_gain_two = norm_backward(
        grad_normed_two.astype(jnp.float32), scaled_two, inverse_two, weights[5].astype(jnp.float32)
    )
    grad_state = grad_state + grad_middle
    grad_attn = (grad_branch + grad_middle).astype(jnp.bfloat16)
    grad_out = matmul_tn(mixed_rows, grad_attn)
    grad_mixed = matmul_nt(grad_attn, weights[4]).astype(jnp.bfloat16)
    grad_queries, grad_keys, grad_values = attend_back(
        queries, keys_all, values_all, allowed, log_totals, grad_mixed
    )
    row_count = hidden_state.shape[0]
    keys_home = grad_keys[:row_count]
    values_home = grad_values[:row_count]
    for distance in range(1, nback + 1):
        returned = (
            from_behind(
                grad_keys[distance * row_count : (distance + 1) * row_count].astype(jnp.bfloat16),
                "tok",
                -distance,
            ).astype(jnp.float32),
            from_behind(
                grad_values[distance * row_count : (distance + 1) * row_count].astype(jnp.bfloat16),
                "tok",
                -distance,
            ).astype(jnp.float32),
        )
        keys_home = keys_home + returned[0]
        values_home = values_home + returned[1]
    grad_q_low = (
        rotate_back(grad_queries.reshape(row_count, H, HD), cosine_table, sine_table)
        .reshape(row_count, H * HD)
        .astype(jnp.bfloat16)
    )
    grad_k_low = (
        rotate_back(keys_home.reshape(row_count, KVH, HD), cosine_table, sine_table)
        .reshape(row_count, KVH * HD)
        .astype(jnp.bfloat16)
    )
    grad_v_low = values_home.astype(jnp.bfloat16)
    grad_query_w = matmul_tn(normed_low, grad_q_low)
    grad_key_w = matmul_tn(normed_low, grad_k_low)
    grad_value_w = matmul_tn(normed_low, grad_v_low)
    grad_normed = (
        matmul_nt(grad_q_low, weights[1])
        + matmul_nt(grad_k_low, weights[2])
        + matmul_nt(grad_v_low, weights[3])
    )
    grad_input, grad_gain_one = norm_backward(
        grad_normed, scaled_one, inverse_one, weights[0].astype(jnp.float32)
    )
    grad_state = grad_state + grad_input
    adding = (
        grad_gain_one,
        grad_query_w,
        grad_key_w,
        grad_value_w,
        grad_out,
        grad_gain_two,
        grad_gate,
        grad_up,
        grad_down,
        grad_router,
    )
    return (grad_state, tuple((running + extra for running, extra in zip(grads, adding))))


def on_device(
    hidden_in,
    cotangent,
    lengths,
    active,
    norm_attn,
    w_query,
    w_key,
    w_value,
    w_out,
    norm_mlp,
    w_gate,
    w_up,
    w_down,
    w_router,
):
    n_tok = lax.axis_size("tok")
    me_index = lax.axis_index("tok")
    tok_dev = hidden_in.shape[0]
    nback = min(SPAN, n_tok // 2)
    shards = (norm_attn, w_query, w_key, w_value, w_out, norm_mlp, w_gate, w_up, w_down, w_router)
    weights = (
        lax.all_gather(shards[0], "tok", axis=0, tiled=True),
        lax.all_gather(shards[1], "tok", axis=0, tiled=True),
        lax.all_gather(shards[2], "tok", axis=0, tiled=True),
        lax.all_gather(shards[3], "tok", axis=0, tiled=True),
        lax.all_gather(shards[4], "tok", axis=0, tiled=True),
        lax.all_gather(shards[5], "tok", axis=0, tiled=True),
        lax.all_gather(shards[6], "tok", axis=0, tiled=True),
        lax.all_gather(shards[7], "tok", axis=0, tiled=True),
        lax.all_gather(shards[8], "tok", axis=0, tiled=True),
        lax.all_gather(shards[9], "tok", axis=0, tiled=True),
    )
    lengths_row = lengths[0]
    global_rows = me_index * tok_dev + jnp.arange(tok_dev, dtype=jnp.int32)
    segment_rows = segment_of(lengths_row, global_rows)
    cosine_table, sine_table = rotary_tables(position_of(lengths_row, global_rows, segment_rows))
    context = (lengths_row, global_rows, cosine_table, sine_table, segment_rows, tok_dev, nback)
    hidden_state = hidden_in.astype(jnp.float32)
    inputs_kept = []
    pieces_kept = []
    mlp_kept = []
    for each_step in range(RECUR):
        inputs_kept.append(hidden_state)
        hidden_state, pieces, mlp_low = recursion_forward(
            hidden_state, active[each_step], weights, context
        )
        pieces_kept.append(pieces)
        mlp_kept.append(mlp_low)
    back_weights = (
        lax.all_gather(shards[0], "tok", axis=0, tiled=True),
        lax.all_gather(shards[1], "tok", axis=0, tiled=True),
        lax.all_gather(shards[2], "tok", axis=0, tiled=True),
        lax.all_gather(shards[3], "tok", axis=0, tiled=True),
        lax.all_gather(shards[4], "tok", axis=0, tiled=True),
        lax.all_gather(shards[5], "tok", axis=0, tiled=True),
        lax.all_gather(shards[6], "tok", axis=0, tiled=True),
        lax.all_gather(shards[7], "tok", axis=0, tiled=True),
        lax.all_gather(shards[8], "tok", axis=0, tiled=True),
        lax.all_gather(shards[9], "tok", axis=0, tiled=True),
    )
    grads = tuple((jnp.zeros(matrix.shape, jnp.float32) for matrix in back_weights))
    grad_state = cotangent.astype(jnp.float32)
    for each_step in reversed(range(RECUR)):
        grad_state, grads = recursion_backward(
            inputs_kept[each_step],
            active[each_step],
            back_weights,
            context,
            None,
            mlp_kept[each_step],
            grad_state,
            grads,
        )
    summed = lax.psum(grads, ("grp", "tok"))
    return (
        hidden_state.astype(jnp.bfloat16),
        grad_state,
        summed[0],
        summed[1],
        summed[2],
        summed[3],
        summed[4],
        summed[5],
        summed[6],
        summed[7],
        summed[8],
        summed[9],
    )


def solution(mesh):
    placed = (
        P(("grp", "tok"), None),
        P(("grp", "tok"), None),
        P("grp", None),
        P(None, ("grp", "tok")),
        P("tok"),
        P("tok", None),
        P("tok", None),
        P("tok", None),
        P("tok", None),
        P("tok"),
        P("tok", None),
        P("tok", None),
        P("tok", None),
        P("tok"),
    )
    return jax.shard_map(
        on_device,
        mesh=mesh,
        in_specs=placed,
        out_specs=(
            P(("grp", "tok"), None),
            P(("grp", "tok"), None),
            P(),
            P(),
            P(),
            P(),
            P(),
            P(),
            P(),
            P(),
            P(),
            P(),
        ),
        check_vma=False,
    )
```

profile of v0, /device:TPU:0, one launch (start us, length us, event | category | flops | bytes accessed | tf_op | source)
XLA Modules:
  0.0 1425.5 jit_solution(14185574392567609747)
XLA Ops:
  10.9 5.9 collective-permute-start.31
  27.0 14.5 %all-reduce.5 = (bf16[960]{0:T(1024)(128)(2,1)S(1)}, bf16[960]{0:T(1024)(128)(2,1)S(1)}, bf16[960]{0:T(1024)(128)(2,1)S(1)}) all-reduce(bf16[960]{0:T(1024)(128)(2,1)S(1)} %dynamic-update-slice.1, bf16[960]{0:T(1024)(128)(2,1)S(1)} %dynamic-update-slice.2, bf16[960]{0:T(1024)(128)(2,1)S(1)} %dynamic-update-slice), channel_id=1, replica_groups=mesh['grp'=4,'tok'=8] {'tok'}, use_global_device_ids=true, to_apply=%add.1 | all-reduce | flops 2880 | bytes 11520
  43.6 17.1 %all-gather.1 = bf16[8,120,320]{1,2,0:T(8,128)(2,1)S(1)} all-gather(bf16[1,120,320]{1,2,0:T(8,128)(2,1)S(1)} %bitcast.1047), channel_id=1, replica_groups=mesh['grp'=4,'tok'=8] {'tok'}, dimensions={0}, use_global_device_ids=true | all-gather | bytes 691200 | tf_op jit(solution)/shard_map/all_gather | solution.py:398
  61.7 17.7 %all-gather = bf16[8,120,320]{1,2,0:T(8,128)(2,1)S(1)} all-gather(bf16[1,120,320]{1,2,0:T(8,128)(2,1)S(1)} %bitcast.1048), channel_id=1, replica_groups=mesh['grp'=4,'tok'=8] {'tok'}, dimensions={0}, use_global_device_ids=true | all-gather | bytes 691200 | tf_op jit(solution)/shard_map/all_gather | solution.py:399
  113.1 18.8 %collective-permute-start.2 = (bf16[128,320]{0,1:T(8,128)(2,1)S(1)}, bf16[128,320]{0,1:T(8,128)(2,1)S(1)}, u32[]{:S(2)}, u32[]{:S(2)}) collective-permute-start(bf16[128,320]{0,1:T(8,128)(2,1)S(1)} %get-tuple-element.1013), channel_id=1, source_target_pairs={{0,3},{1,4},{2,5},{3,6},{4,7},{8,11},{9,12},{10,13},{11,14},{12,15... | collective-permute-start | bytes 245768 | tf_op jit(solution)/shard_map/ppermute | solution.py:22
  141.9 8.1 while.117
  154.1 18.0 %while.124 = (s32[]{:T(128)}, bf16[5,128,3,64]{1,3,2,0:T(8,128)(2,1)}, f32[5,3,128]{2,1,0:T(4,128)S(1)}, bf16[5,640,64]{1,2,0:T(8,128)(2,1)}, bf16[5,640,64]{1,2...) while((s32[]{:T(128)}, ...), condition=%wide.region_47.48_spmd.clone, body=%wide.region_44.47_spmd.clone.sunk | while | flops 65232512 | bytes 3397889 | solution.py:125
  180.3 20.2 %all-gather.14.cloned.1.call-done = bf16[960,2560]{1,0:T(8,128)(2,1)} async-done(((bf16[120,2560]{1,0:T(8,128)(2,1)}), bf16[960,2560]{1,0:T(8,128)(2,1)}) %all-gather.14.cloned.1.call-update) | async-done | bytes 4915216 | tf_op jit(solution)/shard_map/all_gather | solution.py:403
  200.6 56.4 %all-gather.16.cloned.1.call-done = bf16[2560,960]{1,0:T(8,128)(2,1)} async-done(((bf16[320,960]{1,0:T(8,128)(2,1)}), bf16[2560,960]{1,0:T(8,128)(2,1)}) %all-gather.16.cloned.1.call-update) | async-done | bytes 4915216 | tf_op jit(solution)/shard_map/all_gather | solution.py:404
  256.9 7.6 multiply_reduce_fusion.21
  294.8 30.5 %while.118 = (s32[]{:T(128)}, bf16[5,128,3,64]{1,3,2,0:T(8,128)(2,1)}, bf16[5,640,64]{1,2,0:T(8,128)(2,1)}, bf16[5,640,64]{1,2,0:T(8,128)(2,1)}, bf16[5,128,3,64...) while((s32[]{:T(128)}, ...), condition=%wide.region_14.15_spmd.clone, body=%wide.region_11.14_spmd.clone.sunk | while | flops 96937600 | bytes 3601653 | solution.py:125
  332.4 7.6 multiply_reduce_fusion.19
  354.6 18.1 %while.122 = (s32[]{:T(128)}, bf16[5,128,3,64]{1,3,2,0:T(8,128)(2,1)S(1)}, f32[5,3,128]{2,1,0:T(4,128)S(1)}, bf16[5,640,64]{1,2,0:T(8,128)(2,1)}, bf16[5,640,64]...) while((s32[]{:T(128)}, ...), condition=%wide.region_36.37_spmd.clone, body=%wide.region_33.36_spmd.clone.sunk | while | flops 65232512 | bytes 3398913 | solution.py:125
  389.2 30.5 %while.119 = (s32[]{:T(128)}, bf16[5,128,3,64]{1,3,2,0:T(8,128)(2,1)}, bf16[5,640,64]{1,2,0:T(8,128)(2,1)}, bf16[5,640,64]{1,2,0:T(8,128)(2,1)}, bf16[5,128,3,64...) while((s32[]{:T(128)}, ...), condition=%wide.region_20.21_spmd.clone, body=%wide.region_17.20_spmd.clone.sunk | while | flops 96937600 | bytes 3601653 | solution.py:125
  420.3 21.1 %while.120 = (s32[]{:T(128)}, bf16[5,128,3,64]{1,3,2,0:T(8,128)(2,1)S(1)}, f32[5,3,128]{2,1,0:T(4,128)}, bf16[5,640,64]{1,2,0:T(8,128)(2,1)}, bf16[5,640,64]{1,2...) while((s32[]{:T(128)}, ...), condition=%wide.region_25.26_spmd.clone, body=%wide.region_22.25_spmd.clone.sunk | while | flops 65232512 | bytes 3397889 | solution.py:125
  448.4 7.8 fusion.246
  465.9 5.2 fusion.266
  473.3 5.9 fusion.392
  479.2 5.7 fusion.390
  494.2 40.6 %while.121 = (s32[]{:T(128)}, f32[5,128,3,64]{1,3,2,0:T(8,128)}, f32[5,640,64]{1,2,0:T(8,128)}, f32[5,640,64]{1,2,0:T(8,128)}, bf16[5,640,64]{1,2,0:T(8,128)(2,1...) while((s32[]{:T(128)}, f32[5,128,3,64]{1,3,2,0:T(8,128)}, ...), condition=%wide.region_31.32_spmd.clone, body=%wide.region_29.31_spmd.clone.sunk | while | flops 159891072 | bytes 8424729 | solution.py:163
  566.0 5.2 fusion.267
  578.5 5.3 fusion.391
  594.5 47.9 %while.123 = (s32[]{:T(128)}, f32[5,128,3,64]{1,3,2,0:T(8,128)}, f32[5,640,64]{1,2,0:T(8,128)}, f32[5,640,64]{1,2,0:T(8,128)}, bf16[5,640,64]{1,2,0:T(8,128)(2,1...) while((s32[]{:T(128)}, f32[5,128,3,64]{1,3,2,0:T(8,128)}, ...), condition=%wide.region_42.43_spmd.clone, body=%wide.region_40.42_spmd.clone.sunk | while | flops 159891072 | bytes 8424729 | solution.py:163
  673.6 5.1 multiply_convert_fusion.6
  685.4 38.1 %while.125 = (s32[]{:T(128)}, f32[5,128,3,64]{1,3,2,0:T(8,128)}, f32[5,640,64]{1,2,0:T(8,128)S(1)}, f32[5,640,64]{1,2,0:T(8,128)S(1)}, bf16[5,640,64]{1,2,0:T(8,...) while((s32[]{:T(128)}, f32[5,128,3,64]{1,3,2,0:T(8,128)}, ...), condition=%wide.region_53.54_spmd.clone, body=%wide.region_51.53_spmd.clone.sunk | while | flops 159891072 | bytes 8424729 | solution.py:163
  737.9 12.2 add_add_fusion
  750.1 9.4 add_add_fusion.1
  759.6 9.2 add_add_fusion.2
  792.6 47.0 %all-reduce.3 = (f32[960]{0:T(1024)}, f32[960]{0:T(1024)}, f32[960]{0:T(1024)}) all-reduce(f32[960]{0:T(1024)S(1)} %add_add_fusion.7, f32[960]{0:T(1024)S(1)} %add_add_fusion.6, f32[960]{0:T(1024)S(1)} %add_add_fusion.5), channel_id=1, replica_groups=mesh['grp'=4,'tok'=8] {'grp','tok'}, use_global_device_ids=true, to_apply=%region_58.59 | all-reduce | flops 2880 | bytes 23040 | tf_op jit(solution)/shard_map/psum | solution.py:448
  840.9 546.7 %all-reduce.8.cloned.1.call-done = (f32[960,960]{1,0:T(8,128)}, f32[960,320]{0,1:T(8,128)}, f32[960,320]{0,1:T(8,128)}, f32[960,960]{1,0:T(8,128)}, f32[960,2560...) async-done(((f32[960,960]{1,0:T(8,128)}, f32[960,320]{0,1:T(8,128)}, f32[960,320]{0,1:T(8,128)}, f32[960,960]{1,0:T(8,128)}, f32[960,2560]{1,0:T(8,128)}, ...) | async-done | bytes 39321616 | tf_op jit(solution)/shard_map/psum | solution.py:448
  1397.3 8.6 copy.266
  1405.9 8.4 copy.267
  (987 shorter events, 558.1 us)
Async XLA Ops:
  7.3 131.8 %all-gather.8.cloned.1.call-start = ((), (), s32[]{:S(2)}) async-start(), calls=%async_computation | async-start | bytes 2211840 | tf_op jit(solution)/shard_map/all_gather | solution.py:397
  8.0 142.1 %all-gather.10.cloned.1.call-start = ((), (), s32[]{:S(2)}) async-start(), calls=%async_computation.1 | async-start | bytes 2211840 | tf_op jit(solution)/shard_map/all_gather | solution.py:400
  8.8 167.0 %all-gather.12.cloned.1.call-start = ((), (), s32[]{:S(2)}) async-start(), calls=%async_computation.2 | async-start | bytes 5529600 | tf_op jit(solution)/shard_map/all_gather | solution.py:402
  9.5 191.1 %all-gather.14.cloned.1.call-start = ((), (), s32[]{:S(2)}) async-start(), calls=%async_computation.3 | async-start | bytes 5529600 | tf_op jit(solution)/shard_map/all_gather | solution.py:403
  10.1 246.9 %all-gather.16.cloned.1.call-start = ((), (), s32[]{:S(2)}) async-start(), calls=%async_computation.4 | async-start | bytes 5898240 | tf_op jit(solution)/shard_map/all_gather | solution.py:404
  10.9 79.4 %collective-permute-start.31 = (bf16[128]{0:T(256)(128)(2,1)S(1)}, bf16[128]{0:T(256)(128)(2,1)S(1)}, u32[]{:S(2)}, u32[]{:S(2)}) collective-permute-start(bf16[128]{0:T(256)(128)(2,1)S(1)} %get-tuple-element.1007), channel_id=1, source_target_pairs={{0,4},{1,5},{2,6},{3,7},{8,12},{9,13},{10,14},{11,15},{16,20},{17,... | collective-permute-start | bytes 776 | tf_op jit(solution)/shard_map/ppermute | solution.py:22
  16.8 70.8 %collective-permute-start.30 = (bf16[128]{0:T(256)(128)(2,1)S(1)}, bf16[128]{0:T(256)(128)(2,1)S(1)}, u32[]{:S(2)}, u32[]{:S(2)}) collective-permute-start(bf16[128]{0:T(256)(128)(2,1)S(1)} %get-tuple-element.1007), channel_id=1, source_target_pairs={{0,3},{1,4},{2,5},{3,6},{4,7},{8,11},{9,12},{10,13},{11,14},{12,15... | collective-permute-start | bytes 776 | tf_op jit(solution)/shard_map/ppermute | solution.py:22
  19.5 64.2 %collective-permute-start.29 = (bf16[128]{0:T(256)(128)(2,1)S(1)}, bf16[128]{0:T(256)(128)(2,1)S(1)}, u32[]{:S(2)}, u32[]{:S(2)}) collective-permute-start(bf16[128]{0:T(256)(128)(2,1)S(1)} %get-tuple-element.1007), channel_id=1, source_target_pairs={{0,2},{1,3},{2,4},{3,5},{4,6},{5,7},{8,10},{9,11},{10,12},{11,13},... | collective-permute-start | bytes 776 | tf_op jit(solution)/shard_map/ppermute | solution.py:22
  21.6 60.6 %collective-permute-start.28 = (bf16[128]{0:T(256)(128)(2,1)S(1)}, bf16[128]{0:T(256)(128)(2,1)S(1)}, u32[]{:S(2)}, u32[]{:S(2)}) collective-permute-start(bf16[128]{0:T(256)(128)(2,1)S(1)} %get-tuple-element.1007), channel_id=1, source_target_pairs={{0,1},{1,2},{2,3},{3,4},{4,5},{5,6},{6,7},{8,9},{9,10},{10,11},{11... | collective-permute-start | bytes 776 | tf_op jit(solution)/shard_map/ppermute | solution.py:22
  23.4 76.4 %collective-permute-start.7 = (bf16[128]{0:T(256)(128)(2,1)S(1)}, bf16[128]{0:T(256)(128)(2,1)S(1)}, u32[]{:S(2)}, u32[]{:S(2)}) collective-permute-start(bf16[128]{0:T(256)(128)(2,1)S(1)} %get-tuple-element.1008), channel_id=1, source_target_pairs={{0,4},{1,5},{2,6},{3,7},{8,12},{9,13},{10,14},{11,15},{16,20},{17,... | collective-permute-start | bytes 776 | tf_op jit(solution)/shard_map/ppermute | solution.py:22
  25.0 1362.6 %all-reduce.8.cloned.1.call-start = ((), (), s32[]{:S(2)}) async-start(), calls=%async_computation.5 | async-start | bytes 79953920 | tf_op jit(solution)/shard_map/psum | solution.py:448
  82.2 15.2 %collective-permute-start.6 = (bf16[128]{0:T(256)(128)(2,1)S(1)}, bf16[128]{0:T(256)(128)(2,1)S(1)}, u32[]{:S(2)}, u32[]{:S(2)}) collective-permute-start(bf16[128]{0:T(256)(128)(2,1)S(1)} %get-tuple-element.1008), channel_id=1, source_target_pairs={{0,3},{1,4},{2,5},{3,6},{4,7},{8,11},{9,12},{10,13},{11,14},{12,15... | collective-permute-start | bytes 776 | tf_op jit(solution)/shard_map/ppermute | solution.py:22
  90.4 19.5 %collective-permute-start.19 = (bf16[128]{0:T(256)(128)(2,1)S(1)}, bf16[128]{0:T(256)(128)(2,1)S(1)}, u32[]{:S(2)}, u32[]{:S(2)}) collective-permute-start(bf16[128]{0:T(256)(128)(2,1)S(1)} %get-tuple-element.1009), channel_id=1, source_target_pairs={{0,4},{1,5},{2,6},{3,7},{8,12},{9,13},{10,14},{11,15},{16,20},{17,... | collective-permute-start | bytes 776 | tf_op jit(solution)/shard_map/ppermute | solution.py:22
  99.8 38.4 %collective-permute-start.11 = (bf16[128,320]{0,1:T(8,128)(2,1)S(1)}, bf16[128,320]{0,1:T(8,128)(2,1)S(1)}, u32[]{:S(2)}, u32[]{:S(2)}) collective-permute-start(bf16[128,320]{0,1:T(8,128)(2,1)S(1)} %bitcast.1039), channel_id=1, source_target_pairs={{0,4},{1,5},{2,6},{3,7},{8,12},{9,13},{10,14},{11,15},{16,20},{17,... | collective-permute-start | bytes 245768 | tf_op jit(solution)/shard_map/ppermute | solution.py:22
  102.5 30.8 %collective-permute-start.10 = (bf16[128,320]{0,1:T(8,128)(2,1)S(1)}, bf16[128,320]{0,1:T(8,128)(2,1)S(1)}, u32[]{:S(2)}, u32[]{:S(2)}) collective-permute-start(bf16[128,320]{0,1:T(8,128)(2,1)S(1)} %bitcast.1040), channel_id=1, source_target_pairs={{0,3},{1,4},{2,5},{3,6},{4,7},{8,11},{9,12},{10,13},{11,14},{12,15... | collective-permute-start | bytes 245768 | tf_op jit(solution)/shard_map/ppermute | solution.py:22
  104.3 27.7 %collective-permute-start.9 = (bf16[128,320]{0,1:T(8,128)(2,1)S(1)}, bf16[128,320]{0,1:T(8,128)(2,1)S(1)}, u32[]{:S(2)}, u32[]{:S(2)}) collective-permute-start(bf16[128,320]{0,1:T(8,128)(2,1)S(1)} %bitcast.1041), channel_id=1, source_target_pairs={{0,2},{1,3},{2,4},{3,5},{4,6},{5,7},{8,10},{9,11},{10,12},{11,13},... | collective-permute-start | bytes 245768 | tf_op jit(solution)/shard_map/ppermute | solution.py:22
  109.8 29.2 %collective-permute-start.3 = (bf16[128,320]{0,1:T(8,128)(2,1)S(1)}, bf16[128,320]{0,1:T(8,128)(2,1)S(1)}, u32[]{:S(2)}, u32[]{:S(2)}) collective-permute-start(bf16[128,320]{0,1:T(8,128)(2,1)S(1)} %get-tuple-element.1013), channel_id=1, source_target_pairs={{0,4},{1,5},{2,6},{3,7},{8,12},{9,13},{10,14},{11,15},{16,20},{17,... | collective-permute-start | bytes 245768 | tf_op jit(solution)/shard_map/ppermute | solution.py:22
  113.1 25.9 %collective-permute-start.2 = (bf16[128,320]{0,1:T(8,128)(2,1)S(1)}, bf16[128,320]{0,1:T(8,128)(2,1)S(1)}, u32[]{:S(2)}, u32[]{:S(2)}) collective-permute-start(bf16[128,320]{0,1:T(8,128)(2,1)S(1)} %get-tuple-element.1013), channel_id=1, source_target_pairs={{0,3},{1,4},{2,5},{3,6},{4,7},{8,11},{9,12},{10,13},{11,14},{12,15... | collective-permute-start | bytes 245768 | tf_op jit(solution)/shard_map/ppermute | solution.py:22
  266.7 26.4 %collective-permute-start.23 = (bf16[128,320]{0,1:T(8,128)(2,1)S(1)}, bf16[128,320]{0,1:T(8,128)(2,1)S(1)}, u32[]{:S(2)}, u32[]{:S(2)}) collective-permute-start(bf16[128,320]{0,1:T(8,128)(2,1)S(1)} %bitcast.1043), channel_id=1, source_target_pairs={{0,4},{1,5},{2,6},{3,7},{8,12},{9,13},{10,14},{11,15},{16,20},{17,... | collective-permute-start | bytes 245768 | tf_op jit(solution)/shard_map/ppermute | solution.py:22
  270.0 20.3 %collective-permute-start.22 = (bf16[128,320]{0,1:T(8,128)(2,1)S(1)}, bf16[128,320]{0,1:T(8,128)(2,1)S(1)}, u32[]{:S(2)}, u32[]{:S(2)}) collective-permute-start(bf16[128,320]{0,1:T(8,128)(2,1)S(1)} %bitcast.1044), channel_id=1, source_target_pairs={{0,3},{1,4},{2,5},{3,6},{4,7},{8,11},{9,12},{10,13},{11,14},{12,15... | collective-permute-start | bytes 245768 | tf_op jit(solution)/shard_map/ppermute | solution.py:22
  271.7 16.3 %collective-permute-start.21 = (bf16[128,320]{0,1:T(8,128)(2,1)S(1)}, bf16[128,320]{0,1:T(8,128)(2,1)S(1)}, u32[]{:S(2)}, u32[]{:S(2)}) collective-permute-start(bf16[128,320]{0,1:T(8,128)(2,1)S(1)} %bitcast.1045), channel_id=1, source_target_pairs={{0,2},{1,3},{2,4},{3,5},{4,6},{5,7},{8,10},{9,11},{10,12},{11,13},... | collective-permute-start | bytes 245768 | tf_op jit(solution)/shard_map/ppermute | solution.py:22
  278.1 15.8 %collective-permute-start.15 = (bf16[128,320]{0,1:T(8,128)(2,1)S(1)}, bf16[128,320]{0,1:T(8,128)(2,1)S(1)}, u32[]{:S(2)}, u32[]{:S(2)}) collective-permute-start(bf16[128,320]{0,1:T(8,128)(2,1)S(1)} %get-tuple-element.1019), channel_id=1, source_target_pairs={{0,4},{1,5},{2,6},{3,7},{8,12},{9,13},{10,14},{11,15},{16,20},{17,... | collective-permute-start | bytes 245768 | tf_op jit(solution)/shard_map/ppermute | solution.py:22
  342.6 44.0 %collective-permute-start.35 = (bf16[128,320]{0,1:T(8,128)(2,1)}, bf16[128,320]{0,1:T(8,128)(2,1)}, u32[]{:S(2)}, u32[]{:S(2)}) collective-permute-start(bf16[128,320]{0,1:T(8,128)(2,1)} %bitcast.48), channel_id=1, source_target_pairs={{0,4},{1,5},{2,6},{3,7},{8,12},{9,13},{10,14},{11,15},{16,20},{17,... | collective-permute-start | bytes 245768 | tf_op jit(solution)/shard_map/ppermute | solution.py:22
  347.3 35.9 %collective-permute-start.34 = (bf16[128,320]{0,1:T(8,128)(2,1)}, bf16[128,320]{0,1:T(8,128)(2,1)}, u32[]{:S(2)}, u32[]{:S(2)}) collective-permute-start(bf16[128,320]{0,1:T(8,128)(2,1)} %bitcast.48), channel_id=1, source_target_pairs={{0,3},{1,4},{2,5},{3,6},{4,7},{8,11},{9,12},{10,13},{11,14},{12,15... | collective-permute-start | bytes 245768 | tf_op jit(solution)/shard_map/ppermute | solution.py:22
  349.3 31.1 %collective-permute-start.33 = (bf16[128,320]{0,1:T(8,128)(2,1)}, bf16[128,320]{0,1:T(8,128)(2,1)}, u32[]{:S(2)}, u32[]{:S(2)}) collective-permute-start(bf16[128,320]{0,1:T(8,128)(2,1)} %bitcast.48), channel_id=1, source_target_pairs={{0,2},{1,3},{2,4},{3,5},{4,6},{5,7},{8,10},{9,11},{10,12},{11,13},... | collective-permute-start | bytes 245768 | tf_op jit(solution)/shard_map/ppermute | solution.py:22
  351.6 25.9 %collective-permute-start.32 = (bf16[128,320]{0,1:T(8,128)(2,1)}, bf16[128,320]{0,1:T(8,128)(2,1)}, u32[]{:S(2)}, u32[]{:S(2)}) collective-permute-start(bf16[128,320]{0,1:T(8,128)(2,1)} %bitcast.48), channel_id=1, source_target_pairs={{0,1},{1,2},{2,3},{3,4},{4,5},{5,6},{6,7},{8,9},{9,10},{10,11},{11... | collective-permute-start | bytes 245768 | tf_op jit(solution)/shard_map/ppermute | solution.py:22
  537.4 20.0 %collective-permute-start.43 = (bf16[128,320]{0,1:T(8,128)(2,1)S(1)}, bf16[128,320]{0,1:T(8,128)(2,1)S(1)}, u32[]{:S(2)}, u32[]{:S(2)}) collective-permute-start(bf16[128,320]{0,1:T(8,128)(2,1)S(1)} %bitcast.1018), channel_id=1, source_target_pairs={{4,0},{5,1},{6,2},{7,3},{12,8},{13,9},{14,10},{15,11},{20,16},{21,... | collective-permute-start | bytes 245768 | tf_op jit(solution)/shard_map/ppermute | solution.py:22
  645.0 19.9 %collective-permute-start.51 = (bf16[128,320]{0,1:T(8,128)(2,1)S(1)}, bf16[128,320]{0,1:T(8,128)(2,1)S(1)}, u32[]{:S(2)}, u32[]{:S(2)}) collective-permute-start(bf16[128,320]{0,1:T(8,128)(2,1)S(1)} %bitcast.1017), channel_id=1, source_target_pairs={{4,0},{5,1},{6,2},{7,3},{12,8},{13,9},{14,10},{15,11},{20,16},{21,... | collective-permute-start | bytes 245768 | tf_op jit(solution)/shard_map/ppermute | solution.py:22
  726.6 47.4 %collective-permute-start.55 = (bf16[128,320]{0,1:T(8,128)(2,1)}, bf16[128,320]{0,1:T(8,128)(2,1)}, u32[]{:S(2)}, u32[]{:S(2)}) collective-permute-start(bf16[128,320]{0,1:T(8,128)(2,1)} %bitcast.121), channel_id=1, source_target_pairs={{4,0},{5,1},{6,2},{7,3},{12,8},{13,9},{14,10},{15,11},{20,16},{21,... | collective-permute-start | bytes 245768 | tf_op jit(solution)/shard_map/ppermute | solution.py:22
  727.9 47.4 %collective-permute-start.52 = (bf16[128,320]{0,1:T(8,128)(2,1)}, bf16[128,320]{0,1:T(8,128)(2,1)}, u32[]{:S(2)}, u32[]{:S(2)}) collective-permute-start(bf16[128,320]{0,1:T(8,128)(2,1)} %bitcast.118), channel_id=1, source_target_pairs={{1,0},{2,1},{3,2},{4,3},{5,4},{6,5},{7,6},{9,8},{10,9},{11,10},{12... | collective-permute-start | bytes 245768 | tf_op jit(solution)/shard_map/ppermute | solution.py:22
  729.2 47.4 %collective-permute-start.54 = (bf16[128,320]{0,1:T(8,128)(2,1)}, bf16[128,320]{0,1:T(8,128)(2,1)}, u32[]{:S(2)}, u32[]{:S(2)}) collective-permute-start(bf16[128,320]{0,1:T(8,128)(2,1)} %bitcast.120), channel_id=1, source_target_pairs={{3,0},{4,1},{5,2},{6,3},{7,4},{11,8},{12,9},{13,10},{14,11},{15,12... | collective-permute-start | bytes 245768 | tf_op jit(solution)/shard_map/ppermute | solution.py:22
  730.5 47.4 %collective-permute-start.53 = (bf16[128,320]{0,1:T(8,128)(2,1)}, bf16[128,320]{0,1:T(8,128)(2,1)}, u32[]{:S(2)}, u32[]{:S(2)}) collective-permute-start(bf16[128,320]{0,1:T(8,128)(2,1)} %bitcast.119), channel_id=1, source_target_pairs={{2,0},{3,1},{4,2},{5,3},{6,4},{7,5},{10,8},{11,9},{12,10},{13,11},... | collective-permute-start | bytes 245768 | tf_op jit(solution)/shard_map/ppermute | solution.py:22
  (208 other events, 3081.7 us)
Sparse Core Ops, SparseCore 0:
  9.7 31.1 all-gather.7
  42.6 33.5 all-gather.9
  77.8 55.6 all-gather.11
  135.0 65.5 all-gather.13
  202.1 54.8 all-gather.15
  788.7 598.8 all-reduce.7
where the time goes:
time: 1440 us; the launch traced here: 1430 us
  waiting for transfers between devices  647 us (45%)
  matrix products  398 us (28%)
  starting transfers between devices  130 us (9%)
  blocking collectives  96.3 us (7%)
  local copies, waits for them, and re-layouts  75.1 us (5%)
  other arithmetic  58.4 us (4%)
  between operations  18.6 us (1%)
    psum x1, waiting for transfers between devices, on_device(): summed = lax.psum(grads, ('grp', 'tok'))  547 us
    ppermute x60, starting transfers between devices, from_behind(): return lax.ppermute(block, axis, route)  130 us
    dot_general x21, matrix products, matmul_tn(): lax.dot_general(left, right, (((0,), (0,)), ((), ())), preferred_element_...  88.9 us
    dot_general x27, matrix products, matmul(): return jnp.dot(left, right, preferred_element_type=jnp.float32)  72.6 us
    all_gather x1, waiting for transfers between devices, on_device(): lax.all_gather(shards[8], 'tok', axis=0, tiled=True)  56.4 us
    dot_general x45, matrix products, one_head(): jnp.einsum('rgd,kd->grk', query_h, key_h, preferred_element_type=jnp.floa...  52.7 us
    unnamed x395, local copies, waits for them, and re-layouts  47.3 us
    psum x1, blocking collectives, on_device(): summed = lax.psum(grads, ('grp', 'tok'))  47 us
  transfers between devices with their start and end apart: 66, of which 13 were waited for; matrix products, arithmetic and copies ran while one was open for 10% of the time, Pallas kernels for 0%

commit v1 on v0

--- a/solution.py
+++ b/solution.py
@@ -1,7 +1,11 @@
 import jax
 import jax.numpy as jnp
 from jax import lax
+from jax.experimental import pallas as pl
+from jax.experimental.pallas import tpu as pltpu
 from jax.sharding import PartitionSpec as P
+
+MESH = pl.DeviceIdType.MESH
 
 H = 15
 KVH = 5
@@ -16,6 +20,436 @@
 highest = lax.Precision.HIGHEST
 
 
+PARTS = 16
+HALF = 480
+COLS = 640
+STREAMS = (("x", True, 0, 160), ("y", True, 160, 160), ("x", False, 320, 80), ("y", False, 400, 80))
+
+
+def place():
+    g, t = lax.axis_index("grp"), lax.axis_index("tok")
+    return g // 2, lax.rem(g, 2), t // 2, lax.rem(t, 2)
+
+
+def dev(y, x, z, c):
+    return (y * 2 + x, z * 2 + c)
+
+
+def pick(z, values):
+    out = jnp.int32(values[3])
+    for i in (2, 1, 0):
+        out = jnp.where(z == i, jnp.int32(values[i]), out)
+    return out
+
+
+def copy_to(src, dst, send, recv, device):
+    return pltpu.make_async_remote_copy(src_ref=src, dst_ref=dst, send_sem=send, recv_sem=recv, device_id=device, device_id_type=MESH)
+
+
+def add_rows(dst, src, rows, step):
+    def body(i, _):
+        at = pl.ds(pl.multiple_of(i * step, step), step)
+        dst[at, :] = dst[at, :] + src[at, :]
+        return 0
+    lax.fori_loop(0, rows // step, body, 0)
+
+
+def reduce_kernel(g_ref, v_ref, o_ref, vo_ref, mine, other, ra0, ra1, ra2, ra3, rz0, rz1, rz2, rz3, rb0, rb1, rb2, rb3,
+                  vrecv, load_sem, core_s, core_r, as_, ar, zs, zr, bs, br, ob, obr, oz, ozr, oa, oar, oc, ocr, vs, vr, own_sem):
+    y, x, z, c = place()
+    ra, rz, rb = (ra0, ra1, ra2, ra3), (rz0, rz1, rz2, rz3), (rb0, rb1, rb2, rb3)
+    partner = dev(y, x, z, 1 - c)
+    across = {"x": dev(y, 1 - x, z, c), "y": dev(1 - y, x, z, c)}
+    left, right = dev(y, x, z - 1, c), dev(y, x, z + 1, c)
+    at_axis = {"x": x, "y": y}
+    order = (pick(z, (3, 3, 0, 0)), pick(z, (2, 0, 3, 1)), pick(z, (1, 2, 1, 2)), z)
+
+    bar = pltpu.get_barrier_semaphore()
+    for d in (partner, across["x"], across["y"]):
+        pl.semaphore_signal(bar, inc=1, device_id=d, device_id_type=MESH)
+
+    @pl.when(z > 0)
+    def _():
+        pl.semaphore_signal(bar, inc=1, device_id=left, device_id_type=MESH)
+
+    @pl.when(z < 3)
+    def _():
+        pl.semaphore_signal(bar, inc=1, device_id=right, device_id_type=MESH)
+    far = dev(y, x, jnp.where(z < 2, z + 2, z - 2), c)
+    pl.semaphore_signal(bar, inc=1, device_id=far, device_id_type=MESH)
+    pl.semaphore_wait(bar, 4 + (z > 0).astype(jnp.int32) + (z < 3).astype(jnp.int32))
+
+    def part_xy(px, py, pz):
+        return (px * 2 + py) * 4 + pz
+
+    def part_of(s, pa, pb, pz):
+        return part_xy(pa, pb, pz) if STREAMS[s][0] == "x" else part_xy(pb, pa, pz)
+
+    def ab(s):
+        a = STREAMS[s][0]
+        b = "y" if a == "x" else "x"
+        return at_axis[a], at_axis[b], across[a], across[b]
+
+    def core_copy(p):
+        return copy_to(g_ref.at[p, pl.ds(pl.multiple_of((1 - c) * HALF, HALF), HALF)], other.at[p], core_s.at[p], core_r.at[p], partner)
+
+    def load(p):
+        return pltpu.make_async_copy(g_ref.at[p, pl.ds(pl.multiple_of(c * HALF, HALF), HALF)], mine.at[p], load_sem.at[p])
+
+    waits = []
+    seq = [(k, px, py) for k in range(4) for px, py in ((1 - x, 1 - y), (1 - x, y), (x, 1 - y), (x, y))]
+    for k, px, py in seq:
+        p = part_xy(px, py, order[k])
+        core_copy(p).start()
+        load(p).start()
+
+    def a_copy(s, pb, pz):
+        a, b, to_a, _ = ab(s)
+        _, _, r0, n = STREAMS[s]
+        return copy_to(mine.at[part_of(s, 1 - a, pb, pz), pl.ds(r0, n)], ra[s].at[pb * 4 + pz], as_.at[s, pb * 4 + pz], ar.at[s, pb * 4 + pz], to_a)
+
+    def core_step(k):
+        for i, (px, py) in enumerate(((1 - x, 1 - y), (1 - x, y), (x, 1 - y), (x, y))):
+            p = part_xy(px, py, order[k])
+            load(p).wait()
+            core_copy(p).wait_recv()
+            add_rows(mine.at[p], other.at[p], HALF, 16)
+            for s in range(4):
+                a_axis = STREAMS[s][0]
+                if i == 0 or (i == 1 and a_axis == "x") or (i == 2 and a_axis == "y"):
+                    pb = py if a_axis == "x" else px
+                    cp = a_copy(s, pb, order[k])
+                    cp.start()
+                    waits.append(cp)
+
+    def z_copy(s, pb, pz, to_right):
+        a, b, _, _ = ab(s)
+        _, _, r0, n = STREAMS[s]
+        src = mine.at[part_of(s, a, pb, pz), pl.ds(r0, n)]
+        slot = pz if to_right else jnp.where(pz == z - 1, 4, pz)
+        i = pb * 5 + slot
+        return copy_to(src, rz[s].at[i], zs.at[s, i], zr.at[s, i], right if to_right else left)
+
+    def z_wait(s, pb, slot):
+        _, _, r0, n = STREAMS[s]
+        i = pb * 5 + slot
+        copy_to(mine.at[0, pl.ds(r0, n)], rz[s].at[i], zs.at[s, i], zr.at[s, i], left).wait_recv()
+
+    def z_step(s, pb, k):
+        a, b, _, _ = ab(s)
+        _, _, r0, n = STREAMS[s]
+        pz = order[k]
+        acc = mine.at[part_of(s, a, pb, pz), pl.ds(r0, n)]
+        if k < 3:
+            up = jnp.where(pz > z, (z > 0).astype(jnp.int32), (z < 3).astype(jnp.int32))
+
+            @pl.when(up == 1)
+            def _():
+                z_wait(s, pb, pz)
+                add_rows(acc, rz[s].at[pb * 5 + pz], n, 16)
+
+            @pl.when(pz > z)
+            def _():
+                z_copy(s, pb, pz, True).start()
+
+            @pl.when(pz < z)
+            def _():
+                z_copy(s, pb, pz, False).start()
+        else:
+            @pl.when(z > 0)
+            def _():
+                z_wait(s, pb, z)
+                add_rows(acc, rz[s].at[pb * 5 + z], n, 16)
+
+            @pl.when(z < 3)
+            def _():
+                z_wait(s, pb, 4)
+                add_rows(acc, rz[s].at[pb * 5 + 4], n, 16)
+
+    def z_drain(s, pb, k):
+        pz = order[k]
+
+        @pl.when(pz > z)
+        def _():
+            z_copy(s, pb, pz, True).wait_send()
+
+        @pl.when(pz < z)
+        def _():
+            z_copy(s, pb, pz, False).wait_send()
+
+    def a_step(s, pb, k):
+        a, b, to_a, _ = ab(s)
+        _, _, r0, n = STREAMS[s]
+        pz = order[k]
+        a_copy(s, pb, pz).wait_recv()
+        add_rows(mine.at[part_of(s, a, pb, pz), pl.ds(r0, n)], ra[s].at[pb * 4 + pz], n, 16)
+
+    def b_copy(s, pz):
+        a, b, _, to_b = ab(s)
+        _, second_z, r0, n = STREAMS[s]
+        i = 0 if second_z else pz
+        return copy_to(mine.at[part_of(s, a, 1 - b, pz), pl.ds(r0, n)], rb[s].at[i], bs.at[s, i], br.at[s, i], to_b)
+
+    def b_step(s, pz):
+        a, b, _, _ = ab(s)
+        _, second_z, r0, n = STREAMS[s]
+        i = 0 if second_z else pz
+        b_copy(s, pz).wait_recv()
+        add_rows(mine.at[part_of(s, a, b, pz), pl.ds(r0, n)], rb[s].at[i], n, 16)
+
+    def stream_step(k):
+        for s in range(4):
+            _, b, _, _ = ab(s)
+            if STREAMS[s][1]:
+                a_step(s, 1 - b, k)
+                z_step(s, 1 - b, k)
+                a_step(s, b, k)
+                z_step(s, b, k)
+                if k == 3:
+                    cp = b_copy(s, z)
+                    cp.start()
+                    waits.append(cp)
+            else:
+                a_step(s, 1 - b, k)
+                cp = b_copy(s, order[k])
+                cp.start()
+                waits.append(cp)
+                a_step(s, b, k)
+
+    def stream_step2(k):
+        for s in range(4):
+            _, b, _, _ = ab(s)
+            if not STREAMS[s][1]:
+                b_step(s, order[k])
+                z_step(s, b, k)
+            elif k == 3:
+                b_step(s, z)
+
+    def vec_to(i):
+        return (partner, across["x"], across["y"], dev(y, x, jnp.where(lax.rem(z, 2) == 0, z + 1, z - 1), c), far)[i]
+
+    def vec_copy(i):
+        return copy_to(vo_ref, vrecv.at[i], vs.at[i], vr.at[i], vec_to(i))
+
+    def vec_start(i):
+        vec_copy(i).start()
+
+    def vec_end(i):
+        vec_copy(i).wait()
+        vo_ref[...] = vo_ref[...] + vrecv[i]
+
+    vo_ref[...] = v_ref[...]
+    vec_start(0)
+    core_step(0)
+    vec_end(0)
+    vec_start(1)
+    core_step(1)
+    vec_end(1)
+    vec_start(2)
+    stream_step(0)
+    vec_end(2)
+    vec_start(3)
+    core_step(2)
+    stream_step2(0)
+    vec_end(3)
+    vec_start(4)
+    stream_step(1)
+    core_step(3)
+    stream_step2(1)
+    vec_end(4)
+    stream_step(2)
+    stream_step2(2)
+    stream_step(3)
+
+    half0 = c * HALF
+
+    def out_at(s, p):
+        _, _, r0, n = STREAMS[s]
+        return o_ref.at[p, pl.ds(pl.multiple_of(half0 + r0, 16), n)]
+
+    def mine_at(s, p):
+        _, _, r0, n = STREAMS[s]
+        return mine.at[p, pl.ds(r0, n)]
+
+    def go(cp):
+        cp.start()
+        waits.append(cp)
+
+    def to_core(s, p, src):
+        return copy_to(src, out_at(s, p), oc.at[s, p], ocr.at[s, p], partner)
+
+    def to_a(s, pb, pz, src):
+        a, b, na, _ = ab(s)
+        return copy_to(src, out_at(s, part_of(s, a, pb, pz)), oa.at[s, pb * 4 + pz], oar.at[s, pb * 4 + pz], na)
+
+    def to_b(s, pz, src):
+        a, b, _, nb = ab(s)
+        return copy_to(src, out_at(s, part_of(s, a, b, pz)), ob.at[s, pz], obr.at[s, pz], nb)
+
+    def to_z(s, pb, pz, src, to_right):
+        a, b, _, _ = ab(s)
+        i = pb * 8 + pz * 2 + (0 if to_right else 1)
+        return copy_to(src, out_at(s, part_of(s, a, pb, pz)), oz.at[s, i], ozr.at[s, pb * 4 + pz], right if to_right else left)
+
+    def spread_z(s, pb, pz, src, from_left=None):
+        if from_left is None:
+            @pl.when(z < 3)
+            def _():
+                to_z(s, pb, pz, src, True).start()
+
+            @pl.when(z > 0)
+            def _():
+                to_z(s, pb, pz, src, False).start()
+        elif from_left:
+            @pl.when(z < 3)
+            def _():
+                to_z(s, pb, pz, src, True).start()
+        else:
+            @pl.when(z > 0)
+            def _():
+                to_z(s, pb, pz, src, False).start()
+
+    for s in range(4):
+        a, b, _, _ = ab(s)
+        p = part_of(s, a, b, z)
+        if STREAMS[s][1]:
+            b_step(s, z)
+            src = mine_at(s, p)
+            go(to_b(s, z, src))
+            spread_z(s, b, z, src)
+            go(to_a(s, b, z, src))
+        else:
+            b_step(s, z)
+            z_step(s, b, 3)
+            src = mine_at(s, p)
+            spread_z(s, b, z, src)
+            go(to_b(s, z, src))
+            go(to_a(s, b, z, src))
+        go(to_core(s, p, src))
+        pltpu.make_async_copy(src, out_at(s, p), own_sem.at[s]).start()
+
+    def got_b(s, pz):
+        a, b, _, _ = ab(s)
+        p = part_of(s, a, 1 - b, pz)
+        src = out_at(s, p)
+        copy_to(src, src, ob.at[s, pz], obr.at[s, pz], partner).wait_recv()
+        if STREAMS[s][1]:
+            spread_z(s, 1 - b, pz, src)
+        to_a(s, 1 - b, pz, src).start()
+        to_core(s, p, src).start()
+
+    def got_z(s, pb, pz, from_left):
+        a, b, _, _ = ab(s)
+        p = part_of(s, a, pb, pz)
+        src = out_at(s, p)
+        copy_to(src, src, oz.at[s, 0], ozr.at[s, pb * 4 + pz], partner).wait_recv()
+        spread_z(s, pb, pz, src, from_left)
+        to_a(s, pb, pz, src).start()
+        to_core(s, p, src).start()
+        if not STREAMS[s][1]:
+            to_b(s, pz, src).start()
+
+    def got_a(s, pb, pz):
+        a, b, _, _ = ab(s)
+        p = part_of(s, 1 - a, pb, pz)
+        src = out_at(s, p)
+        copy_to(src, src, oa.at[s, pb * 4 + pz], oar.at[s, pb * 4 + pz], partner).wait_recv()
+        to_core(s, p, src).start()
+
+    for s in range(4):
+        got_b(s, z)
+    for s in range(4):
+        a, b, _, _ = ab(s)
+        got_a(s, b, z)
+        got_a(s, 1 - b, z)
+    for t in range(1, 4):
+        for lft in (True, False):
+            pz = z - t if lft else z + t
+            ok = (z >= t) if lft else (z + t <= 3)
+
+            @pl.when(ok)
+            def _():
+                for s in range(4):
+                    a, b, _, _ = ab(s)
+                    got_z(s, b, pz, lft)
+                    if STREAMS[s][1]:
+                        got_z(s, 1 - b, pz, lft)
+                for s in range(4):
+                    if not STREAMS[s][1]:
+                        got_b(s, pz)
+                for s in range(4):
+                    a, b, _, _ = ab(s)
+                    got_a(s, b, pz)
+                    got_a(s, 1 - b, pz)
+
+    for cp in waits:
+        cp.wait_send()
+    for k, px, py in seq:
+        core_copy(part_xy(px, py, order[k])).wait_send()
+    for s in range(4):
+        a, b, _, _ = ab(s)
+        pltpu.make_async_copy(mine_at(s, part_of(s, a, b, z)), out_at(s, part_of(s, a, b, z)), own_sem.at[s]).wait()
+        pbs = (b, 1 - b) if STREAMS[s][1] else (b,)
+        for pb in pbs:
+            for k in range(3):
+                z_drain(s, pb, k)
+        for pz in range(4):
+            for pb in pbs:
+                src = out_at(s, part_of(s, a, pb, pz))
+
+                @pl.when((z >= pz) & (z < 3))
+                def _():
+                    to_z(s, pb, pz, src, True).wait_send()
+
+                @pl.when((z <= pz) & (z > 0))
+                def _():
+                    to_z(s, pb, pz, src, False).wait_send()
+            for pb in (0, 1):
+                src = out_at(s, part_of(s, a, pb, pz))
+
+                @pl.when(((pb == b) & (pz == z)) == False)
+                def _():
+                    to_a(s, pb, pz, src).wait_send()
+            if not STREAMS[s][1]:
+                @pl.when(z != pz)
+                def _():
+                    to_b(s, pz, out_at(s, 0)).wait_send()
+        for p in range(16):
+            src = out_at(s, p)
+
+            @pl.when(p != part_of(s, a, b, z))
+            def _():
+                to_core(s, p, src).wait_send()
+            _, _, r0, n = STREAMS[s]
+            dst = o_ref.at[p, pl.ds(pl.multiple_of((1 - c) * HALF + r0, 16), n)]
+            copy_to(dst, dst, oc.at[s, p], ocr.at[s, p], partner).wait_recv()
+
+
+def all_sum(grads, vectors):
+    dma = pltpu.SemaphoreType.DMA
+    bf = jnp.bfloat16
+    rows = [s[3] for s in STREAMS]
+    return pl.pallas_call(
+        reduce_kernel,
+        name="all_sum",
+        out_shape=(jax.ShapeDtypeStruct(grads.shape, bf), jax.ShapeDtypeStruct(vectors.shape, jnp.float32)),
+        in_specs=[pl.BlockSpec(memory_space=pl.ANY), pl.BlockSpec(memory_space=pltpu.VMEM)],
+        out_specs=(pl.BlockSpec(memory_space=pl.ANY), pl.BlockSpec(memory_space=pltpu.VMEM)),
+        scratch_shapes=[
+            pltpu.VMEM((PARTS, HALF, COLS), bf), pltpu.VMEM((PARTS, HALF, COLS), bf),
+            *[pltpu.VMEM((8, n, COLS), bf) for n in rows],
+            *[pltpu.VMEM((10, n, COLS), bf) for n in rows],
+            *[pltpu.VMEM((1 if s[1] else 4, s[3], COLS), bf) for s in STREAMS],
+            pltpu.VMEM((5, *vectors.shape), jnp.float32),
+            dma((16,)), dma((16,)), dma((16,)),
+            dma((4, 8)), dma((4, 8)), dma((4, 10)), dma((4, 10)), dma((4, 4)), dma((4, 4)),
+            dma((4, 4)), dma((4, 4)), dma((4, 16)), dma((4, 8)), dma((4, 8)), dma((4, 8)), dma((4, 16)), dma((4, 16)),
+            dma((5,)), dma((5,)), dma((4,)),
+        ],
+        compiler_params=pltpu.CompilerParams(collective_id=1, has_side_effects=True, vmem_limit_bytes=56 * 2**20),
+    )(grads, vectors)
+
+
 def from_behind(block, axis, distance):
     devices = range(lax.axis_size(axis))
     route = [(i - distance, i) for i in devices if i - distance in devices]
@@ -50,13 +484,19 @@
     return (inverse_rms * (grad_scaled - scaled * inner), jnp.sum(grad_in * scaled, axis=0))
 
 
+def ends_of(lengths_row):
+    count = lengths_row.shape[0]
+    until = jnp.arange(count)[:, None] >= jnp.arange(count)[None, :]
+    return jnp.sum(jnp.where(until, lengths_row[None, :], 0), axis=1)
+
+
 def segment_of(lengths_row, global_rows):
-    ends_at = jnp.cumsum(lengths_row)
+    ends_at = ends_of(lengths_row)
     return jnp.sum((global_rows[:, None] >= ends_at[None, :]).astype(jnp.int32), axis=1)
 
 
 def position_of(lengths_row, global_rows, segments):
-    ends_at = jnp.cumsum(lengths_row)
+    ends_at = ends_of(lengths_row)
     starts_at = ends_at - lengths_row
     picked = segments[:, None] == jnp.arange(lengths_row.shape[0], dtype=jnp.int32)[None, :]
     return global_rows - jnp.sum(jnp.where(picked, starts_at[None, :], 0), axis=1)
@@ -235,30 +675,20 @@
     sigmoid_gate = jax.nn.sigmoid(gate_pre)
     silu_gate = jax.nn.silu(gate_pre)
     hidden_low = (silu_gate * up_pre).astype(jnp.bfloat16)
-    grad_down = matmul_tn(hidden_low, grad_rows)
     grad_hidden = matmul_nt(grad_rows, w_down)
     grad_up_low = (grad_hidden * silu_gate).astype(jnp.bfloat16)
     grad_gate_low = (
         grad_hidden * up_pre * (sigmoid_gate * (1.0 + gate_pre * (1.0 - sigmoid_gate)))
     ).astype(jnp.bfloat16)
-    grad_gate = matmul_tn(rows_in, grad_gate_low)
-    grad_up = matmul_tn(rows_in, grad_up_low)
     grad_input = (matmul_nt(grad_gate_low, w_gate) + matmul_nt(grad_up_low, w_up)).astype(
         jnp.bfloat16
     )
-    return (grad_input, grad_gate, grad_up, grad_down)
+    return (grad_input, hidden_low, grad_gate_low, grad_up_low)
 
 
 def feed_forward(normed_two, weights):
     mlp_low = ffn_forward(normed_two, weights[6], weights[7], weights[8])
     return mlp_low
-
-
-def feed_back(normed_two, grad_mlp, weights):
-    grad_normed, grad_gate, grad_up, grad_down = ffn_backward(
-        normed_two, grad_mlp, weights[6], weights[7], weights[8]
-    )
-    return (grad_normed, grad_gate, grad_up, grad_down)
 
 
 def recursion_forward(hidden_state, live_int, weights, context):
@@ -269,12 +699,10 @@
     )
     factor = live_int.astype(jnp.float32) * router_gate
     updated = hidden_state + factor[:, None] * (front[9] + mlp_low.astype(jnp.float32))
-    return (updated, front[13], mlp_low)
-
-
-def recursion_backward(
-    hidden_state, live_int, weights, context, pieces, mlp_low, grad_after, grads
-):
+    return (updated, front, mlp_low)
+
+
+def recursion_backward(hidden_state, live_int, weights, context, front, mlp_low, grad_after):
     (
         normed_low,
         scaled_one,
@@ -290,7 +718,7 @@
         scaled_two,
         inverse_two,
         pieces,
-    ) = attention_front(hidden_state, live_int, weights, context, pieces)
+    ) = front
     lengths_row, global_rows, cosine_table, sine_table, segment_rows, tok_dev, nback = context
     live_f = live_int.astype(jnp.float32)
     router_vec = weights[9].astype(jnp.float32)
@@ -302,15 +730,15 @@
     )
     grad_router = jnp.dot(grad_logit, hidden_state, precision=highest)
     grad_state = grad_after + grad_logit[:, None] * router_vec[None, :]
-    grad_normed_two, grad_gate, grad_up, grad_down = feed_back(
-        normed_two, grad_branch.astype(jnp.bfloat16), weights
+    grad_mlp_low = grad_branch.astype(jnp.bfloat16)
+    grad_normed_two, hidden_low, grad_gate_low, grad_up_low = ffn_backward(
+        normed_two, grad_mlp_low, weights[6], weights[7], weights[8]
     )
     grad_middle, grad_gain_two = norm_backward(
         grad_normed_two.astype(jnp.float32), scaled_two, inverse_two, weights[5].astype(jnp.float32)
     )
     grad_state = grad_state + grad_middle
     grad_attn = (grad_branch + grad_middle).astype(jnp.bfloat16)
-    grad_out = matmul_tn(mixed_rows, grad_attn)
     grad_mixed = matmul_nt(grad_attn, weights[4]).astype(jnp.bfloat16)
     grad_queries, grad_keys, grad_values = attend_back(
         queries, keys_all, values_all, allowed, log_totals, grad_mixed
@@ -344,9 +772,6 @@
         .astype(jnp.bfloat16)
     )
     grad_v_low = values_home.astype(jnp.bfloat16)
-    grad_query_w = matmul_tn(normed_low, grad_q_low)
-    grad_key_w = matmul_tn(normed_low, grad_k_low)
-    grad_value_w = matmul_tn(normed_low, grad_v_low)
     grad_normed = (
         matmul_nt(grad_q_low, weights[1])
         + matmul_nt(grad_k_low, weights[2])
@@ -356,19 +781,65 @@
         grad_normed, scaled_one, inverse_one, weights[0].astype(jnp.float32)
     )
     grad_state = grad_state + grad_input
-    adding = (
-        grad_gain_one,
-        grad_query_w,
-        grad_key_w,
-        grad_value_w,
-        grad_out,
-        grad_gain_two,
-        grad_gate,
-        grad_up,
-        grad_down,
-        grad_router,
-    )
-    return (grad_state, tuple((running + extra for running, extra in zip(grads, adding))))
+    rows = (
+        normed_two,
+        grad_mlp_low,
+        normed_low,
+        mixed_rows,
+        grad_gate_low,
+        grad_up_low,
+        hidden_low,
+        grad_q_low,
+        grad_k_low,
+        grad_v_low,
+        grad_attn,
+    )
+    return (grad_state, rows, (grad_gain_one, grad_gain_two, grad_router))
+
+
+def weight_grads(rows):
+    (n_two, g_mlp, n_one, mixed, g_gate, g_up, hidden, g_q, g_k, g_v, g_attn) = rows
+    low = jnp.bfloat16
+
+    def product(left, right):
+        return matmul_tn(left, right).astype(low)
+
+    return (
+        product(n_two, g_gate),
+        product(n_two, g_up),
+        product(g_mlp, hidden),
+        product(n_one, g_q),
+        product(n_one, g_k),
+        product(n_one, g_v),
+        product(mixed, g_attn),
+    )
+
+
+def to_parts(d_gate, d_up, d_down_t, d_q, d_k, d_v, d_o):
+    blocks = []
+    for wide in (d_gate, d_up, d_down_t, jnp.concatenate([d_q, d_k], axis=1), jnp.concatenate([d_o, d_v], axis=1)):
+        blocks += [wide[:, i : i + COLS] for i in range(0, wide.shape[1], COLS)]
+    return jnp.stack(blocks)
+
+
+def from_parts(parts):
+    wide = parts.astype(jnp.float32)
+
+    def side(low, high):
+        return jnp.concatenate([wide[i] for i in range(low, high)], axis=1)
+
+    d_down = jnp.concatenate([wide[i].T for i in range(8, 12)], axis=0)
+    width = wide.shape[1]
+    queries_keys, out_values = side(12, 14), side(14, 16)
+    return (
+        side(0, 4),
+        side(4, 8),
+        d_down,
+        queries_keys[:, :width],
+        queries_keys[:, width:],
+        out_values[:, width:],
+        out_values[:, :width],
+    )
 
 
 def on_device(
@@ -388,22 +859,12 @@
     w_router,
 ):
     n_tok = lax.axis_size("tok")
+    n_grp = lax.axis_size("grp")
     me_index = lax.axis_index("tok")
     tok_dev = hidden_in.shape[0]
     nback = min(SPAN, n_tok // 2)
     shards = (norm_attn, w_query, w_key, w_value, w_out, norm_mlp, w_gate, w_up, w_down, w_router)
-    weights = (
-        lax.all_gather(shards[0], "tok", axis=0, tiled=True),
-        lax.all_gather(shards[1], "tok", axis=0, tiled=True),
-        lax.all_gather(shards[2], "tok", axis=0, tiled=True),
-        lax.all_gather(shards[3], "tok", axis=0, tiled=True),
-        lax.all_gather(shards[4], "tok", axis=0, tiled=True),
-        lax.all_gather(shards[5], "tok", axis=0, tiled=True),
-        lax.all_gather(shards[6], "tok", axis=0, tiled=True),
-        lax.all_gather(shards[7], "tok", axis=0, tiled=True),
-        lax.all_gather(shards[8], "tok", axis=0, tiled=True),
-        lax.all_gather(shards[9], "tok", axis=0, tiled=True),
-    )
+    weights = tuple(lax.all_gather(shard, "tok", axis=0, tiled=True) for shard in shards)
     lengths_row = lengths[0]
     global_rows = me_index * tok_dev + jnp.arange(tok_dev, dtype=jnp.int32)
     segment_rows = segment_of(lengths_row, global_rows)
@@ -411,54 +872,56 @@
     context = (lengths_row, global_rows, cosine_table, sine_table, segment_rows, tok_dev, nback)
     hidden_state = hidden_in.astype(jnp.float32)
     inputs_kept = []
-    pieces_kept = []
+    fronts_kept = []
     mlp_kept = []
     for each_step in range(RECUR):
         inputs_kept.append(hidden_state)
-        hidden_state, pieces, mlp_low = recursion_forward(
+        hidden_state, front, mlp_low = recursion_forward(
             hidden_state, active[each_step], weights, context
         )
-        pieces_kept.append(pieces)
+        fronts_kept.append(front)
         mlp_kept.append(mlp_low)
-    back_weights = (
-        lax.all_gather(shards[0], "tok", axis=0, tiled=True),
-        lax.all_gather(shards[1], "tok", axis=0, tiled=True),
-        lax.all_gather(shards[2], "tok", axis=0, tiled=True),
-        lax.all_gather(shards[3], "tok", axis=0, tiled=True),
-        lax.all_gather(shards[4], "tok", axis=0, tiled=True),
-        lax.all_gather(shards[5], "tok", axis=0, tiled=True),
-        lax.all_gather(shards[6], "tok", axis=0, tiled=True),
-        lax.all_gather(shards[7], "tok", axis=0, tiled=True),
-        lax.all_gather(shards[8], "tok", axis=0, tiled=True),
-        lax.all_gather(shards[9], "tok", axis=0, tiled=True),
-    )
-    grads = tuple((jnp.zeros(matrix.shape, jnp.float32) for matrix in back_weights))
     grad_state = cotangent.astype(jnp.float32)
+    all_rows = []
+    small = None
     for each_step in reversed(range(RECUR)):
-        grad_state, grads = recursion_backward(
+        grad_state, rows, gains = recursion_backward(
             inputs_kept[each_step],
             active[each_step],
-            back_weights,
+            weights,
             context,
-            None,
+            fronts_kept[each_step],
             mlp_kept[each_step],
             grad_state,
-            grads,
         )
-    summed = lax.psum(grads, ("grp", "tok"))
+        all_rows.append(rows)
+        small = gains if small is None else tuple(a + b for a, b in zip(small, gains))
+    matrices = weight_grads(tuple(jnp.concatenate(each, axis=0) for each in zip(*all_rows)))
+    if (n_grp, n_tok) == (4, 8):
+        width = small[0].shape[0]
+        vectors = jnp.pad(jnp.stack(small), ((0, 8 - len(small)), (0, 1024 - width)))
+        parts, vectors = all_sum(to_parts(*matrices), vectors)
+        d_gate, d_up, d_down, d_q, d_k, d_v, d_o = from_parts(parts)
+        small = tuple(vectors[i, :width] for i in range(3))
+    else:
+        d_gate, d_up, d_down, d_q, d_k, d_v, d_o = lax.psum(
+            tuple(each.astype(jnp.float32) for each in matrices), ("grp", "tok")
+        )
+        d_down = d_down.T
+        small = lax.psum(small, ("grp", "tok"))
     return (
         hidden_state.astype(jnp.bfloat16),
         grad_state,
-        summed[0],
-        summed[1],
-        summed[2],
-        summed[3],
-        summed[4],
-        summed[5],
-        summed[6],
-        summed[7],
-        summed[8],
-        summed[9],
+        small[0],
+        d_q,
+        d_k,
+        d_v,
+        d_o,
+        small[1],
+        d_gate,
+        d_up,
+        d_down,
+        small[2],
     )
 
 

time: 1440 us -> 1000 us (0.69)
  waiting for transfers between devices: 647 us -> 126 us
  Pallas kernels: 0 us -> 195 us
  matrix products: 398 us -> 253 us
  other arithmetic: 58.4 us -> 112 us
  blocking collectives: 96.3 us -> 48.9 us
  local copies, waits for them, and re-layouts: 75.1 us -> 98.2 us
    psum x1 -> x0, waiting for transfers between devices: 547 us -> none  [on_device(): summed = lax.psum(grads, ('grp', 'tok'))]
    pallas_call x0 -> x1, Pallas kernels: none -> 195 us  [all_sum(): pl.pallas_call(reduce_kernel, name='all_sum', out_shape=(jax.ShapeDtypeSt...]
    dot_general x21 -> x7, matrix products: 88.9 us -> 19.5 us  [matmul_tn(): lax.dot_general(left, right, (((0,), (0,)), ((), ())), preferred_element_...]
    psum x1 -> x0, blocking collectives: 47 us -> none  [on_device(): summed = lax.psum(grads, ('grp', 'tok'))]
    transpose x0 -> x1, local copies, waits for them, and re-layouts: none -> 25.3 us  [from_parts(): d_down = jnp.concatenate([wide[i].T for i in range(8, 12)], axis=0)]
    concatenate x0 -> x5, other arithmetic: none -> 24.9 us  [the longest x4 16.2 us: side(): return jnp.concatenate([wide[i] for i in range(low, high)], axis=1)]
    dot_general x27 -> x21, matrix products: 72.6 us -> 48.2 us  [matmul(): return jnp.dot(left, right, preferred_element_type=jnp.float32)]
    sub x15 -> x0, matrix products: 22.7 us -> none  [one_head(): exponent = jnp.exp(scores - largest)]
  transfers between devices with their start and end apart: 66 -> 65, of which waited for: 13 -> 13; matrix products, arithmetic and copies ran while one was open for 10% -> 7% of each run, Pallas kernels for 0% -> 0%
where the time goes in v1:
time: 1000 us; the launch traced here: 987 us
  matrix products  253 us (25%)
  Pallas kernels  195 us (20%)
  starting transfers between devices  135 us (14%)
  waiting for transfers between devices  126 us (13%)
  other arithmetic  112 us (11%)
  local copies, waits for them, and re-layouts  98.2 us (10%)
  blocking collectives  48.9 us (5%)
  between operations  18.8 us (2%)
    pallas_call x1, Pallas kernels, all_sum(): pl.pallas_call(reduce_kernel, name='all_sum', out_shape=(jax.ShapeDtypeSt...  195 us
    ppermute x60, starting transfers between devices, from_behind(): return lax.ppermute(block, axis, route)  135 us
    all_gather x5, waiting for transfers between devices, on_device(): lax.all_gather(shard, 'tok', axis=0, tiled=True)  92.9 us
    dot_general x21, matrix products, matmul(): return jnp.dot(left, right, preferred_element_type=jnp.float32)  48.2 us
    unnamed x484, local copies, waits for them, and re-layouts  37.3 us
    all_gather x2, blocking collectives, on_device(): lax.all_gather(shard, 'tok', axis=0, tiled=True)  34.7 us
    dot_general x30, matrix products, one_head(): jnp.einsum('rgd,kd->grk', query_h, key_h, preferred_element_type=jnp.floa...  34.4 us
    ppermute x60, waiting for transfers between devices, from_behind(): return lax.ppermute(block, axis, route)  30.1 us
  transfers between devices with their start and end apart: 65, of which 13 were waited for; matrix products, arithmetic and copies ran while one was open for 7% of the time, Pallas kernels for 0%

profile of v1, /device:TPU:0, one launch (start us, length us, event | category | flops | bytes accessed | tf_op | source)
XLA Modules:
  0.0 987.1 jit_solution(17710472690157324905)
XLA Ops:
  10.9 5.9 collective-permute-start.31
  29.4 14.2 %all-reduce.4 = (bf16[960]{0:T(1024)(128)(2,1)S(1)}, bf16[960]{0:T(1024)(128)(2,1)S(1)}, bf16[960]{0:T(1024)(128)(2,1)S(1)}) all-reduce(bf16[960]{0:T(1024)(128)(2,1)S(1)} %dynamic-update-slice.1, bf16[960]{0:T(1024)(128)(2,1)S(1)} %dynamic-update-slice.2, bf16[960]{0:T(1024)(128)(2,1)S(1)} %dynamic-update-slice), channel_id=1, replica_groups=mesh['grp'=4,'tok'=8] {'tok'}, use_global_device_ids=true, to_apply=%add.2 | all-reduce | flops 2880 | bytes 11520
  45.6 17.6 %all-gather.1 = bf16[8,120,320]{1,2,0:T(8,128)(2,1)S(1)} all-gather(bf16[1,120,320]{1,2,0:T(8,128)(2,1)S(1)} %bitcast.966), channel_id=1, replica_groups=mesh['grp'=4,'tok'=8] {'tok'}, dimensions={0}, use_global_device_ids=true | all-gather | bytes 691200 | tf_op jit(solution)/shard_map/all_gather | solution.py:867
  64.2 17.1 %all-gather = bf16[8,120,320]{1,2,0:T(8,128)(2,1)S(1)} all-gather(bf16[1,120,320]{1,2,0:T(8,128)(2,1)S(1)} %bitcast.967), channel_id=1, replica_groups=mesh['grp'=4,'tok'=8] {'tok'}, dimensions={0}, use_global_device_ids=true | all-gather | bytes 691200 | tf_op jit(solution)/shard_map/all_gather | solution.py:867
  113.3 19.6 %collective-permute-start.2 = (bf16[128,320]{0,1:T(8,128)(2,1)S(1)}, bf16[128,320]{0,1:T(8,128)(2,1)S(1)}, u32[]{:S(2)}, u32[]{:S(2)}) collective-permute-start(bf16[128,320]{0,1:T(8,128)(2,1)S(1)} %get-tuple-element.837), channel_id=1, source_target_pairs={{0,3},{1,4},{2,5},{3,6},{4,7},{8,11},{9,12},{10,13},{11,14},{12,15... | collective-permute-start | bytes 245768 | tf_op jit(solution)/shard_map/ppermute | solution.py:456
  134.3 6.6 collective-permute-start
  144.4 5.9 while.84
  158.2 41.3 %all-gather.14.cloned.1.call-done = bf16[960,2560]{1,0:T(8,128)(2,1)} async-done(((bf16[120,2560]{1,0:T(8,128)(2,1)}), bf16[960,2560]{1,0:T(8,128)(2,1)}) %all-gather.14.cloned.1.call-update) | async-done | bytes 4915216 | tf_op jit(solution)/shard_map/all_gather | solution.py:867
  199.4 4.8 multiply_convert_fusion.11
  204.2 51.6 %all-gather.16.cloned.1.call-done = bf16[2560,960]{1,0:T(8,128)(2,1)} async-done(((bf16[320,960]{1,0:T(8,128)(2,1)}), bf16[2560,960]{1,0:T(8,128)(2,1)}) %all-gather.16.cloned.1.call-update) | async-done | bytes 4915216 | tf_op jit(solution)/shard_map/all_gather | solution.py:867
  255.8 5.3 multiply_reduce_fusion.18
  278.6 4.2 collective-permute-start.12
  284.7 23.8 %while.85 = (s32[]{:T(128)}, bf16[5,128,3,64]{1,3,2,0:T(8,128)(2,1)}, f32[5,3,128]{2,1,0:T(4,128)}, bf16[5,640,64]{1,2,0:T(8,128)(2,1)}, bf16[5,640,64]{1,2,0:T(...) while((s32[]{:T(128)}, ...), condition=%wide.region_14.15_spmd.clone, body=%wide.region_11.14_spmd.clone.sunk | while | flops 65232512 | bytes 3396865 | solution.py:565
  315.5 4.9 multiply_convert_fusion.10
  324.6 5.5 collective-permute-start.35
  348.1 23.9 %while.86 = (s32[]{:T(128)}, bf16[5,128,3,64]{1,3,2,0:T(8,128)(2,1)}, f32[5,3,128]{2,1,0:T(4,128)}, bf16[5,640,64]{1,2,0:T(8,128)(2,1)}, bf16[5,640,64]{1,2,0:T(...) while((s32[]{:T(128)}, ...), condition=%wide.region_20.21_spmd.clone, body=%wide.region_17.20_spmd.clone.sunk | while | flops 65232512 | bytes 3396865 | solution.py:565
  396.7 48.0 %while.87 = (s32[]{:T(128)}, f32[5,128,3,64]{1,3,2,0:T(8,128)}, f32[5,640,64]{1,2,0:T(8,128)}, f32[5,640,64]{1,2,0:T(8,128)}, bf16[5,640,64]{1,2,0:T(8,128)(2,1)...) while((s32[]{:T(128)}, f32[5,128,3,64]{1,3,2,0:T(8,128)}, ...), condition=%wide.region_26.27_spmd.clone, body=%wide.region_24.26_spmd.clone.sunk | while | flops 159891072 | bytes 8424729 | solution.py:603
  455.3 6.6 collective-permute-done.39
  468.9 3.7 collective-permute-done.41
  488.2 47.9 %while.88 = (s32[]{:T(128)}, f32[5,128,3,64]{1,3,2,0:T(8,128)}, f32[5,640,64]{1,2,0:T(8,128)}, f32[5,640,64]{1,2,0:T(8,128)}, bf16[5,640,64]{1,2,0:T(8,128)(2,1)...) while((s32[]{:T(128)}, f32[5,128,3,64]{1,3,2,0:T(8,128)}, ...), condition=%wide.region_32.33_spmd.clone, body=%wide.region_30.32_spmd.clone.sunk | while | flops 159891072 | bytes 8424729 | solution.py:603
  546.3 7.0 collective-permute-done.47
  568.0 4.3 convolution_convert_fusion.3
  574.7 4.3 convolution_convert_fusion.4
  579.1 4.3 convolution_convert_fusion.5
  591.4 47.8 %while.89 = (s32[]{:T(128)}, f32[5,128,3,64]{1,3,2,0:T(8,128)}, f32[5,640,64]{1,2,0:T(8,128)}, f32[5,640,64]{1,2,0:T(8,128)}, bf16[5,640,64]{1,2,0:T(8,128)(2,1)...) while((s32[]{:T(128)}, f32[5,128,3,64]{1,3,2,0:T(8,128)}, ...), condition=%wide.region_38.39_spmd.clone, body=%wide.region_36.38_spmd.clone.sunk | while | flops 159891072 | bytes 8424729 | solution.py:603
  695.9 195.0 %all_sum.1 = (bf16[16,960,640]{2,1,0:T(8,128)(2,1)}, f32[8,1024]{1,0:T(8,128)}) custom-call(bf16[16,960,640]{2,1,0:T(8,128)(2,1)} %fusion.163.g_ref, f32[8,1024]{1,0:T(8,128)} %select_maximum_fusion.v_ref), custom_call_target="tpu_custom_call" | custom-call | tf_op jit(solution)/shard_map/all_sum/pallas_call | solution.py:432
  892.4 21.6 %convert_element_type.636 = f32[16,960,640]{2,1,0:T(8,128)} convert(bf16[16,960,640]{2,1,0:T(8,128)(2,1)} %get-tuple-element.306) | non-fusion elementwise | flops 9830400 | bytes 58982400 | tf_op jit(solution)/shard_map/convert_element_type | solution.py:826
  914.0 25.3 %slice_bitcast_fusion.3 = (f32[640,960]{0,1:T(8,128)}, f32[640,960]{0,1:T(8,128)}, f32[640,960]{0,1:T(8,128)}, f32[640,960]{0,1:T(8,128)}, f32[960,640]{1,0:T(8,...) fusion(f32[16,960,640]{2,1,0:T(8,128)} %convert_element_type.636), kind=kLoop, calls=%fused_computation.194 | loop fusion | bytes 78643200 | tf_op jit(solution)/shard_map/transpose | solution.py:831
  942.4 4.2 pad_maximum_fusion.3
  960.0 8.7 pad_maximum_fusion.2
  968.8 5.3 pad_maximum_fusion.1
  976.1 4.3 pad_maximum_fusion
  (1006 shorter events, 474.5 us)
Async XLA Ops:
  7.2 134.5 %all-gather.8.cloned.1.call-start = ((), (), s32[]{:S(2)}) async-start(), calls=%async_computation | async-start | bytes 2211840 | tf_op jit(solution)/shard_map/all_gather | solution.py:867
  8.0 142.4 %all-gather.10.cloned.1.call-start = ((), (), s32[]{:S(2)}) async-start(), calls=%async_computation.1 | async-start | bytes 2211840 | tf_op jit(solution)/shard_map/all_gather | solution.py:867
  8.7 145.9 %all-gather.12.cloned.1.call-start = ((), (), s32[]{:S(2)}) async-start(), calls=%async_computation.2 | async-start | bytes 5529600 | tf_op jit(solution)/shard_map/all_gather | solution.py:867
  9.4 190.0 %all-gather.14.cloned.1.call-start = ((), (), s32[]{:S(2)}) async-start(), calls=%async_computation.3 | async-start | bytes 5529600 | tf_op jit(solution)/shard_map/all_gather | solution.py:867
  10.0 245.7 %all-gather.16.cloned.1.call-start = ((), (), s32[]{:S(2)}) async-start(), calls=%async_computation.4 | async-start | bytes 5898240 | tf_op jit(solution)/shard_map/all_gather | solution.py:867
  10.9 81.3 %collective-permute-start.31 = (bf16[128]{0:T(256)(128)(2,1)S(1)}, bf16[128]{0:T(256)(128)(2,1)S(1)}, u32[]{:S(2)}, u32[]{:S(2)}) collective-permute-start(bf16[128]{0:T(256)(128)(2,1)S(1)} %get-tuple-element.831), channel_id=1, source_target_pairs={{0,4},{1,5},{2,6},{3,7},{8,12},{9,13},{10,14},{11,15},{16,20},{17,... | collective-permute-start | bytes 776 | tf_op jit(solution)/shard_map/ppermute | solution.py:456
  16.8 72.8 %collective-permute-start.30 = (bf16[128]{0:T(256)(128)(2,1)S(1)}, bf16[128]{0:T(256)(128)(2,1)S(1)}, u32[]{:S(2)}, u32[]{:S(2)}) collective-permute-start(bf16[128]{0:T(256)(128)(2,1)S(1)} %get-tuple-element.831), channel_id=1, source_target_pairs={{0,3},{1,4},{2,5},{3,6},{4,7},{8,11},{9,12},{10,13},{11,14},{12,15... | collective-permute-start | bytes 776 | tf_op jit(solution)/shard_map/ppermute | solution.py:456
  19.5 66.2 %collective-permute-start.29 = (bf16[128]{0:T(256)(128)(2,1)S(1)}, bf16[128]{0:T(256)(128)(2,1)S(1)}, u32[]{:S(2)}, u32[]{:S(2)}) collective-permute-start(bf16[128]{0:T(256)(128)(2,1)S(1)} %get-tuple-element.831), channel_id=1, source_target_pairs={{0,2},{1,3},{2,4},{3,5},{4,6},{5,7},{8,10},{9,11},{10,12},{11,13},... | collective-permute-start | bytes 776 | tf_op jit(solution)/shard_map/ppermute | solution.py:456
  21.6 62.5 %collective-permute-start.28 = (bf16[128]{0:T(256)(128)(2,1)S(1)}, bf16[128]{0:T(256)(128)(2,1)S(1)}, u32[]{:S(2)}, u32[]{:S(2)}) collective-permute-start(bf16[128]{0:T(256)(128)(2,1)S(1)} %get-tuple-element.831), channel_id=1, source_target_pairs={{0,1},{1,2},{2,3},{3,4},{4,5},{5,6},{6,7},{8,9},{9,10},{10,11},{11... | collective-permute-start | bytes 776 | tf_op jit(solution)/shard_map/ppermute | solution.py:456
  23.4 77.8 %collective-permute-start.7 = (bf16[128]{0:T(256)(128)(2,1)S(1)}, bf16[128]{0:T(256)(128)(2,1)S(1)}, u32[]{:S(2)}, u32[]{:S(2)}) collective-permute-start(bf16[128]{0:T(256)(128)(2,1)S(1)} %get-tuple-element.832), channel_id=1, source_target_pairs={{0,4},{1,5},{2,6},{3,7},{8,12},{9,13},{10,14},{11,15},{16,20},{17,... | collective-permute-start | bytes 776 | tf_op jit(solution)/shard_map/ppermute | solution.py:456
  84.1 15.1 %collective-permute-start.6 = (bf16[128]{0:T(256)(128)(2,1)S(1)}, bf16[128]{0:T(256)(128)(2,1)S(1)}, u32[]{:S(2)}, u32[]{:S(2)}) collective-permute-start(bf16[128]{0:T(256)(128)(2,1)S(1)} %get-tuple-element.832), channel_id=1, source_target_pairs={{0,3},{1,4},{2,5},{3,6},{4,7},{8,11},{9,12},{10,13},{11,14},{12,15... | collective-permute-start | bytes 776 | tf_op jit(solution)/shard_map/ppermute | solution.py:456
  92.1 17.9 %collective-permute-start.19 = (bf16[128]{0:T(256)(128)(2,1)S(1)}, bf16[128]{0:T(256)(128)(2,1)S(1)}, u32[]{:S(2)}, u32[]{:S(2)}) collective-permute-start(bf16[128]{0:T(256)(128)(2,1)S(1)} %get-tuple-element.833), channel_id=1, source_target_pairs={{0,4},{1,5},{2,6},{3,7},{8,12},{9,13},{10,14},{11,15},{16,20},{17,... | collective-permute-start | bytes 776 | tf_op jit(solution)/shard_map/ppermute | solution.py:456
  95.0 13.4 %collective-permute-start.18 = (bf16[128]{0:T(256)(128)(2,1)S(1)}, bf16[128]{0:T(256)(128)(2,1)S(1)}, u32[]{:S(2)}, u32[]{:S(2)}) collective-permute-start(bf16[128]{0:T(256)(128)(2,1)S(1)} %get-tuple-element.833), channel_id=1, source_target_pairs={{0,3},{1,4},{2,5},{3,6},{4,7},{8,11},{9,12},{10,13},{11,14},{12,15... | collective-permute-start | bytes 776 | tf_op jit(solution)/shard_map/ppermute | solution.py:456
  101.2 39.8 %collective-permute-start.11 = (bf16[128,320]{0,1:T(8,128)(2,1)S(1)}, bf16[128,320]{0,1:T(8,128)(2,1)S(1)}, u32[]{:S(2)}, u32[]{:S(2)}) collective-permute-start(bf16[128,320]{0,1:T(8,128)(2,1)S(1)} %bitcast.954), channel_id=1, source_target_pairs={{0,4},{1,5},{2,6},{3,7},{8,12},{9,13},{10,14},{11,15},{16,20},{17,... | collective-permute-start | bytes 245768 | tf_op jit(solution)/shard_map/ppermute | solution.py:456
  103.6 30.7 %collective-permute-start.10 = (bf16[128,320]{0,1:T(8,128)(2,1)S(1)}, bf16[128,320]{0,1:T(8,128)(2,1)S(1)}, u32[]{:S(2)}, u32[]{:S(2)}) collective-permute-start(bf16[128,320]{0,1:T(8,128)(2,1)S(1)} %bitcast.955), channel_id=1, source_target_pairs={{0,3},{1,4},{2,5},{3,6},{4,7},{8,11},{9,12},{10,13},{11,14},{12,15... | collective-permute-start | bytes 245768 | tf_op jit(solution)/shard_map/ppermute | solution.py:456
  105.4 27.6 %collective-permute-start.9 = (bf16[128,320]{0,1:T(8,128)(2,1)S(1)}, bf16[128,320]{0,1:T(8,128)(2,1)S(1)}, u32[]{:S(2)}, u32[]{:S(2)}) collective-permute-start(bf16[128,320]{0,1:T(8,128)(2,1)S(1)} %bitcast.956), channel_id=1, source_target_pairs={{0,2},{1,3},{2,4},{3,5},{4,6},{5,7},{8,10},{9,11},{10,12},{11,13},... | collective-permute-start | bytes 245768 | tf_op jit(solution)/shard_map/ppermute | solution.py:456
  110.1 31.6 %collective-permute-start.3 = (bf16[128,320]{0,1:T(8,128)(2,1)S(1)}, bf16[128,320]{0,1:T(8,128)(2,1)S(1)}, u32[]{:S(2)}, u32[]{:S(2)}) collective-permute-start(bf16[128,320]{0,1:T(8,128)(2,1)S(1)} %get-tuple-element.837), channel_id=1, source_target_pairs={{0,4},{1,5},{2,6},{3,7},{8,12},{9,13},{10,14},{11,15},{16,20},{17,... | collective-permute-start | bytes 245768 | tf_op jit(solution)/shard_map/ppermute | solution.py:456
  113.3 28.3 %collective-permute-start.2 = (bf16[128,320]{0,1:T(8,128)(2,1)S(1)}, bf16[128,320]{0,1:T(8,128)(2,1)S(1)}, u32[]{:S(2)}, u32[]{:S(2)}) collective-permute-start(bf16[128,320]{0,1:T(8,128)(2,1)S(1)} %get-tuple-element.837), channel_id=1, source_target_pairs={{0,3},{1,4},{2,5},{3,6},{4,7},{8,11},{9,12},{10,13},{11,14},{12,15... | collective-permute-start | bytes 245768 | tf_op jit(solution)/shard_map/ppermute | solution.py:456
  262.6 20.2 %collective-permute-start.23 = (bf16[128,320]{0,1:T(8,128)(2,1)S(1)}, bf16[128,320]{0,1:T(8,128)(2,1)S(1)}, u32[]{:S(2)}, u32[]{:S(2)}) collective-permute-start(bf16[128,320]{0,1:T(8,128)(2,1)S(1)} %bitcast.962), channel_id=1, source_target_pairs={{0,4},{1,5},{2,6},{3,7},{8,12},{9,13},{10,14},{11,15},{16,20},{17,... | collective-permute-start | bytes 245768 | tf_op jit(solution)/shard_map/ppermute | solution.py:456
  265.7 12.9 %collective-permute-start.22 = (bf16[128,320]{0,1:T(8,128)(2,1)S(1)}, bf16[128,320]{0,1:T(8,128)(2,1)S(1)}, u32[]{:S(2)}, u32[]{:S(2)}) collective-permute-start(bf16[128,320]{0,1:T(8,128)(2,1)S(1)} %bitcast.963), channel_id=1, source_target_pairs={{0,3},{1,4},{2,5},{3,6},{4,7},{8,11},{9,12},{10,13},{11,14},{12,15... | collective-permute-start | bytes 245768 | tf_op jit(solution)/shard_map/ppermute | solution.py:456
  324.6 21.3 %collective-permute-start.35 = (bf16[128,320]{0,1:T(8,128)(2,1)S(1)}, bf16[128,320]{0,1:T(8,128)(2,1)S(1)}, u32[]{:S(2)}, u32[]{:S(2)}) collective-permute-start(bf16[128,320]{0,1:T(8,128)(2,1)S(1)} %bitcast.958), channel_id=1, source_target_pairs={{0,4},{1,5},{2,6},{3,7},{8,12},{9,13},{10,14},{11,15},{16,20},{17,... | collective-permute-start | bytes 245768 | tf_op jit(solution)/shard_map/ppermute | solution.py:456
  330.1 13.2 %collective-permute-start.34 = (bf16[128,320]{0,1:T(8,128)(2,1)S(1)}, bf16[128,320]{0,1:T(8,128)(2,1)S(1)}, u32[]{:S(2)}, u32[]{:S(2)}) collective-permute-start(bf16[128,320]{0,1:T(8,128)(2,1)S(1)} %bitcast.959), channel_id=1, source_target_pairs={{0,3},{1,4},{2,5},{3,6},{4,7},{8,11},{9,12},{10,13},{11,14},{12,15... | collective-permute-start | bytes 245768 | tf_op jit(solution)/shard_map/ppermute | solution.py:456
  448.2 19.1 %collective-permute-start.43 = (bf16[128,320]{0,1:T(8,128)(2,1)S(1)}, bf16[128,320]{0,1:T(8,128)(2,1)S(1)}, u32[]{:S(2)}, u32[]{:S(2)}) collective-permute-start(bf16[128,320]{0,1:T(8,128)(2,1)S(1)} %bitcast.930), channel_id=1, source_target_pairs={{4,0},{5,1},{6,2},{7,3},{12,8},{13,9},{14,10},{15,11},{20,16},{21,... | collective-permute-start | bytes 245768 | tf_op jit(solution)/shard_map/ppermute | solution.py:456
  539.7 19.3 %collective-permute-start.51 = (bf16[128,320]{0,1:T(8,128)(2,1)S(1)}, bf16[128,320]{0,1:T(8,128)(2,1)S(1)}, u32[]{:S(2)}, u32[]{:S(2)}) collective-permute-start(bf16[128,320]{0,1:T(8,128)(2,1)S(1)} %bitcast.931), channel_id=1, source_target_pairs={{4,0},{5,1},{6,2},{7,3},{12,8},{13,9},{14,10},{15,11},{20,16},{21,... | collective-permute-start | bytes 245768 | tf_op jit(solution)/shard_map/ppermute | solution.py:456
  541.0 12.3 %collective-permute-start.47 = (bf16[128,320]{0,1:T(8,128)(2,1)S(1)}, bf16[128,320]{0,1:T(8,128)(2,1)S(1)}, u32[]{:S(2)}, u32[]{:S(2)}) collective-permute-start(bf16[128,320]{0,1:T(8,128)(2,1)S(1)} %bitcast.941), channel_id=1, source_target_pairs={{4,0},{5,1},{6,2},{7,3},{12,8},{13,9},{14,10},{15,11},{20,16},{21,... | collective-permute-start | bytes 245768 | tf_op jit(solution)/shard_map/ppermute | solution.py:456
  543.6 12.3 %collective-permute-start.46 = (bf16[128,320]{0,1:T(8,128)(2,1)S(1)}, bf16[128,320]{0,1:T(8,128)(2,1)S(1)}, u32[]{:S(2)}, u32[]{:S(2)}) collective-permute-start(bf16[128,320]{0,1:T(8,128)(2,1)S(1)} %bitcast.937), channel_id=1, source_target_pairs={{3,0},{4,1},{5,2},{6,3},{7,4},{11,8},{12,9},{13,10},{14,11},{15,12... | collective-permute-start | bytes 245768 | tf_op jit(solution)/shard_map/ppermute | solution.py:456
  544.9 12.7 %collective-permute-start.45 = (bf16[128,320]{0,1:T(8,128)(2,1)S(1)}, bf16[128,320]{0,1:T(8,128)(2,1)S(1)}, u32[]{:S(2)}, u32[]{:S(2)}) collective-permute-start(bf16[128,320]{0,1:T(8,128)(2,1)S(1)} %bitcast.935), channel_id=1, source_target_pairs={{2,0},{3,1},{4,2},{5,3},{6,4},{7,5},{10,8},{11,9},{12,10},{13,11},... | collective-permute-start | bytes 245768 | tf_op jit(solution)/shard_map/ppermute | solution.py:456
  642.9 34.9 %collective-permute-start.59 = (bf16[128,320]{0,1:T(8,128)(2,1)S(1)}, bf16[128,320]{0,1:T(8,128)(2,1)S(1)}, u32[]{:S(2)}, u32[]{:S(2)}) collective-permute-start(bf16[128,320]{0,1:T(8,128)(2,1)S(1)} %bitcast.921), channel_id=1, source_target_pairs={{4,0},{5,1},{6,2},{7,3},{12,8},{13,9},{14,10},{15,11},{20,16},{21,... | collective-permute-start | bytes 245768 | tf_op jit(solution)/shard_map/ppermute | solution.py:456
  644.3 27.6 %collective-permute-start.55 = (bf16[128,320]{0,1:T(8,128)(2,1)S(1)}, bf16[128,320]{0,1:T(8,128)(2,1)S(1)}, u32[]{:S(2)}, u32[]{:S(2)}) collective-permute-start(bf16[128,320]{0,1:T(8,128)(2,1)S(1)} %bitcast.933), channel_id=1, source_target_pairs={{4,0},{5,1},{6,2},{7,3},{12,8},{13,9},{14,10},{15,11},{20,16},{21,... | collective-permute-start | bytes 245768 | tf_op jit(solution)/shard_map/ppermute | solution.py:456
  645.9 27.3 %collective-permute-start.52 = (bf16[128,320]{0,1:T(8,128)(2,1)S(1)}, bf16[128,320]{0,1:T(8,128)(2,1)S(1)}, u32[]{:S(2)}, u32[]{:S(2)}) collective-permute-start(bf16[128,320]{0,1:T(8,128)(2,1)S(1)} %bitcast.932), channel_id=1, source_target_pairs={{1,0},{2,1},{3,2},{4,3},{5,4},{6,5},{7,6},{9,8},{10,9},{11,10},{12... | collective-permute-start | bytes 245768 | tf_op jit(solution)/shard_map/ppermute | solution.py:456
  647.2 27.3 %collective-permute-start.54 = (bf16[128,320]{0,1:T(8,128)(2,1)S(1)}, bf16[128,320]{0,1:T(8,128)(2,1)S(1)}, u32[]{:S(2)}, u32[]{:S(2)}) collective-permute-start(bf16[128,320]{0,1:T(8,128)(2,1)S(1)} %bitcast.925), channel_id=1, source_target_pairs={{3,0},{4,1},{5,2},{6,3},{7,4},{11,8},{12,9},{13,10},{14,11},{15,12... | collective-permute-start | bytes 245768 | tf_op jit(solution)/shard_map/ppermute | solution.py:456
  648.5 27.4 %collective-permute-start.53 = (bf16[128,320]{0,1:T(8,128)(2,1)S(1)}, bf16[128,320]{0,1:T(8,128)(2,1)S(1)}, u32[]{:S(2)}, u32[]{:S(2)}) collective-permute-start(bf16[128,320]{0,1:T(8,128)(2,1)S(1)} %bitcast.922), channel_id=1, source_target_pairs={{2,0},{3,1},{4,2},{5,3},{6,4},{7,5},{10,8},{11,9},{12,10},{13,11},... | collective-permute-start | bytes 245768 | tf_op jit(solution)/shard_map/ppermute | solution.py:456
  (247 other events, 2020.9 us)
Sparse Core Ops, SparseCore 0:
  9.7 31.1 all-gather.7
  42.5 33.7 all-gather.9
  78.0 55.1 all-gather.11
  134.7 64.7 all-gather.13
  200.9 54.8 all-gather.15

commit v2 on v1

v2 whole, which is shorter than its diff:
```python
import jax
import jax.numpy as jnp
from jax import lax
from jax.experimental import pallas as pl
from jax.experimental.pallas import tpu as pltpu
from jax.sharding import PartitionSpec as P

MESH = pl.DeviceIdType.MESH

H = 15
KVH = 5
HD = 64
RECUR = 3
SPAN = 16

epsilon = 1e-05
theta = 10000.0
masked = -1000000000.0

def ends_of(lengths_row):
    count = lengths_row.shape[0]
    until = jnp.arange(count)[:, None] >= jnp.arange(count)[None, :]
    return jnp.sum(jnp.where(until, lengths_row[None, :], 0), axis=1)


def segment_of(lengths_row, global_rows):
    ends_at = ends_of(lengths_row)
    return jnp.sum((global_rows[:, None] >= ends_at[None, :]).astype(jnp.int32), axis=1)


def position_of(lengths_row, global_rows, segments):
    ends_at = ends_of(lengths_row)
    starts_at = ends_at - lengths_row
    picked = segments[:, None] == jnp.arange(lengths_row.shape[0], dtype=jnp.int32)[None, :]
    return global_rows - jnp.sum(jnp.where(picked, starts_at[None, :], 0), axis=1)


def rotary_tables(positions):
    half_dim = HD // 2
    inverse = jnp.power(theta, -jnp.arange(half_dim, dtype=jnp.float32) * (2.0 / HD))
    angle = positions.astype(jnp.float32)[..., None] * inverse
    return (jnp.cos(angle), jnp.sin(angle))


PARTS = 16
HALF = 480
COLS = 640
STREAMS = (("x", True, 0, 160), ("y", True, 160, 160), ("x", False, 320, 80), ("y", False, 400, 80))


def place():
    g, t = lax.axis_index("grp"), lax.axis_index("tok")
    return g // 2, lax.rem(g, 2), t // 2, lax.rem(t, 2)


def dev(y, x, z, c):
    return (y * 2 + x, z * 2 + c)


def pick(z, values):
    out = jnp.int32(values[3])
    for i in (2, 1, 0):
        out = jnp.where(z == i, jnp.int32(values[i]), out)
    return out


def copy_to(src, dst, send, recv, device):
    return pltpu.make_async_remote_copy(src_ref=src, dst_ref=dst, send_sem=send, recv_sem=recv, device_id=device, device_id_type=MESH)


def add_rows(dst, src, rows, step):
    def body(i, _):
        at = pl.ds(pl.multiple_of(i * step, step), step)
        dst[at, :] = dst[at, :] + src[at, :]
        return 0
    lax.fori_loop(0, rows // step, body, 0)


def reduce_kernel(g_ref, v_ref, o_ref, vo_ref, mine, other, ra0, ra1, ra2, ra3, rz0, rz1, rz2, rz3, rb0, rb1, rb2, rb3,
                  vrecv, load_sem, core_s, core_r, as_, ar, zs, zr, bs, br, ob, obr, oz, ozr, oa, oar, oc, ocr, vs, vr, own_sem):
    y, x, z, c = place()
    ra, rz, rb = (ra0, ra1, ra2, ra3), (rz0, rz1, rz2, rz3), (rb0, rb1, rb2, rb3)
    partner = dev(y, x, z, 1 - c)
    across = {"x": dev(y, 1 - x, z, c), "y": dev(1 - y, x, z, c)}
    left, right = dev(y, x, z - 1, c), dev(y, x, z + 1, c)
    at_axis = {"x": x, "y": y}
    order = (pick(z, (3, 3, 0, 0)), pick(z, (2, 0, 3, 1)), pick(z, (1, 2, 1, 2)), z)

    bar = pltpu.get_barrier_semaphore()
    for d in (partner, across["x"], across["y"]):
        pl.semaphore_signal(bar, inc=1, device_id=d, device_id_type=MESH)

    @pl.when(z > 0)
    def _():
        pl.semaphore_signal(bar, inc=1, device_id=left, device_id_type=MESH)

    @pl.when(z < 3)
    def _():
        pl.semaphore_signal(bar, inc=1, device_id=right, device_id_type=MESH)
    far = dev(y, x, jnp.where(z < 2, z + 2, z - 2), c)
    pl.semaphore_signal(bar, inc=1, device_id=far, device_id_type=MESH)
    pl.semaphore_wait(bar, 4 + (z > 0).astype(jnp.int32) + (z < 3).astype(jnp.int32))

    def part_xy(px, py, pz):
        return (px * 2 + py) * 4 + pz

    def part_of(s, pa, pb, pz):
        return part_xy(pa, pb, pz) if STREAMS[s][0] == "x" else part_xy(pb, pa, pz)

    def ab(s):
        a = STREAMS[s][0]
        b = "y" if a == "x" else "x"
        return at_axis[a], at_axis[b], across[a], across[b]

    def core_copy(p):
        return copy_to(g_ref.at[p, pl.ds(pl.multiple_of((1 - c) * HALF, HALF), HALF)], other.at[p], core_s.at[p], core_r.at[p], partner)

    def load(p):
        return pltpu.make_async_copy(g_ref.at[p, pl.ds(pl.multiple_of(c * HALF, HALF), HALF)], mine.at[p], load_sem.at[p])

    waits = []
    seq = [(k, px, py) for k in range(4) for px, py in ((1 - x, 1 - y), (1 - x, y), (x, 1 - y), (x, y))]
    for k, px, py in seq:
        p = part_xy(px, py, order[k])
        core_copy(p).start()
        load(p).start()

    def a_copy(s, pb, pz):
        a, b, to_a, _ = ab(s)
        _, _, r0, n = STREAMS[s]
        return copy_to(mine.at[part_of(s, 1 - a, pb, pz), pl.ds(r0, n)], ra[s].at[pb * 4 + pz], as_.at[s, pb * 4 + pz], ar.at[s, pb * 4 + pz], to_a)

    def core_step(k):
        for i, (px, py) in enumerate(((1 - x, 1 - y), (1 - x, y), (x, 1 - y), (x, y))):
            p = part_xy(px, py, order[k])
            load(p).wait()
            core_copy(p).wait_recv()
            add_rows(mine.at[p], other.at[p], HALF, 16)
            for s in range(4):
                a_axis = STREAMS[s][0]
                if i == 0 or (i == 1 and a_axis == "x") or (i == 2 and a_axis == "y"):
                    pb = py if a_axis == "x" else px
                    cp = a_copy(s, pb, order[k])
                    cp.start()
                    waits.append(cp)

    def z_copy(s, pb, pz, to_right):
        a, b, _, _ = ab(s)
        _, _, r0, n = STREAMS[s]
        src = mine.at[part_of(s, a, pb, pz), pl.ds(r0, n)]
        slot = pz if to_right else jnp.where(pz == z - 1, 4, pz)
        i = pb * 5 + slot
        return copy_to(src, rz[s].at[i], zs.at[s, i], zr.at[s, i], right if to_right else left)

    def z_wait(s, pb, slot):
        _, _, r0, n = STREAMS[s]
        i = pb * 5 + slot
        copy_to(mine.at[0, pl.ds(r0, n)], rz[s].at[i], zs.at[s, i], zr.at[s, i], left).wait_recv()

    def z_step(s, pb, k):
        a, b, _, _ = ab(s)
        _, _, r0, n = STREAMS[s]
        pz = order[k]
        acc = mine.at[part_of(s, a, pb, pz), pl.ds(r0, n)]
        if k < 3:
            up = jnp.where(pz > z, (z > 0).astype(jnp.int32), (z < 3).astype(jnp.int32))

            @pl.when(up == 1)
            def _():
                z_wait(s, pb, pz)
                add_rows(acc, rz[s].at[pb * 5 + pz], n, 16)

            @pl.when(pz > z)
            def _():
                z_copy(s, pb, pz, True).start()

            @pl.when(pz < z)
            def _():
                z_copy(s, pb, pz, False).start()
        else:
            @pl.when(z > 0)
            def _():
                z_wait(s, pb, z)
                add_rows(acc, rz[s].at[pb * 5 + z], n, 16)

            @pl.when(z < 3)
            def _():
                z_wait(s, pb, 4)
                add_rows(acc, rz[s].at[pb * 5 + 4], n, 16)

    def z_drain(s, pb, k):
        pz = order[k]

        @pl.when(pz > z)
        def _():
            z_copy(s, pb, pz, True).wait_send()

        @pl.when(pz < z)
        def _():
            z_copy(s, pb, pz, False).wait_send()

    def a_step(s, pb, k):
        a, b, to_a, _ = ab(s)
        _, _, r0, n = STREAMS[s]
        pz = order[k]
        a_copy(s, pb, pz).wait_recv()
        add_rows(mine.at[part_of(s, a, pb, pz), pl.ds(r0, n)], ra[s].at[pb * 4 + pz], n, 16)

    def b_copy(s, pz):
        a, b, _, to_b = ab(s)
        _, second_z, r0, n = STREAMS[s]
        i = 0 if second_z else pz
        return copy_to(mine.at[part_of(s, a, 1 - b, pz), pl.ds(r0, n)], rb[s].at[i], bs.at[s, i], br.at[s, i], to_b)

    def b_step(s, pz):
        a, b, _, _ = ab(s)
        _, second_z, r0, n = STREAMS[s]
        i = 0 if second_z else pz
        b_copy(s, pz).wait_recv()
        add_rows(mine.at[part_of(s, a, b, pz), pl.ds(r0, n)], rb[s].at[i], n, 16)

    def stream_step(k):
        for s in range(4):
            _, b, _, _ = ab(s)
            if STREAMS[s][1]:
                a_step(s, 1 - b, k)
                z_step(s, 1 - b, k)
                a_step(s, b, k)
                z_step(s, b, k)
                if k == 3:
                    cp = b_copy(s, z)
                    cp.start()
                    waits.append(cp)
            else:
                a_step(s, 1 - b, k)
                cp = b_copy(s, order[k])
                cp.start()
                waits.append(cp)
                a_step(s, b, k)

    def stream_step2(k):
        for s in range(4):
            _, b, _, _ = ab(s)
            if not STREAMS[s][1]:
                b_step(s, order[k])
                z_step(s, b, k)
            elif k == 3:
                b_step(s, z)

    def vec_to(i):
        return (partner, across["x"], across["y"], dev(y, x, jnp.where(lax.rem(z, 2) == 0, z + 1, z - 1), c), far)[i]

    def vec_copy(i):
        return copy_to(vo_ref, vrecv.at[i], vs.at[i], vr.at[i], vec_to(i))

    def vec_start(i):
        vec_copy(i).start()

    def vec_end(i):
        vec_copy(i).wait()
        vo_ref[...] = vo_ref[...] + vrecv[i]

    vo_ref[...] = v_ref[...]
    vec_start(0)
    core_step(0)
    vec_end(0)
    vec_start(1)
    core_step(1)
    vec_end(1)
    vec_start(2)
    stream_step(0)
    vec_end(2)
    vec_start(3)
    core_step(2)
    stream_step2(0)
    vec_end(3)
    vec_start(4)
    stream_step(1)
    core_step(3)
    stream_step2(1)
    vec_end(4)
    stream_step(2)
    stream_step2(2)
    stream_step(3)

    half0 = c * HALF

    def out_at(s, p):
        _, _, r0, n = STREAMS[s]
        return o_ref.at[p, pl.ds(pl.multiple_of(half0 + r0, 16), n)]

    def mine_at(s, p):
        _, _, r0, n = STREAMS[s]
        return mine.at[p, pl.ds(r0, n)]

    def go(cp):
        cp.start()
        waits.append(cp)

    def to_core(s, p, src):
        return copy_to(src, out_at(s, p), oc.at[s, p], ocr.at[s, p], partner)

    def to_a(s, pb, pz, src):
        a, b, na, _ = ab(s)
        return copy_to(src, out_at(s, part_of(s, a, pb, pz)), oa.at[s, pb * 4 + pz], oar.at[s, pb * 4 + pz], na)

    def to_b(s, pz, src):
        a, b, _, nb = ab(s)
        return copy_to(src, out_at(s, part_of(s, a, b, pz)), ob.at[s, pz], obr.at[s, pz], nb)

    def to_z(s, pb, pz, src, to_right):
        a, b, _, _ = ab(s)
        i = pb * 8 + pz * 2 + (0 if to_right else 1)
        return copy_to(src, out_at(s, part_of(s, a, pb, pz)), oz.at[s, i], ozr.at[s, pb * 4 + pz], right if to_right else left)

    def spread_z(s, pb, pz, src, from_left=None):
        if from_left is None:
            @pl.when(z < 3)
            def _():
                to_z(s, pb, pz, src, True).start()

            @pl.when(z > 0)
            def _():
                to_z(s, pb, pz, src, False).start()
        elif from_left:
            @pl.when(z < 3)
            def _():
                to_z(s, pb, pz, src, True).start()
        else:
            @pl.when(z > 0)
            def _():
                to_z(s, pb, pz, src, False).start()

    for s in range(4):
        a, b, _, _ = ab(s)
        p = part_of(s, a, b, z)
        if STREAMS[s][1]:
            b_step(s, z)
            src = mine_at(s, p)
            go(to_b(s, z, src))
            spread_z(s, b, z, src)
            go(to_a(s, b, z, src))
        else:
            b_step(s, z)
            z_step(s, b, 3)
            src = mine_at(s, p)
            spread_z(s, b, z, src)
            go(to_b(s, z, src))
            go(to_a(s, b, z, src))
        go(to_core(s, p, src))
        pltpu.make_async_copy(src, out_at(s, p), own_sem.at[s]).start()

    def got_b(s, pz):
        a, b, _, _ = ab(s)
        p = part_of(s, a, 1 - b, pz)
        src = out_at(s, p)
        copy_to(src, src, ob.at[s, pz], obr.at[s, pz], partner).wait_recv()
        if STREAMS[s][1]:
            spread_z(s, 1 - b, pz, src)
        to_a(s, 1 - b, pz, src).start()
        to_core(s, p, src).start()

    def got_z(s, pb, pz, from_left):
        a, b, _, _ = ab(s)
        p = part_of(s, a, pb, pz)
        src = out_at(s, p)
        copy_to(src, src, oz.at[s, 0], ozr.at[s, pb * 4 + pz], partner).wait_recv()
        spread_z(s, pb, pz, src, from_left)
        to_a(s, pb, pz, src).start()
        to_core(s, p, src).start()
        if not STREAMS[s][1]:
            to_b(s, pz, src).start()

    def got_a(s, pb, pz):
        a, b, _, _ = ab(s)
        p = part_of(s, 1 - a, pb, pz)
        src = out_at(s, p)
        copy_to(src, src, oa.at[s, pb * 4 + pz], oar.at[s, pb * 4 + pz], partner).wait_recv()
        to_core(s, p, src).start()

    for s in range(4):
        got_b(s, z)
    for s in range(4):
        a, b, _, _ = ab(s)
        got_a(s, b, z)
        got_a(s, 1 - b, z)
    for t in range(1, 4):
        for lft in (True, False):
            pz = z - t if lft else z + t
            ok = (z >= t) if lft else (z + t <= 3)

            @pl.when(ok)
            def _():
                for s in range(4):
                    a, b, _, _ = ab(s)
                    got_z(s, b, pz, lft)
                    if STREAMS[s][1]:
                        got_z(s, 1 - b, pz, lft)
                for s in range(4):
                    if not STREAMS[s][1]:
                        got_b(s, pz)
                for s in range(4):
                    a, b, _, _ = ab(s)
                    got_a(s, b, pz)
                    got_a(s, 1 - b, pz)

    for cp in waits:
        cp.wait_send()
    for k, px, py in seq:
        core_copy(part_xy(px, py, order[k])).wait_send()
    for s in range(4):
        a, b, _, _ = ab(s)
        pltpu.make_async_copy(mine_at(s, part_of(s, a, b, z)), out_at(s, part_of(s, a, b, z)), own_sem.at[s]).wait()
        pbs = (b, 1 - b) if STREAMS[s][1] else (b,)
        for pb in pbs:
            for k in range(3):
                z_drain(s, pb, k)
        for pz in range(4):
            for pb in pbs:
                src = out_at(s, part_of(s, a, pb, pz))

                @pl.when((z >= pz) & (z < 3))
                def _():
                    to_z(s, pb, pz, src, True).wait_send()

                @pl.when((z <= pz) & (z > 0))
                def _():
                    to_z(s, pb, pz, src, False).wait_send()
            for pb in (0, 1):
                src = out_at(s, part_of(s, a, pb, pz))

                @pl.when(((pb == b) & (pz == z)) == False)
                def _():
                    to_a(s, pb, pz, src).wait_send()
            if not STREAMS[s][1]:
                @pl.when(z != pz)
                def _():
                    to_b(s, pz, out_at(s, 0)).wait_send()
        for p in range(16):
            src = out_at(s, p)

            @pl.when(p != part_of(s, a, b, z))
            def _():
                to_core(s, p, src).wait_send()
            _, _, r0, n = STREAMS[s]
            dst = o_ref.at[p, pl.ds(pl.multiple_of((1 - c) * HALF + r0, 16), n)]
            copy_to(dst, dst, oc.at[s, p], ocr.at[s, p], partner).wait_recv()


def all_sum(grads, vectors):
    dma = pltpu.SemaphoreType.DMA
    bf = jnp.bfloat16
    rows = [s[3] for s in STREAMS]
    return pl.pallas_call(
        reduce_kernel,
        name="all_sum",
        out_shape=(jax.ShapeDtypeStruct(grads.shape, bf), jax.ShapeDtypeStruct(vectors.shape, jnp.float32)),
        in_specs=[pl.BlockSpec(memory_space=pl.ANY), pl.BlockSpec(memory_space=pltpu.VMEM)],
        out_specs=(pl.BlockSpec(memory_space=pl.ANY), pl.BlockSpec(memory_space=pltpu.VMEM)),
        scratch_shapes=[
            pltpu.VMEM((PARTS, HALF, COLS), bf), pltpu.VMEM((PARTS, HALF, COLS), bf),
            *[pltpu.VMEM((8, n, COLS), bf) for n in rows],
            *[pltpu.VMEM((10, n, COLS), bf) for n in rows],
            *[pltpu.VMEM((1 if s[1] else 4, s[3], COLS), bf) for s in STREAMS],
            pltpu.VMEM((5, *vectors.shape), jnp.float32),
            dma((16,)), dma((16,)), dma((16,)),
            dma((4, 8)), dma((4, 8)), dma((4, 10)), dma((4, 10)), dma((4, 4)), dma((4, 4)),
            dma((4, 4)), dma((4, 4)), dma((4, 16)), dma((4, 8)), dma((4, 8)), dma((4, 8)), dma((4, 16)), dma((4, 16)),
            dma((5,)), dma((5,)), dma((4,)),
        ],
        compiler_params=pltpu.CompilerParams(collective_id=1, has_side_effects=True, vmem_limit_bytes=56 * 2**20),
    )(grads, vectors)


F32 = jnp.float32
BF = jnp.bfloat16
CHUNK = 512
WEIGHTS = ("wq", "wk", "wv", "wo", "wg", "wu", "wd")


def dot_nn(left, right):
    return lax.dot_general(left, right, (((1,), (0,)), ((), ())), preferred_element_type=F32)


def dot_nt(left, right):
    return lax.dot_general(left, right, (((1,), (1,)), ((), ())), preferred_element_type=F32)


def rope_lanes(tensor, cosine, sine, sign):
    rows, width = tensor.shape
    lane = lax.broadcasted_iota(jnp.int32, (rows, 2 * HD), 1)
    first = lax.rem(lane, HD) < HD // 2
    out = []
    for i in range(0, width, 2 * HD):
        piece = tensor[:, i : i + 2 * HD]
        other = jnp.where(first, pltpu.roll(piece, 2 * HD - HD // 2, 1), pltpu.roll(piece, HD // 2, 1))
        out.append(piece * cosine + (other * sine) * sign)
    return jnp.concatenate(out, axis=1)


def inverse_of(rows):
    return lax.rsqrt(jnp.mean(rows * rows, axis=1, keepdims=True) + epsilon)


def front_part(r, wait, state):
    gain = r["gains"][0:1, :]
    normed = (state * inverse_of(state) * gain).astype(BF)
    r["normed"][...] = normed
    wait("wk")
    keys = dot_nn(normed, r["wk_v"][...])
    wait("wv")
    values = dot_nn(normed, r["wv_v"][...])
    wait("wq")
    queries = dot_nn(normed, r["wq_v"][...])
    turned = rope_lanes(jnp.concatenate([queries, keys], axis=1), r["cos"][...], r["sin"][...], 1.0).astype(BF)
    qw = queries.shape[1]
    r["q"][...] = turned[:, :qw]
    r["kv"][...] = jnp.concatenate([turned[:, qw:], values.astype(BF)], axis=1)


def head_rows(tensor, g):
    per = H // KVH
    return jnp.concatenate([tensor[:, (g * per + i) * HD : (g * per + i + 1) * HD] for i in range(per)], axis=0)


def window(r):
    rows = r["mask"].shape[0]
    start = lax.rem(lax.axis_index("tok"), 2) * r["q_in"].shape[0]
    return r["kvw"][pl.ds(pl.multiple_of(start, 128), rows), :]


def attention_part(r):
    per = H // KVH
    kv = window(r)
    q = r["q_in"][...]
    rows = q.shape[0]
    allowed = jnp.concatenate([r["mask"][...]] * per, axis=1) > 0
    mixed_t, logs = [], []
    for g in range(KVH):
        k_g = kv[:, g * HD : (g + 1) * HD]
        v_g = kv[:, (KVH + g) * HD : (KVH + g + 1) * HD]
        scores = jnp.where(allowed, dot_nt(k_g, head_rows(q, g)) * HD**-0.5, masked)
        largest = jnp.max(scores, axis=0, keepdims=True)
        exponent = jnp.exp(scores - largest)
        total = jnp.sum(exponent, axis=0, keepdims=True)
        probs = (exponent * (1.0 / total)).astype(BF)
        mix = dot_nn(v_g.T, probs)
        mixed_t += [mix[:, i * rows : (i + 1) * rows] for i in range(per)]
        logs.append(largest + jnp.log(total))
    r["lse"][...] = jnp.concatenate(logs + [logs[0]] * (r["lse"].shape[0] - KVH), axis=0)
    return jnp.concatenate(mixed_t, axis=0).T.astype(BF)


def rest_part(r, wait):
    state = r["state"][...]
    mixed = attention_part(r)
    r["mixed"][...] = mixed
    wait("wo")
    attn_out = dot_nn(mixed, r["wo_v"][...])
    middle = state + attn_out
    r["middle"][...] = middle
    normed_two = (middle * inverse_of(middle) * r["gains"][1:2, :]).astype(BF)
    r["normed_two"][...] = normed_two
    wait("wg")
    wait("wu")
    wait("wd")
    ff = r["wg_v"].shape[1]
    mlp = jnp.zeros(state.shape, F32)
    for i in range(0, ff, CHUNK):
        at = slice(i, i + CHUNK)
        gate = dot_nn(normed_two, r["wg_v"][:, at])
        up = dot_nn(normed_two, r["wu_v"][:, at])
        r["gate"][:, at] = gate
        r["up"][:, at] = up
        hidden = (gate * jax.nn.sigmoid(gate) * up).astype(BF)
        r["hidden"][:, at] = hidden
        mlp = mlp + dot_nn(hidden, r["wd_v"][at, :])
    branch = attn_out + mlp.astype(BF).astype(F32)
    r["branch"][...] = branch
    router = jax.nn.sigmoid(jnp.sum(state * r["gains"][2:3, :], axis=1, keepdims=True))
    return state + (r["live"][:, 0:1] * router) * branch


def norm_back(grad, rows, gain):
    inverse = inverse_of(rows)
    scaled = rows * inverse
    weighted = grad * gain
    inner = jnp.mean(weighted * scaled, axis=1, keepdims=True)
    return inverse * (weighted - scaled * inner), jnp.sum(grad * scaled, axis=0, keepdims=True)


def back_part(r, wait, grad_after):
    state, live = r["b_state"][...], r["b_live"][:, 0:1]
    width = state.shape[1]
    router_vec = r["gains"][2:3, :]
    router = jax.nn.sigmoid(jnp.sum(state * router_vec, axis=1, keepdims=True))
    d_branch = (live * router) * grad_after
    d_logit = live * (router * (1.0 - router)) * jnp.sum(r["b_branch"][...] * grad_after, axis=1, keepdims=True)
    d_router = jnp.sum(d_logit * state, axis=0, keepdims=True)
    d_mlp = d_branch.astype(BF)
    r["d_mlp"][...] = d_mlp
    wait("wd")
    wait("wg")
    wait("wu")
    ff = r["wg_v"].shape[1]
    d_two = jnp.zeros(state.shape, F32)
    for i in range(0, ff, CHUNK):
        at = slice(i, i + CHUNK)
        gate, up = r["b_gate"][:, at], r["b_up"][:, at]
        sig = jax.nn.sigmoid(gate)
        d_hidden = dot_nt(d_mlp, r["wd_v"][at, :])
        d_up = (d_hidden * (gate * sig)).astype(BF)
        d_gate = (d_hidden * up * (sig * (1.0 + gate * (1.0 - sig)))).astype(BF)
        r["d_up"][:, at] = d_up
        r["d_gate"][:, at] = d_gate
        d_two = d_two + dot_nt(d_gate, r["wg_v"][:, at]) + dot_nt(d_up, r["wu_v"][:, at])
    d_two = d_two.astype(BF).astype(F32)
    d_middle, d_gain_two = norm_back(d_two, r["b_middle"][...], r["gains"][1:2, :])
    r["acc_out"][1:2, :width] = r["acc"][1:2, :width] + d_gain_two
    r["acc_out"][2:3, :width] = r["acc"][2:3, :width] + d_router
    d_attn = (d_branch + d_middle).astype(BF)
    r["d_attn"][...] = d_attn
    r["d_state"][...] = grad_after + d_logit * router_vec + d_middle
    wait("wo")
    d_mixed = dot_nt(d_attn, r["wo_v"][...]).astype(BF)

    per = H // KVH
    kv = window(r)
    q = r["q_in"][...]
    rows = q.shape[0]
    allowed = jnp.concatenate([r["mask"][...]] * per, axis=1) > 0
    d_keys, d_values, dq_t = [], [], []
    for g in range(KVH):
        k_g = kv[:, g * HD : (g + 1) * HD]
        v_g = kv[:, (KVH + g) * HD : (KVH + g + 1) * HD]
        q_g, do_g = head_rows(q, g), head_rows(d_mixed, g)
        scores = jnp.where(allowed, dot_nt(k_g, q_g) * HD**-0.5, masked)
        probs = jnp.exp(scores - r["b_lse"][g : g + 1, :])
        d_values.append(dot_nn(probs.astype(BF), do_g))
        d_probs = dot_nt(v_g, do_g)
        d_scores = (probs * (d_probs - jnp.sum(probs * d_probs, axis=0, keepdims=True))).astype(BF)
        d_keys.append(dot_nn(d_scores, q_g) * HD**-0.5)
        dq = dot_nn(k_g.T, d_scores) * HD**-0.5
        dq_t += [dq[:, i * rows : (i + 1) * rows] for i in range(per)]
    d_queries = jnp.concatenate(dq_t + [jnp.zeros((HD, rows), F32)], axis=0).T
    d_queries = rope_lanes(d_queries, r["cos"][...], r["sin"][...], -1.0)
    r["d_q"][...] = d_queries[:, : H * HD].astype(BF)
    start = lax.rem(lax.axis_index("tok"), 2) * rows
    partial = r["dkv"]
    keep = partial.shape[0] - kv.shape[0]
    partial[pl.ds(pl.multiple_of((1 - lax.rem(lax.axis_index("tok"), 2)) * kv.shape[0], 128), keep), :] = jnp.zeros((keep, kv.shape[1]), BF)
    partial[pl.ds(pl.multiple_of(start, 128), kv.shape[0]), :] = jnp.concatenate(d_keys + d_values, axis=1).astype(BF)


def home_part(r, wait):
    half = KVH * HD
    total = r["home"][0].astype(F32)
    for i in range(1, r["home"].shape[0]):
        total = total + r["home"][i].astype(F32)
    rows = total.shape[0]
    padded = jnp.concatenate([total[:, :half], jnp.zeros((rows, half % (2 * HD)), F32)], axis=1)
    d_keys = rope_lanes(padded, r["cos"][...], r["sin"][...], -1.0)[:, :half].astype(BF)
    d_values = total[:, half:].astype(BF)
    r["d_k"][...] = d_keys
    r["d_v"][...] = d_values
    wait("wq")
    wait("wk")
    wait("wv")
    d_normed = dot_nt(r["h_dq"][...], r["wq_v"][...]) + dot_nt(d_keys, r["wk_v"][...]) + dot_nt(d_values, r["wv_v"][...])
    state = r["h_state"][...]
    width = state.shape[1]
    d_in, d_gain = norm_back(d_normed, state, r["gains"][0:1, :])
    r["acc_out"][0:1, :width] = r["acc"][0:1, :width] + d_gain
    return r["h_d_state"][...] + d_in


def stage(name, parts, needed, inputs, outputs, weights, rename=None):
    in_names, out_names = list(inputs), list(outputs)
    w_names = [w for w in needed]

    def body(*refs):
        it = iter(refs)
        r = {n: next(it) for n in in_names}
        src = {n: next(it) for n in w_names}
        for n in out_names:
            r[n] = next(it)
        for n in w_names:
            r[n + "_v"] = next(it)
        sems = next(it)
        copies = {n: pltpu.make_async_copy(src[n], r[n + "_v"], sems.at[i]) for i, n in enumerate(w_names)}
        for n in w_names:
            copies[n].start()
        done = set()

        def wait(n):
            if n not in done:
                copies[n].wait()
                done.add(n)

        parts(r, wait)
        for n in w_names:
            wait(n)

    vm = pl.BlockSpec(memory_space=pltpu.VMEM)
    out = pl.pallas_call(
        body,
        name=name,
        out_shape=tuple(outputs.values()),
        in_specs=[vm] * len(in_names) + [pl.BlockSpec(memory_space=pl.ANY)] * len(w_names),
        out_specs=tuple([vm] * len(out_names)),
        scratch_shapes=[pltpu.VMEM(weights[n].shape, BF) for n in w_names] + [pltpu.SemaphoreType.DMA((len(w_names),))],
        compiler_params=pltpu.CompilerParams(vmem_limit_bytes=60 * 2**20),
    )(*inputs.values(), *[weights[n] for n in w_names])
    return dict(zip(out_names, out))


def shaped(shape, kind):
    return jax.ShapeDtypeStruct(shape, kind)


def front_outs(rows, width):
    return {"normed": shaped((rows, width), BF), "q": shaped((rows, H * HD), BF), "kv": shaped((rows, 2 * KVH * HD), BF)}


def forward_stage(state, q, kvw, mask, live, tables, gains, weights, last):
    rows, width = state.shape
    ff = weights["wg"].shape[1]
    outs = {
        "mixed": shaped((rows, H * HD), BF), "lse": shaped((8, (H // KVH) * rows), F32), "middle": shaped((rows, width), F32),
        "normed_two": shaped((rows, width), BF), "gate": shaped((rows, ff), F32), "up": shaped((rows, ff), F32),
        "hidden": shaped((rows, ff), BF), "branch": shaped((rows, width), F32), "next": shaped((rows, width), F32),
    }
    if not last:
        outs |= front_outs(rows, width)

    def parts(r, wait):
        state_next = rest_part(r, wait)
        r["next"][...] = state_next
        if not last:
            front_part(r, wait, state_next)

    needed = ("wo", "wg", "wu", "wd") + (() if last else ("wk", "wv", "wq"))
    ins = {"state": state, "q_in": q, "kvw": kvw, "mask": mask, "live": live, "cos": tables[0], "sin": tables[1], "gains": gains}
    return stage("forward", parts, needed, ins, outs, weights)


def first_stage(hidden_in, tables, gains, weights):
    rows, width = hidden_in.shape

    def parts(r, wait):
        state = r["hidden"][...].astype(F32)
        r["state"][...] = state
        front_part(r, wait, state)

    outs = front_outs(rows, width) | {"state": shaped((rows, width), F32)}
    return stage("first", parts, ("wk", "wv", "wq"), {"hidden": hidden_in, "cos": tables[0], "sin": tables[1], "gains": gains}, outs, weights)


def backward_stage(kept, before, mask, live, tables, gains, acc, weights, cotangent):
    ins = {"cos": tables[0], "sin": tables[1], "gains": gains, "acc": acc}
    outs = {"acc_out": shaped(acc.shape, F32)}
    needed = ()
    rows, width = (kept or before)["state"].shape
    ff = weights["wg"].shape[1]
    kvr = 2 * KVH * HD
    if before is not None:
        ins |= {"home": before["home"], "h_dq": before["d_q"], "h_state": before["state"], "h_d_state": before["d_state"]}
        outs |= {"d_k": shaped((rows, kvr // 2), BF), "d_v": shaped((rows, kvr // 2), BF)}
        needed += ("wq", "wk", "wv")
    else:
        ins |= {"cot": cotangent}
    if kept is not None:
        ins |= {"b_state": kept["state"], "b_live": live, "b_branch": kept["branch"], "b_gate": kept["gate"], "b_up": kept["up"],
                "b_middle": kept["middle"], "b_lse": kept["lse"], "kvw": kept["kvw"], "q_in": kept["q"], "mask": mask}
        outs |= {"d_mlp": shaped((rows, width), BF), "d_up": shaped((rows, ff), BF), "d_gate": shaped((rows, ff), BF),
                 "d_attn": shaped((rows, width), BF), "d_state": shaped((rows, width), F32), "d_q": shaped((rows, H * HD), BF),
                 "dkv": shaped(kept["kvw"].shape, BF)}
        needed += ("wd", "wg", "wu", "wo")
    else:
        outs |= {"grad": shaped((rows, width), F32)}

    def parts(r, wait):
        r["acc_out"][...] = r["acc"][...]
        grad = home_part(r, wait) if before is not None else r["cot"][...].astype(F32)
        if kept is not None:
            back_part(r, wait, grad)
        else:
            r["grad"][...] = grad

    return stage("backward", parts, needed, ins, outs, weights)


def keys_kernel(chips, back, kv_ref, w_ref, s_right, r_left, s_core, r_core):
    g, t = lax.axis_index("grp"), lax.axis_index("tok")
    z, c = t // 2, lax.rem(t, 2)
    rows = kv_ref.shape[0]
    partner, right = (g, z * 2 + 1 - c), (g, t + 2)

    def slot(d, core):
        return w_ref.at[pl.ds(pl.multiple_of(((back - d) * 2 + core) * rows, 128), rows)]

    bar = pltpu.get_barrier_semaphore()
    pl.semaphore_signal(bar, inc=1, device_id=partner, device_id_type=MESH)

    @pl.when(z > 0)
    def _():
        pl.semaphore_signal(bar, inc=1, device_id=(g, t - 2), device_id_type=MESH)

    def along(d, src):
        return copy_to(src, slot(d, c), s_right.at[d - 1], r_left.at[d - 1], right)

    def beside(d, src):
        return copy_to(src, slot(d, c), s_core.at[d], r_core.at[d], partner)

    own = w_ref.at[pl.ds(pl.multiple_of((back * 2 + c) * rows, 128), rows)]
    own[...] = kv_ref[...]
    for d in range(1, back + 1):
        @pl.when(z < d)
        def _():
            for core in (0, 1):
                slot(d, core)[...] = jnp.zeros(kv_ref.shape, kv_ref.dtype)

    pl.semaphore_wait(bar, 1 + (z < chips - 1).astype(jnp.int32))

    @pl.when(z < chips - 1)
    def _():
        along(1, kv_ref).start()

    beside(0, kv_ref).start()
    for d in range(1, back + 1):
        @pl.when(z >= d)
        def _():
            along(d, slot(d, c)).wait_recv()
            if d < back:
                @pl.when(z < chips - 1)
                def _():
                    along(d + 1, slot(d, c)).start()
            beside(d, slot(d, c)).start()

    def mine_to(d):
        return copy_to(slot(d, 1 - c), slot(d, 1 - c), s_core.at[d], r_core.at[d], partner)

    mine_to(0).wait_recv()
    beside(0, kv_ref).wait_send()

    @pl.when(z < chips - 1)
    def _():
        along(1, kv_ref).wait_send()

    for d in range(1, back + 1):
        @pl.when(z >= d)
        def _():
            mine_to(d).wait_recv()
            beside(d, slot(d, c)).wait_send()
            if d < back:
                @pl.when(z < chips - 1)
                def _():
                    along(d + 1, slot(d, c)).wait_send()


def exchange_keys(kv, n_tok, nback):
    back = nback // 2
    rows = kv.shape[0]
    dma = pltpu.SemaphoreType.DMA
    return pl.pallas_call(
        lambda *refs: keys_kernel(n_tok // 2, back, *refs),
        name="exchange_keys",
        out_shape=jax.ShapeDtypeStruct(((2 * back + 2) * rows, kv.shape[1]), kv.dtype),
        in_specs=[pl.BlockSpec(memory_space=pltpu.VMEM)],
        out_specs=pl.BlockSpec(memory_space=pltpu.VMEM),
        scratch_shapes=[dma((back,)), dma((back,)), dma((back + 1,)), dma((back + 1,))],
        compiler_params=pltpu.CompilerParams(collective_id=2, has_side_effects=True, vmem_limit_bytes=32 * 2**20),
    )(kv)


def home_kernel(chips, back, p_ref, h_ref, beside_in, sums, after_in, s_left, r_right, s_core, r_core):
    g, t = lax.axis_index("grp"), lax.axis_index("tok")
    z, c = t // 2, lax.rem(t, 2)
    rows = h_ref.shape[1]
    partner, left = (g, z * 2 + 1 - c), (g, t - 2)

    def block(d, core):
        return p_ref.at[pl.ds(pl.multiple_of(((back - d) * 2 + core) * rows, 128), rows)]

    bar = pltpu.get_barrier_semaphore()
    pl.semaphore_signal(bar, inc=1, device_id=partner, device_id_type=MESH)

    @pl.when(z < chips - 1)
    def _():
        pl.semaphore_signal(bar, inc=1, device_id=(g, t + 2), device_id_type=MESH)

    pl.semaphore_wait(bar, 1 + (z > 0).astype(jnp.int32))

    def beside(d):
        return copy_to(block(d, 1 - c), beside_in.at[d], s_core.at[d], r_core.at[d], partner)

    def along(d):
        return copy_to(sums.at[d - 1], after_in.at[d - 1], s_left.at[d - 1], r_right.at[d - 1], left)

    for d in range(back, 0, -1):
        @pl.when(z >= d)
        def _():
            beside(d).start()
    beside(0).start()
    for d in range(back, 0, -1):
        @pl.when(z >= d)
        def _():
            beside(d).wait_recv()
            sums[d - 1] = (block(d, c)[...].astype(F32) + beside_in[d].astype(F32)).astype(BF)
            if d < back:
                @pl.when(z < chips - 1)
                def _():
                    along(d + 1).wait_recv()
                    sums[d - 1] = (sums[d - 1].astype(F32) + after_in[d].astype(F32)).astype(BF)
            along(d).start()
    beside(0).wait_recv()
    h_ref[0] = block(0, c)[...].astype(F32) + beside_in[0].astype(F32)

    @pl.when(z < chips - 1)
    def _():
        along(1).wait_recv()
        h_ref[0] = h_ref[0] + after_in[0].astype(F32)

    beside(0).wait_send()
    for d in range(1, back + 1):
        @pl.when(z >= d)
        def _():
            beside(d).wait_send()
            along(d).wait_send()


def exchange_home(partial, n_tok, nback):
    back = nback // 2
    rows = partial.shape[0] // (2 * back + 2)
    width = partial.shape[1]
    dma = pltpu.SemaphoreType.DMA
    return pl.pallas_call(
        lambda *refs: home_kernel(n_tok // 2, back, *refs),
        name="exchange_home",
        out_shape=jax.ShapeDtypeStruct((1, rows, width), F32),
        in_specs=[pl.BlockSpec(memory_space=pltpu.VMEM)],
        out_specs=pl.BlockSpec(memory_space=pltpu.VMEM),
        scratch_shapes=[
            pltpu.VMEM((back + 1, rows, width), BF), pltpu.VMEM((back, rows, width), BF), pltpu.VMEM((back, rows, width), BF),
            dma((back,)), dma((back,)), dma((back + 1,)), dma((back + 1,)),
        ],
        compiler_params=pltpu.CompilerParams(collective_id=3, has_side_effects=True, vmem_limit_bytes=32 * 2**20),
    )(partial)


ROW_NAMES = ("normed_two", "d_mlp", "normed", "mixed", "d_gate", "d_up", "hidden", "d_q", "d_k", "d_v", "d_attn")


def grads_kernel(count, *refs):
    n = len(ROW_NAMES)
    r = {name: refs[i * count : (i + 1) * count] for i, name in enumerate(ROW_NAMES)}
    g_ref, left_t, slots, sems = refs[n * count :]
    for i, name in enumerate(ROW_NAMES[:4]):
        left_t[i] = jnp.concatenate([each[...].astype(F32).T.astype(BF) for each in r[name]], axis=1)

    def rows_of(name, low, high):
        return jnp.concatenate([each[:, low:high] for each in r[name]], axis=0)

    def out_copy(p):
        return pltpu.make_async_copy(slots.at[p % 2], g_ref.at[p], sems.at[p % 2])

    width = left_t.shape[1]
    for p in range(PARTS):
        if p >= 2:
            out_copy(p - 2).wait()
        slot = slots.at[p % 2]
        if p < 12:
            name, left = (("d_gate", 0), ("d_up", 0), ("hidden", 1))[p // 4]
            low = (p % 4) * COLS
            slot[...] = dot_nn(left_t[left], rows_of(name, low, low + COLS)).astype(BF)
        elif p == 12:
            slot[...] = dot_nn(left_t[2], rows_of("d_q", 0, COLS)).astype(BF)
        elif p == 13:
            right = jnp.concatenate([rows_of("d_q", COLS, width), rows_of("d_k", 0, 2 * COLS - width)], axis=1)
            slot[...] = dot_nn(left_t[2], right).astype(BF)
        elif p == 14:
            slot[...] = dot_nn(left_t[3], rows_of("d_attn", 0, COLS)).astype(BF)
        else:
            one = dot_nn(left_t[3], rows_of("d_attn", COLS, width))
            two = dot_nn(left_t[2], rows_of("d_v", 0, 2 * COLS - width))
            slot[...] = jnp.concatenate([one, two], axis=1).astype(BF)
        out_copy(p).start()
    out_copy(PARTS - 2).wait()
    out_copy(PARTS - 1).wait()


def weight_gradients(rows):
    count = len(rows["d_q"])
    flat = [each for name in ROW_NAMES for each in rows[name]]
    tokens, width = rows["normed"][0].shape
    return pl.pallas_call(
        lambda *refs: grads_kernel(count, *refs),
        name="weight_gradients",
        out_shape=jax.ShapeDtypeStruct((PARTS, width, COLS), BF),
        in_specs=[pl.BlockSpec(memory_space=pltpu.VMEM)] * len(flat),
        out_specs=pl.BlockSpec(memory_space=pl.ANY),
        scratch_shapes=[pltpu.VMEM((4, width, count * tokens), BF), pltpu.VMEM((2, width, COLS), BF), pltpu.SemaphoreType.DMA((2,))],
        compiler_params=pltpu.CompilerParams(vmem_limit_bytes=60 * 2**20),
    )(*flat)


def spread_kernel(p_ref, gate, up, down, d_q, d_k, d_v, d_o, came, wide, turned, q_full, k_full, o_full, v_full, sem_in, sem_out, sem_full):
    width = q_full.shape[0]
    cut = 2 * COLS - width
    order = [12, 13, 14, 15] + list(range(12))

    def fetch(i):
        return pltpu.make_async_copy(p_ref.at[order[i]], came.at[i % 3], sem_in.at[i % 3])

    def put(i):
        p = order[i]
        if p >= 8:
            return pltpu.make_async_copy(turned.at[i % 2], down.at[pl.ds((p - 8) * COLS, COLS)], sem_out.at[i % 2])
        return pltpu.make_async_copy(wide.at[i % 2], (gate, up)[p // 4].at[:, pl.ds((p % 4) * COLS, COLS)], sem_out.at[i % 2])

    fulls = [(q_full, d_q), (k_full, d_k), (o_full, d_o), (v_full, d_v)]

    def put_full(j):
        return pltpu.make_async_copy(fulls[j][0], fulls[j][1], sem_full.at[j])

    fetch(0).start()
    fetch(1).start()
    for i, p in enumerate(order):
        if i + 2 < len(order):
            fetch(i + 2).start()
        fetch(i).wait()
        part = came.at[i % 3]
        if i >= 6:
            put(i - 2).wait()
        if p >= 12:
            full, other = (q_full, k_full) if p < 14 else (o_full, v_full)
            if p % 2 == 0:
                full[:, :COLS] = part[...].astype(F32)
            else:
                got = part[...].astype(F32)
                full[:, COLS:] = got[:, : width - COLS]
                other[...] = got[:, width - COLS :]
                put_full(0 if p < 14 else 2).start()
                put_full(1 if p < 14 else 3).start()
        elif p >= 8:
            turned[i % 2] = part[...].astype(F32).T
            put(i).start()
        else:
            wide[i % 2] = part[...].astype(F32)
            put(i).start()
    put(len(order) - 2).wait()
    put(len(order) - 1).wait()
    for j in range(4):
        put_full(j).wait()


def spread_out(parts):
    n, width, cols = parts.shape
    kv = 2 * cols - width
    ff = 4 * cols
    shapes = [(width, ff), (width, ff), (ff, width), (width, width), (width, kv), (width, kv), (width, width)]
    vm = pltpu.VMEM
    return pl.pallas_call(
        spread_kernel,
        name="spread_out",
        out_shape=tuple(jax.ShapeDtypeStruct(s, F32) for s in shapes),
        in_specs=[pl.BlockSpec(memory_space=pl.ANY)],
        out_specs=tuple([pl.BlockSpec(memory_space=pl.ANY)] * 7),
        scratch_shapes=[
            vm((3, width, cols), BF), vm((2, width, cols), F32), vm((2, cols, width), F32),
            vm((width, width), F32), vm((width, kv), F32), vm((width, width), F32), vm((width, kv), F32),
            pltpu.SemaphoreType.DMA((3,)), pltpu.SemaphoreType.DMA((2,)), pltpu.SemaphoreType.DMA((4,)),
        ],
        compiler_params=pltpu.CompilerParams(vmem_limit_bytes=60 * 2**20),
    )(parts)


def on_device(
    hidden_in,
    cotangent,
    lengths,
    active,
    norm_attn,
    w_query,
    w_key,
    w_value,
    w_out,
    norm_mlp,
    w_gate,
    w_up,
    w_down,
    w_router,
):
    n_tok = lax.axis_size("tok")
    n_grp = lax.axis_size("grp")
    me_index = lax.axis_index("tok")
    rows, width = hidden_in.shape
    nback = min(SPAN, n_tok // 2)

    def gathered(shard):
        return lax.all_gather(shard, "tok", axis=0, tiled=True)

    matrices = (w_query, w_key, w_value, w_out, w_gate, w_up, w_down)
    weights = {name: gathered(shard) for name, shard in zip(WEIGHTS, matrices)}
    gains = jnp.stack([gathered(norm_attn), gathered(norm_mlp), gathered(w_router)]).astype(F32)
    gains = jnp.pad(gains, ((0, 5), (0, 0)))

    lengths_row = lengths[0]
    token = jnp.arange(rows, dtype=jnp.int32)
    global_rows = me_index * rows + token
    segment_rows = segment_of(lengths_row, global_rows)
    cosine, sine = rotary_tables(position_of(lengths_row, global_rows, segment_rows))
    tables = (jnp.concatenate([cosine] * 4, axis=1), jnp.concatenate([-sine, sine] * 2, axis=1))
    reach = (nback + 1) * rows
    global_keys = (me_index - nback) * rows + jnp.arange(reach, dtype=jnp.int32)
    live_all = lax.all_gather(active.astype(BF), "tok", axis=1, tiled=True)
    live_all = jnp.pad(live_all, ((0, 0), (nback * rows, 0)))
    live_keys = lax.dynamic_slice_in_dim(live_all, me_index * rows, reach, 1)
    reachable = (segment_rows[None, :] == segment_of(lengths_row, global_keys)[:, None]) & (
        global_keys[:, None] <= global_rows[None, :]
    )
    masks = jnp.where(reachable[None] & (live_keys[:, :, None] > 0), 1.0, 0.0).astype(F32)
    lives = [active[i].astype(F32)[:, None] for i in range(RECUR)]

    kept = []
    made = first_stage(hidden_in, tables, gains, weights)
    state = made["state"]
    for step in range(RECUR):
        kvw = exchange_keys(made["kv"], n_tok, nback)
        last = step == RECUR - 1
        done = forward_stage(state, made["q"], kvw, masks[step], lives[step], tables, gains, weights, last)
        kept.append({**done, "state": state, "q": made["q"], "kvw": kvw, "normed_r": made["normed"]})
        made, state = done, done["next"]

    acc = jnp.zeros((8, 1024), F32)
    before = None
    rows_of = {name: [] for name in ROW_NAMES}
    for step in reversed(range(RECUR)):
        back = backward_stage(kept[step], before, masks[step], lives[step], tables, gains, acc, weights, cotangent)
        acc = back["acc_out"]
        for name in ("d_k", "d_v"):
            if before is not None:
                rows_of[name].append(back[name])
        for name in ("d_mlp", "d_gate", "d_up", "d_q", "d_attn"):
            rows_of[name].append(back[name])
        for name in ("normed_two", "mixed", "hidden"):
            rows_of[name].append(kept[step][name])
        rows_of["normed"].append(kept[step]["normed_r"])
        before = {"home": exchange_home(back["dkv"], n_tok, nback), "d_q": back["d_q"], "state": kept[step]["state"], "d_state": back["d_state"]}
    back = backward_stage(None, before, None, None, tables, gains, acc, weights, None)
    for name in ("d_k", "d_v"):
        rows_of[name].append(back[name])
    acc = back["acc_out"]
    parts = weight_gradients(rows_of)
    if (n_grp, n_tok) == (4, 8):
        parts, acc = all_sum(parts, acc)
    else:
        parts = lax.psum(parts.astype(F32), ("grp", "tok")).astype(BF)
        acc = lax.psum(acc, ("grp", "tok"))
    d_gate, d_up, d_down, d_q, d_k, d_v, d_o = spread_out(parts)
    return (
        state.astype(BF),
        back["grad"],
        acc[0, :width],
        d_q,
        d_k,
        d_v,
        d_o,
        acc[1, :width],
        d_gate,
        d_up,
        d_down,
        acc[2, :width],
    )


def solution(mesh):
    placed = (
        P(("grp", "tok"), None),
        P(("grp", "tok"), None),
        P("grp", None),
        P(None, ("grp", "tok")),
        P("tok"),
        P("tok", None),
        P("tok", None),
        P("tok", None),
        P("tok", None),
        P("tok"),
        P("tok", None),
        P("tok", None),
        P("tok", None),
        P("tok"),
    )
    return jax.shard_map(
        on_device,
        mesh=mesh,
        in_specs=placed,
        out_specs=(
            P(("grp", "tok"), None),
            P(("grp", "tok"), None),
            P(),
            P(),
            P(),
            P(),
            P(),
            P(),
            P(),
            P(),
            P(),
            P(),
        ),
        check_vma=False,
    )
```

time: 1000 us -> 696 us (0.70)
  matrix products: 253 us -> 0 us
  Pallas kernels: 195 us -> 416 us
  starting transfers between devices: 135 us -> 0.19 us
  other arithmetic: 112 us -> 3.84 us
  local copies, waits for them, and re-layouts: 98.2 us -> 40.5 us
  waiting for transfers between devices: 126 us -> 151 us
  blocking collectives: 48.9 us -> 62.3 us
    dot_general x160 -> x0, matrix products: 253 us -> none  [the longest x21 48.2 us: matmul(): return jnp.dot(left, right, preferred_element_type=jnp.float32)]
    pallas_call x0 -> x16, Pallas kernels: none -> 225 us  [the longest x8 113 us: stage(): pl.pallas_call(body, name=name, out_shape=tuple(outputs.values()), in_spe...]
    ppermute x60 -> x0, starting transfers between devices: 135 us -> none  [from_behind(): return lax.ppermute(block, axis, route)]
    all_gather x5, waiting for transfers between devices: 92.9 us -> 148 us  [gathered(): return lax.all_gather(shard, 'tok', axis=0, tiled=True)]
    ppermute x60 -> x0, waiting for transfers between devices: 30.1 us -> none  [from_behind(): return lax.ppermute(block, axis, route)]
    and x30 -> x1, other arithmetic: 26.4 us -> 0.24 us  [on_device(): (segment_rows[None, :] == segment_of(lengths_row, global_keys)[:, None])...]
    convert_element_type x33 -> x4, other arithmetic: 27.2 us -> 1.09 us  [the longest x1 1.07 us: on_device(): state.astype(BF)]
    transpose x1 -> x0, local copies, waits for them, and re-layouts: 25.3 us -> none  [from_parts(): d_down = jnp.concatenate([wide[i].T for i in range(8, 12)], axis=0)]
  transfers between devices with their start and end apart: 65 -> 5, of which waited for: 13 -> 3; matrix products, arithmetic and copies ran while one was open for 7% -> 2% of each run, Pallas kernels for 0% -> 2%
where the time goes in v2:
time: 696 us; the launch traced here: 689 us
  Pallas kernels  416 us (60%)
  waiting for transfers between devices  151 us (22%)
  blocking collectives  62.3 us (9%)
  local copies, waits for them, and re-layouts  40.5 us (6%)
  between operations  15.1 us (2%)
    pallas_call x1, Pallas kernels, all_sum(): pl.pallas_call(reduce_kernel, name='all_sum', out_shape=(jax.ShapeDtypeSt...  191 us
    all_gather x5, waiting for transfers between devices, gathered(): return lax.all_gather(shard, 'tok', axis=0, tiled=True)  148 us
    pallas_call x8, Pallas kernels, stage(): pl.pallas_call(body, name=name, out_shape=tuple(outputs.values()), in_spe...  113 us
    pallas_call x3, Pallas kernels, exchange_home(): pl.pallas_call(lambda *refs: home_kernel(n_tok // 2, back, *refs), name='...  49 us
    all_gather x2, blocking collectives, gathered(): return lax.all_gather(shard, 'tok', axis=0, tiled=True)  33.4 us
    unnamed x60, local copies, waits for them, and re-layouts  32.9 us
    pallas_call x3, Pallas kernels, exchange_keys(): pl.pallas_call(lambda *refs: keys_kernel(n_tok // 2, back, *refs), name='...  21.9 us
    pallas_call x1, Pallas kernels, weight_gradients(): pl.pallas_call(lambda *refs: grads_kernel(count, *refs), name='weight_gra...  21.5 us
  transfers between devices with their start and end apart: 5, of which 3 were waited for; matrix products, arithmetic and copies ran while one was open for 2% of the time, Pallas kernels for 2%

profile of v2, /device:TPU:0, one launch (start us, length us, event | category | flops | bytes accessed | tf_op | source)
XLA Modules:
  0.0 689.3 jit_solution(14698382162025831846)
XLA Ops:
  12.7 18.8 %all-reduce.5 = (bf16[960]{0:T(1024)(128)(2,1)S(1)}, bf16[960]{0:T(1024)(128)(2,1)S(1)}, bf16[960]{0:T(1024)(128)(2,1)S(1)}) all-reduce(bf16[960]{0:T(1024)(128)(2,1)S(1)} %dynamic-update-slice.2, bf16[960]{0:T(1024)(128)(2,1)S(1)} %dynamic-update-slice.1, bf16[960]{0:T(1024)(128)(2,1)S(1)} %dynamic-update-slice), channel_id=1, replica_groups=mesh['grp'=4,'tok'=8] {'tok'}, use_global_device_ids=true, to_apply=%add.4 | all-reduce | flops 2880 | bytes 11520
  35.4 15.5 %all-gather = bf16[8,120,320]{1,2,0:T(8,128)(2,1)S(1)} all-gather(bf16[1,120,320]{1,2,0:T(8,128)(2,1)S(1)} %bitcast.39), channel_id=1, replica_groups=mesh['grp'=4,'tok'=8] {'tok'}, dimensions={0}, use_global_device_ids=true | all-gather | bytes 691200 | tf_op jit(solution)/shard_map/all_gather | solution.py:1101
  52.1 17.9 %all-gather.1 = bf16[8,120,320]{1,2,0:T(8,128)(2,1)S(1)} all-gather(bf16[1,120,320]{1,2,0:T(8,128)(2,1)S(1)} %bitcast.40), channel_id=1, replica_groups=mesh['grp'=4,'tok'=8] {'tok'}, dimensions={0}, use_global_device_ids=true | all-gather | bytes 691200 | tf_op jit(solution)/shard_map/all_gather | solution.py:1101
  71.2 10.0 %all_gather.39 = bf16[3,1024]{1,0:T(4,128)(2,1)S(1)} all-gather(bf16[3,128]{1,0:T(4,128)(2,1)S(1)} %convert_element_type.66), channel_id=1, replica_groups=mesh['grp'=4,'tok'=8] {'tok'}, dimensions={1}, use_global_device_ids=true | all-gather | bytes 6912 | tf_op jit(solution)/shard_map/all_gather | solution.py:1116
  85.0 5.0 first.1
  90.9 8.3 %exchange_keys.3.refs_2_.refs_15_ = bf16[768,640]{1,0:T(8,128)(2,1)S(1)} custom-call(bf16[128,640]{1,0:T(8,128)(2,1)S(1)} %copy-done.11), custom_call_target="tpu_custom_call" | custom-call | tf_op jit(solution)/shard_map/exchange_keys/pallas_call | solution.py:865
  100.2 31.6 %all-gather.12.cloned.1.call-done.refs_9_.refs_16_.refs_22_ = bf16[960,2560]{1,0:T(8,128)(2,1)} async-done(((bf16[120,2560]{1,0:T(8,128)(2,1)}), bf16[960,2560]{1,0:T(8,128)(2,1)}) %all-gather.12.cloned.1.call-update) | async-done | bytes 4915216 | tf_op jit(solution)/shard_map/all_gather | solution.py:1101
  131.8 60.3 %all-gather.14.cloned.1.call-done.refs_10_.refs_17_.refs_23_ = bf16[960,2560]{1,0:T(8,128)(2,1)} async-done(((bf16[120,2560]{1,0:T(8,128)(2,1)}), bf16[960,2560]{1,0:T(8,128)(2,1)}) %all-gather.14.cloned.1.call-update) | async-done | bytes 4915216 | tf_op jit(solution)/shard_map/all_gather | solution.py:1101
  192.1 56.4 %all-gather.16.cloned.1.call-done.refs_11_.refs_15_.refs_21_ = bf16[2560,960]{1,0:T(8,128)(2,1)} async-done(((bf16[320,960]{1,0:T(8,128)(2,1)}), bf16[2560,960]{1,0:T(8,128)(2,1)}) %all-gather.16.cloned.1.call-update) | async-done | bytes 4915216 | tf_op jit(solution)/shard_map/all_gather | solution.py:1101
  248.4 13.5 %forward.3 = (bf16[128,960]{1,0:T(8,128)(2,1)}, f32[8,384]{1,0:T(8,128)}, f32[128,960]{1,0:T(8,128)}, bf16[128,960]{1,0:T(8,128)(2,1)}, f32[128,2560]{1,0:T(8,12...) custom-call(f32[128,960]{1,0:T(8,128)} %get-tuple-element.90.refs_0_, ...), custom_call_target="tpu_custom_call" | custom-call | tf_op jit(solution)/shard_map/forward/pallas_call | solution.py:705
  262.9 4.5 exchange_keys.4.refs_2_.refs_15_
  268.4 13.5 %forward.4 = (bf16[128,960]{1,0:T(8,128)(2,1)}, f32[8,384]{1,0:T(8,128)}, f32[128,960]{1,0:T(8,128)}, bf16[128,960]{1,0:T(8,128)(2,1)}, f32[128,2560]{1,0:T(8,12...) custom-call(f32[128,960]{1,0:T(8,128)} %get-tuple-element.93.refs_0_, ...), custom_call_target="tpu_custom_call" | custom-call | tf_op jit(solution)/shard_map/forward/pallas_call | solution.py:705
  282.8 9.0 %exchange_keys.5.refs_2_.refs_12_ = bf16[768,640]{1,0:T(8,128)(2,1)S(1)} custom-call(bf16[128,640]{1,0:T(8,128)(2,1)S(1)} %copy-done.10), custom_call_target="tpu_custom_call" | custom-call | tf_op jit(solution)/shard_map/exchange_keys/pallas_call | solution.py:865
  292.9 12.0 %forward.5 = (bf16[128,960]{1,0:T(8,128)(2,1)}, f32[8,384]{1,0:T(8,128)}, f32[128,960]{1,0:T(8,128)}, bf16[128,960]{1,0:T(8,128)(2,1)}, f32[128,2560]{1,0:T(8,12...) custom-call(f32[128,960]{1,0:T(8,128)} %get-tuple-element.96.refs_0_.refs_5_.refs, ...), custom_call_target="tpu_custom_call" | custom-call | tf_op jit(solution)/shard_map/forward/pallas_call | solution.py:705
  307.4 20.1 %backward.4 = (f32[8,1024]{1,0:T(8,128)}, bf16[128,960]{1,0:T(8,128)(2,1)}, bf16[128,2560]{1,0:T(8,128)(2,1)}, bf16[128,2560]{1,0:T(8,128)(2,1)}, bf16[128,960]{...) custom-call(f32[128,128]{1,0:T(8,128)} %get-tuple-element.231.refs_1_.refs_5_.refs_0_, ...), custom_call_target="tpu_custom_call" | custom-call | tf_op jit(solution)/shard_map/backward/pallas_call | solution.py:705
  327.5 1.2 copy-done.8
  328.7 22.2 %exchange_home.3.refs_4_ = f32[1,128,640]{2,1,0:T(8,128)S(1)} custom-call(bf16[768,640]{1,0:T(8,128)(2,1)S(1)} %copy-done.8), custom_call_target="tpu_custom_call" | custom-call | tf_op jit(solution)/shard_map/exchange_home/pallas_call | solution.py:937
  351.7 21.4 %backward.5 = (f32[8,1024]{1,0:T(8,128)}, bf16[128,320]{1,0:T(8,128)(2,1)}, bf16[128,320]{1,0:T(8,128)(2,1)}, bf16[128,960]{1,0:T(8,128)(2,1)}, bf16[128,2560]{1...) custom-call(f32[128,128]{1,0:T(8,128)} %get-tuple-element.231.refs_1, ...), custom_call_target="tpu_custom_call" | custom-call | tf_op jit(solution)/shard_map/backward/pallas_call | solution.py:705
  373.0 1.2 copy-done.7
  374.2 14.1 %exchange_home.4.refs_4_ = f32[1,128,640]{2,1,0:T(8,128)S(1)} custom-call(bf16[768,640]{1,0:T(8,128)(2,1)S(1)} %copy-done.7), custom_call_target="tpu_custom_call" | custom-call | tf_op jit(solution)/shard_map/exchange_home/pallas_call | solution.py:937
  389.1 21.4 %backward.6 = (f32[8,1024]{1,0:T(8,128)}, bf16[128,320]{1,0:T(8,128)(2,1)}, bf16[128,320]{1,0:T(8,128)(2,1)}, bf16[128,960]{1,0:T(8,128)(2,1)}, bf16[128,2560]{1...) custom-call(f32[128,128]{1,0:T(8,128)} %get-tuple-element.231.refs_1, ...), custom_call_target="tpu_custom_call" | custom-call | tf_op jit(solution)/shard_map/backward/pallas_call | solution.py:705
  410.5 1.2 copy-done.6
  411.7 12.7 %exchange_home.5.refs_4_ = f32[1,128,640]{2,1,0:T(8,128)S(1)} custom-call(bf16[768,640]{1,0:T(8,128)(2,1)S(1)} %copy-done.6), custom_call_target="tpu_custom_call" | custom-call | tf_op jit(solution)/shard_map/exchange_home/pallas_call | solution.py:937
  425.1 5.7 backward.7
  430.8 2.0 copy.83
  432.8 21.5 %weight_gradients.1.g_ref = bf16[16,960,640]{2,1,0:T(8,128)(2,1)} custom-call(bf16[128,960]{1,0:T(8,128)(2,1)} %get-tuple-element.128.refs_0_, bf16[128,960]{1,0:T(8,128)(2,1)} %get-tuple-element.129.refs_1_, bf16[128,960]{1,0:T(8,128)(2,1)} %get-tuple-element.130.refs_2_, bf16[128,960]{1,0:T(8,128)(2,1)} %get-tuple-element.131.refs_3_, ...), custom_call_target="tpu_custom_call" | custom-call | tf_op jit(solution)/shard_map/weight_gradients/pallas_call | solution.py:996
  454.3 190.7 %all_sum.1 = (bf16[16,960,640]{2,1,0:T(8,128)(2,1)}, f32[8,1024]{1,0:T(8,128)}) custom-call(bf16[16,960,640]{2,1,0:T(8,128)(2,1)} %weight_gradients.1.g_ref, f32[8,1024]{1,0:T(8,128)} %get-tuple-element.158.v_ref), custom_call_target="tpu_custom_call" | custom-call | tf_op jit(solution)/shard_map/all_sum/pallas_call | solution.py:454
  645.0 1.5 fusion.9
  646.5 20.4 %spread_out.1 = (f32[960,2560]{1,0:T(8,128)}, f32[960,2560]{1,0:T(8,128)}, f32[2560,960]{1,0:T(8,128)}, f32[960,960]{1,0:T(8,128)}, f32[960,320]{1,0:T(8,128)}, /*index=5*/f32[960,320]{1,0:T(8,128)}, f32[960,960]{1,0:T(8,128)}) custom-call(bf16[16,960,640]{2,1,0:T(8,128)(2,1)} %get-tuple-element.160.p_ref), custom_call_target="tpu_custom_call" | custom-call | tf_op jit(solution)/shard_map/spread_out/pallas_call | solution.py:1063
  666.9 3.0 copy.84
  669.9 1.5 copy.85
  671.4 11.2 %copy.86 = f32[2560,960]{0,1:T(8,128)} copy(f32[2560,960]{1,0:T(8,128)} %get-tuple-element.214) | data formatting | bytes 19660800
  (93 shorter events, 24.9 us)
Async XLA Ops:
  7.2 3.5 copy-start.22
  7.2 3.5 copy-start.17
  7.2 4.7 copy-start.18
  7.2 5.0 copy-start.19
  7.2 5.2 copy-start.20
  7.2 26.5 %copy-start.13 = (bf16[128,960]{0,1:T(8,128)(2,1)S(1)}, bf16[128,960]{0,1:T(8,128)(2,1)}, u32[]{:S(2)}) copy-start(bf16[128,960]{0,1:T(8,128)(2,1)} %param.14) | copy-start | bytes 737284
  7.2 27.4 %copy-start.14 = (bf16[128,960]{0,1:T(8,128)(2,1)S(1)}, bf16[128,960]{0,1:T(8,128)(2,1)}, u32[]{:S(2)}) copy-start(bf16[128,960]{0,1:T(8,128)(2,1)} %param.15) | copy-start | bytes 737284
  7.3 28.2 %copy-start.15 = (bf16[120,320]{0,1:T(8,128)(2,1)S(1)}, bf16[120,320]{0,1:T(8,128)(2,1)}, u32[]{:S(2)}) copy-start(bf16[120,320]{0,1:T(8,128)(2,1)} %param.20) | copy-start | bytes 230404
  7.3 77.7 %all-gather.8.cloned.1.call-start = ((), (), s32[]{:S(2)}) async-start(), calls=%async_computation | async-start | bytes 2211840 | tf_op jit(solution)/shard_map/all_gather | solution.py:1101
  8.0 92.2 %all-gather.10.cloned.1.call-start = ((), (), s32[]{:S(2)}) async-start(), calls=%async_computation.1 | async-start | bytes 2211840 | tf_op jit(solution)/shard_map/all_gather | solution.py:1101
  8.7 123.1 %all-gather.12.cloned.1.call-start = ((), (), s32[]{:S(2)}) async-start(), calls=%async_computation.2 | async-start | bytes 5529600 | tf_op jit(solution)/shard_map/all_gather | solution.py:1101
  9.5 182.6 %all-gather.14.cloned.1.call-start = ((), (), s32[]{:S(2)}) async-start(), calls=%async_computation.3 | async-start | bytes 5529600 | tf_op jit(solution)/shard_map/all_gather | solution.py:1101
  10.1 42.1 %copy-start.16 = (bf16[120,320]{0,1:T(8,128)(2,1)S(1)}, bf16[120,320]{0,1:T(8,128)(2,1)}, u32[]{:S(2)}) copy-start(bf16[120,320]{0,1:T(8,128)(2,1)} %param.21) | copy-start | bytes 230404
  10.1 238.3 %all-gather.16.cloned.1.call-start = ((), (), s32[]{:S(2)}) async-start(), calls=%async_computation.4 | async-start | bytes 5898240 | tf_op jit(solution)/shard_map/all_gather | solution.py:1101
  35.4 45.8 %copy-start.21 = (s32[1,3]{1,0:T(1,128)S(1)}, s32[1,3]{1,0:T(1,128)}, u32[]{:S(2)}) copy-start(s32[1,3]{1,0:T(1,128)} %param.16) | copy-start | bytes 40
  90.0 0.9 copy-start.11
  99.3 0.9 copy-start
  262.0 0.9 copy-start.9
  267.4 1.0 copy-start.1
  281.9 0.9 copy-start.10
  291.9 1.0 copy-start.2
  327.5 1.2 copy-start.8
  350.9 0.7 copy-start.4
  373.0 1.2 copy-start.7
  388.3 0.7 copy-start.3
  410.4 1.2 copy-start.6
  424.4 0.7 copy-start.5
  666.9 3.0 copy-start.12
Sparse Core Ops, SparseCore 0:
  9.7 33.2 all-gather.7
  44.6 32.1 all-gather.9
  78.5 53.2 all-gather.11
  133.3 58.7 all-gather.13
  193.5 54.8 all-gather.15

commit v3 on v2

--- a/solution.py
+++ b/solution.py
@@ -475,7 +475,9 @@
 F32 = jnp.float32
 BF = jnp.bfloat16
 CHUNK = 512
-WEIGHTS = ("wq", "wk", "wv", "wo", "wg", "wu", "wd")
+WEIGHTS = ("wa", "wg", "wu", "wd")
+QK = (H + KVH) * HD
+QKO = QK + H * HD
 
 
 def dot_nn(left, right):
@@ -506,14 +508,10 @@
     gain = r["gains"][0:1, :]
     normed = (state * inverse_of(state) * gain).astype(BF)
     r["normed"][...] = normed
-    wait("wk")
-    keys = dot_nn(normed, r["wk_v"][...])
-    wait("wv")
-    values = dot_nn(normed, r["wv_v"][...])
-    wait("wq")
-    queries = dot_nn(normed, r["wq_v"][...])
-    turned = rope_lanes(jnp.concatenate([queries, keys], axis=1), r["cos"][...], r["sin"][...], 1.0).astype(BF)
-    qw = queries.shape[1]
+    wait("wa")
+    values = dot_nn(normed, r["wa_v"][:, QKO:])
+    turned = rope_lanes(dot_nn(normed, r["wa_v"][:, :QK]), r["cos"][...], r["sin"][...], 1.0).astype(BF)
+    qw = H * HD
     r["q"][...] = turned[:, :qw]
     r["kv"][...] = jnp.concatenate([turned[:, qw:], values.astype(BF)], axis=1)
 
@@ -555,8 +553,8 @@
     state = r["state"][...]
     mixed = attention_part(r)
     r["mixed"][...] = mixed
-    wait("wo")
-    attn_out = dot_nn(mixed, r["wo_v"][...])
+    wait("wa")
+    attn_out = dot_nn(mixed, r["wa_v"][:, QK:QKO])
     middle = state + attn_out
     r["middle"][...] = middle
     normed_two = (middle * inverse_of(middle) * r["gains"][1:2, :]).astype(BF)
@@ -621,8 +619,8 @@
     d_attn = (d_branch + d_middle).astype(BF)
     r["d_attn"][...] = d_attn
     r["d_state"][...] = grad_after + d_logit * router_vec + d_middle
-    wait("wo")
-    d_mixed = dot_nt(d_attn, r["wo_v"][...]).astype(BF)
+    wait("wa")
+    d_mixed = dot_nt(d_attn, r["wa_v"][:, QK:QKO]).astype(BF)
 
     per = H // KVH
     kv = window(r)
@@ -663,10 +661,9 @@
     d_values = total[:, half:].astype(BF)
     r["d_k"][...] = d_keys
     r["d_v"][...] = d_values
-    wait("wq")
-    wait("wk")
-    wait("wv")
-    d_normed = dot_nt(r["h_dq"][...], r["wq_v"][...]) + dot_nt(d_keys, r["wk_v"][...]) + dot_nt(d_values, r["wv_v"][...])
+    wait("wa")
+    both = jnp.concatenate([r["h_dq"][...], d_keys], axis=1)
+    d_normed = dot_nt(both, r["wa_v"][:, :QK]) + dot_nt(d_values, r["wa_v"][:, QKO:])
     state = r["h_state"][...]
     width = state.shape[1]
     d_in, d_gain = norm_back(d_normed, state, r["gains"][0:1, :])
@@ -728,32 +725,36 @@
     outs = {
         "mixed": shaped((rows, H * HD), BF), "lse": shaped((8, (H // KVH) * rows), F32), "middle": shaped((rows, width), F32),
         "normed_two": shaped((rows, width), BF), "gate": shaped((rows, ff), F32), "up": shaped((rows, ff), F32),
-        "hidden": shaped((rows, ff), BF), "branch": shaped((rows, width), F32), "next": shaped((rows, width), F32),
+        "hidden": shaped((rows, ff), BF), "branch": shaped((rows, width), F32),
     }
-    if not last:
-        outs |= front_outs(rows, width)
+    if last:
+        outs["output"] = shaped((width, rows), BF)
+    else:
+        outs |= front_outs(rows, width) | {"next": shaped((rows, width), F32)}
 
     def parts(r, wait):
         state_next = rest_part(r, wait)
-        r["next"][...] = state_next
-        if not last:
+        if last:
+            r["output"][...] = state_next.T.astype(BF)
+        else:
+            r["next"][...] = state_next
             front_part(r, wait, state_next)
 
-    needed = ("wo", "wg", "wu", "wd") + (() if last else ("wk", "wv", "wq"))
+    needed = ("wa", "wg", "wu", "wd")
     ins = {"state": state, "q_in": q, "kvw": kvw, "mask": mask, "live": live, "cos": tables[0], "sin": tables[1], "gains": gains}
     return stage("forward", parts, needed, ins, outs, weights)
 
 
 def first_stage(hidden_in, tables, gains, weights):
-    rows, width = hidden_in.shape
+    width, rows = hidden_in.shape
 
     def parts(r, wait):
-        state = r["hidden"][...].astype(F32)
+        state = r["hidden"][...].astype(F32).T
         r["state"][...] = state
         front_part(r, wait, state)
 
     outs = front_outs(rows, width) | {"state": shaped((rows, width), F32)}
-    return stage("first", parts, ("wk", "wv", "wq"), {"hidden": hidden_in, "cos": tables[0], "sin": tables[1], "gains": gains}, outs, weights)
+    return stage("first", parts, ("wa",), {"hidden": hidden_in, "cos": tables[0], "sin": tables[1], "gains": gains}, outs, weights)
 
 
 def backward_stage(kept, before, mask, live, tables, gains, acc, weights, cotangent):
@@ -766,7 +767,7 @@
     if before is not None:
         ins |= {"home": before["home"], "h_dq": before["d_q"], "h_state": before["state"], "h_d_state": before["d_state"]}
         outs |= {"d_k": shaped((rows, kvr // 2), BF), "d_v": shaped((rows, kvr // 2), BF)}
-        needed += ("wq", "wk", "wv")
+        needed += ("wa",)
     else:
         ins |= {"cot": cotangent}
     if kept is not None:
@@ -775,19 +776,221 @@
         outs |= {"d_mlp": shaped((rows, width), BF), "d_up": shaped((rows, ff), BF), "d_gate": shaped((rows, ff), BF),
                  "d_attn": shaped((rows, width), BF), "d_state": shaped((rows, width), F32), "d_q": shaped((rows, H * HD), BF),
                  "dkv": shaped(kept["kvw"].shape, BF)}
-        needed += ("wd", "wg", "wu", "wo")
+        needed += ("wd", "wg", "wu") + (("wa",) if before is None else ())
     else:
-        outs |= {"grad": shaped((rows, width), F32)}
+        outs |= {"grad": shaped((width, rows), F32)}
 
     def parts(r, wait):
         r["acc_out"][...] = r["acc"][...]
-        grad = home_part(r, wait) if before is not None else r["cot"][...].astype(F32)
+        grad = home_part(r, wait) if before is not None else r["cot"][...].astype(F32).T
         if kept is not None:
             back_part(r, wait, grad)
         else:
-            r["grad"][...] = grad
+            r["grad"][...] = grad.T
 
     return stage("backward", parts, needed, ins, outs, weights)
+
+
+QUARTERS = 4
+
+
+def gather_kernel(*refs):
+    ins, outs = refs[:5], refs[5:10]
+    zs, xs, ys, cs, got, cgot, own_s, own_c, own_r, ss, sr, sc, scr = refs[10:]
+    y, x, z, c = place()
+    partner, to_x, to_y = dev(y, x, z, 1 - c), dev(y, 1 - x, z, c), dev(1 - y, x, z, c)
+    left, right = dev(y, x, z - 1, c), dev(y, x, z + 1, c)
+    quarter = (x * 2 + y, (1 - x) * 2 + y, x * 2 + (1 - y), (1 - x) * 2 + (1 - y))
+    lasting = []
+
+    def go(cp, when=None):
+        if when is None:
+            cp.start()
+        else:
+            @pl.when(when)
+            def _():
+                cp.start()
+        lasting.append((cp, when))
+
+    def cut(ref, m, q):
+        if m < 3:
+            n = ref.shape[1] // QUARTERS
+            return ref.at[:, pl.ds(pl.multiple_of(q * n, 128), n)]
+        n = ref.shape[0] // QUARTERS
+        return ref.at[pl.ds(pl.multiple_of(q * n, 16), n), :]
+
+    def out_piece(m, kind, zz, core):
+        return cut(outs[m].at[zz * 2 + core], m, quarter[kind])
+
+    bar = pltpu.get_barrier_semaphore()
+    for d in (partner, to_x, to_y):
+        pl.semaphore_signal(bar, inc=1, device_id=d, device_id_type=MESH)
+
+    @pl.when(z > 0)
+    def _():
+        pl.semaphore_signal(bar, inc=1, device_id=left, device_id_type=MESH)
+
+    @pl.when(z < 3)
+    def _():
+        pl.semaphore_signal(bar, inc=1, device_id=right, device_id_type=MESH)
+
+    pl.semaphore_wait(bar, 3 + (z > 0).astype(jnp.int32) + (z < 3).astype(jnp.int32))
+
+    def small_copy(zz, core, src, device, sems):
+        return copy_to(src, outs[4].at[zz * 2 + core], sems[0], sems[1], device)
+
+    go(small_copy(z, c, ins[4], right, (ss.at[z, 0], sr.at[z])), z < 3)
+    go(small_copy(z, c, ins[4], left, (ss.at[z, 1], sr.at[z])), z > 0)
+    go(small_copy(z, c, ins[4], partner, (sc.at[z], scr.at[z])))
+    for m in range(4):
+        src, dst = cut(ins[m], m, quarter[0]), out_piece(m, 0, z, c)
+        go(copy_to(src, dst, zs.at[m, z, 0], got.at[0, m, z], right), z < 3)
+        go(copy_to(src, dst, zs.at[m, z, 1], got.at[0, m, z], left), z > 0)
+    for m in range(4):
+        go(copy_to(ins[m], outs[m].at[z * 2 + c], own_c.at[m], own_r.at[m], partner))
+    local = [pltpu.make_async_copy(ins[m], outs[m].at[z * 2 + c], own_s.at[m]) for m in range(5)]
+    for cp in local:
+        cp.start()
+
+    steps = [(t, side) for t in (1, 2, 3) for side in (0, 1)]
+
+    def source(t, side):
+        return (z - t, z >= t) if side == 0 else (z + t, z + t <= 3)
+
+    def wait_for(kind, m, zz):
+        piece = out_piece(m, kind, zz, c)
+        copy_to(piece, piece, cs.at[kind, m, zz], got.at[kind, m, zz], partner).wait_recv()
+        return piece
+
+    def each(kind, m, t, side):
+        zz, there = source(t, side)
+        onward = (z < 3) if side == 0 else (z > 0)
+
+        @pl.when(there)
+        def _():
+            piece = wait_for(kind, m, zz)
+            first_x = m % 2 == 0
+            sends = []
+            if kind == 0:
+                on = copy_to(piece, piece, zs.at[m, zz, side], got.at[0, m, zz], right if side == 0 else left)
+
+                @pl.when(onward)
+                def _():
+                    on.start()
+
+                sends.append(copy_to(piece, piece, xs.at[0, m, zz], got.at[1, m, zz], to_x))
+                sends.append(copy_to(piece, piece, ys.at[0, m, zz], got.at[2, m, zz], to_y))
+            elif kind == 1 and first_x:
+                sends.append(copy_to(piece, piece, ys.at[1, m, zz], got.at[3, m, zz], to_y))
+            elif kind == 2 and not first_x:
+                sends.append(copy_to(piece, piece, xs.at[1, m, zz], got.at[3, m, zz], to_x))
+            sends.append(copy_to(piece, piece, cs.at[kind, m, zz], cgot.at[kind, m, zz], partner))
+            for cp in sends:
+                cp.start()
+
+        lasting.append((("s", kind, m, t, side), there))
+        if kind == 0:
+            lasting.append((("z", m, t, side), there & onward))
+
+    def small_step(t, side):
+        zz, there = source(t, side)
+
+        @pl.when(there)
+        def _():
+            piece = outs[4].at[zz * 2 + c]
+            copy_to(piece, piece, sc.at[zz], sr.at[zz], partner).wait_recv()
+
+            @pl.when((z < 3) if side == 0 else (z > 0))
+            def _():
+                small_copy(zz, c, piece, right if side == 0 else left, (ss.at[zz, side], sr.at[zz])).start()
+
+            small_copy(zz, c, piece, partner, (sc.at[zz], scr.at[zz])).start()
+
+        lasting.append((("m", t, side), there))
+
+    for t, side in steps:
+        small_step(t, side)
+    for turn in range(4 + 2):
+        for t, side in steps:
+            if turn < 4:
+                each(0, turn, t, side)
+            if 1 <= turn < 5:
+                m = turn - 1
+                relay, leaf = (1, 2) if m % 2 == 0 else (2, 1)
+                each(relay, m, t, side)
+                each(leaf, m, t, side)
+            if turn >= 2:
+                each(3, turn - 2, t, side)
+
+    for cp, when in lasting:
+        if not isinstance(cp, tuple):
+            if when is None:
+                cp.wait_send()
+            else:
+                @pl.when(when)
+                def _():
+                    cp.wait_send()
+        elif cp[0] == "z":
+            _, m, t, side = cp
+            zz, _ = source(t, side)
+            piece = out_piece(m, 0, zz, c)
+
+            @pl.when(when)
+            def _():
+                copy_to(piece, piece, zs.at[m, zz, side], got.at[0, m, zz], partner).wait_send()
+        elif cp[0] == "m":
+            _, t, side = cp
+            zz, _ = source(t, side)
+            piece = outs[4].at[zz * 2 + c]
+
+            @pl.when(when)
+            def _():
+                @pl.when((z < 3) if side == 0 else (z > 0))
+                def _():
+                    small_copy(zz, c, piece, partner, (ss.at[zz, side], sr.at[zz])).wait_send()
+
+                small_copy(zz, c, piece, partner, (sc.at[zz], scr.at[zz])).wait_send()
+                other = outs[4].at[zz * 2 + 1 - c]
+                copy_to(other, other, sc.at[zz], scr.at[zz], partner).wait_recv()
+        else:
+            _, kind, m, t, side = cp
+            zz, _ = source(t, side)
+            piece = out_piece(m, kind, zz, c)
+            other = out_piece(m, kind, zz, 1 - c)
+            first_x = m % 2 == 0
+
+            @pl.when(when)
+            def _():
+                if kind == 0 or (kind == 2 and not first_x):
+                    copy_to(piece, piece, xs.at[min(kind, 1), m, zz], got.at[1, m, zz], partner).wait_send()
+                if kind == 0 or (kind == 1 and first_x):
+                    copy_to(piece, piece, ys.at[min(kind, 1), m, zz], got.at[1, m, zz], partner).wait_send()
+                copy_to(piece, piece, cs.at[kind, m, zz], cgot.at[kind, m, zz], partner).wait_send()
+                copy_to(other, other, cs.at[kind, m, zz], cgot.at[kind, m, zz], partner).wait_recv()
+
+    for m in range(4):
+        other = outs[m].at[z * 2 + 1 - c]
+        copy_to(other, other, own_c.at[m], own_r.at[m], partner).wait_recv()
+    other = outs[4].at[z * 2 + 1 - c]
+    copy_to(other, other, sc.at[z], scr.at[z], partner).wait_recv()
+    for cp in local:
+        cp.wait()
+
+
+def gather_rows(shards):
+    dma = pltpu.SemaphoreType.DMA
+    return pl.pallas_call(
+        gather_kernel,
+        name="gather_rows",
+        out_shape=tuple(jax.ShapeDtypeStruct((8, *s.shape), s.dtype) for s in shards),
+        in_specs=[pl.BlockSpec(memory_space=pl.ANY)] * 5,
+        out_specs=tuple([pl.BlockSpec(memory_space=pl.ANY)] * 5),
+        scratch_shapes=[
+            dma((4, 4, 2)), dma((2, 4, 4)), dma((2, 4, 4)), dma((4, 4, 4)), dma((4, 4, 4)), dma((4, 4, 4)),
+            dma((5,)), dma((4,)), dma((4,)), dma((4, 2)), dma((4,)), dma((4,)), dma((4,)),
+        ],
+        compiler_params=pltpu.CompilerParams(collective_id=4, has_side_effects=True),
+    )(*shards)
 
 
 def keys_kernel(chips, back, kv_ref, w_ref, s_right, r_left, s_core, r_core):
@@ -1004,9 +1207,8 @@
     )(*flat)
 
 
-def spread_kernel(p_ref, gate, up, down, d_q, d_k, d_v, d_o, came, wide, turned, q_full, k_full, o_full, v_full, sem_in, sem_out, sem_full):
+def spread_kernel(p_ref, gate, up, down, d_q, d_k, d_v, d_o, came, wide, q_full, k_full, o_full, v_full, sem_in, sem_out, sem_full):
     width = q_full.shape[0]
-    cut = 2 * COLS - width
     order = [12, 13, 14, 15] + list(range(12))
 
     def fetch(i):
@@ -1014,9 +1216,7 @@
 
     def put(i):
         p = order[i]
-        if p >= 8:
-            return pltpu.make_async_copy(turned.at[i % 2], down.at[pl.ds((p - 8) * COLS, COLS)], sem_out.at[i % 2])
-        return pltpu.make_async_copy(wide.at[i % 2], (gate, up)[p // 4].at[:, pl.ds((p % 4) * COLS, COLS)], sem_out.at[i % 2])
+        return pltpu.make_async_copy(wide.at[i % 2], (gate, up, down)[p // 4].at[:, pl.ds((p % 4) * COLS, COLS)], sem_out.at[i % 2])
 
     fulls = [(q_full, d_q), (k_full, d_k), (o_full, d_o), (v_full, d_v)]
 
@@ -1039,12 +1239,9 @@
             else:
                 got = part[...].astype(F32)
                 full[:, COLS:] = got[:, : width - COLS]
-                other[...] = got[:, width - COLS :]
+                other[...] = got[:, width - COLS :].T
                 put_full(0 if p < 14 else 2).start()
                 put_full(1 if p < 14 else 3).start()
-        elif p >= 8:
-            turned[i % 2] = part[...].astype(F32).T
-            put(i).start()
         else:
             wide[i % 2] = part[...].astype(F32)
             put(i).start()
@@ -1058,7 +1255,7 @@
     n, width, cols = parts.shape
     kv = 2 * cols - width
     ff = 4 * cols
-    shapes = [(width, ff), (width, ff), (ff, width), (width, width), (width, kv), (width, kv), (width, width)]
+    shapes = [(width, ff), (width, ff), (width, ff), (width, width), (kv, width), (kv, width), (width, width)]
     vm = pltpu.VMEM
     return pl.pallas_call(
         spread_kernel,
@@ -1067,8 +1264,8 @@
         in_specs=[pl.BlockSpec(memory_space=pl.ANY)],
         out_specs=tuple([pl.BlockSpec(memory_space=pl.ANY)] * 7),
         scratch_shapes=[
-            vm((3, width, cols), BF), vm((2, width, cols), F32), vm((2, cols, width), F32),
-            vm((width, width), F32), vm((width, kv), F32), vm((width, width), F32), vm((width, kv), F32),
+            vm((3, width, cols), BF), vm((2, width, cols), F32),
+            vm((width, width), F32), vm((kv, width), F32), vm((width, width), F32), vm((kv, width), F32),
             pltpu.SemaphoreType.DMA((3,)), pltpu.SemaphoreType.DMA((2,)), pltpu.SemaphoreType.DMA((4,)),
         ],
         compiler_params=pltpu.CompilerParams(vmem_limit_bytes=60 * 2**20),
@@ -1097,12 +1294,13 @@
     rows, width = hidden_in.shape
     nback = min(SPAN, n_tok // 2)
 
-    def gathered(shard):
-        return lax.all_gather(shard, "tok", axis=0, tiled=True)
-
-    matrices = (w_query, w_key, w_value, w_out, w_gate, w_up, w_down)
-    weights = {name: gathered(shard) for name, shard in zip(WEIGHTS, matrices)}
-    gains = jnp.stack([gathered(norm_attn), gathered(norm_mlp), gathered(w_router)]).astype(F32)
+    share = norm_attn.shape[0]
+    vectors = jnp.pad(jnp.stack([norm_attn, norm_mlp, w_router]), ((0, 0), (0, 128 - share)))
+    small = jnp.concatenate([vectors, active.astype(BF), jnp.zeros((10, 128), BF)], axis=0)
+    shards = (jnp.concatenate([w_query, w_key, w_out, w_value], axis=1), w_gate, w_up, w_down, small)
+    whole = gather_rows(shards) if (n_grp, n_tok) == (4, 8) else [lax.all_gather(each, "tok", axis=0) for each in shards]
+    weights = {name: each.reshape(-1, each.shape[-1]) for name, each in zip(WEIGHTS, whole)}
+    gains = jnp.transpose(whole[4][:, :3, :share], (1, 0, 2)).reshape(3, width).astype(F32)
     gains = jnp.pad(gains, ((0, 5), (0, 0)))
 
     lengths_row = lengths[0]
@@ -1113,7 +1311,7 @@
     tables = (jnp.concatenate([cosine] * 4, axis=1), jnp.concatenate([-sine, sine] * 2, axis=1))
     reach = (nback + 1) * rows
     global_keys = (me_index - nback) * rows + jnp.arange(reach, dtype=jnp.int32)
-    live_all = lax.all_gather(active.astype(BF), "tok", axis=1, tiled=True)
+    live_all = jnp.transpose(whole[4][:, 3:6], (1, 0, 2)).reshape(3, -1)
     live_all = jnp.pad(live_all, ((0, 0), (nback * rows, 0)))
     live_keys = lax.dynamic_slice_in_dim(live_all, me_index * rows, reach, 1)
     reachable = (segment_rows[None, :] == segment_of(lengths_row, global_keys)[:, None]) & (
@@ -1123,20 +1321,20 @@
     lives = [active[i].astype(F32)[:, None] for i in range(RECUR)]
 
     kept = []
-    made = first_stage(hidden_in, tables, gains, weights)
+    made = first_stage(hidden_in.T, tables, gains, weights)
     state = made["state"]
     for step in range(RECUR):
         kvw = exchange_keys(made["kv"], n_tok, nback)
         last = step == RECUR - 1
         done = forward_stage(state, made["q"], kvw, masks[step], lives[step], tables, gains, weights, last)
         kept.append({**done, "state": state, "q": made["q"], "kvw": kvw, "normed_r": made["normed"]})
-        made, state = done, done["next"]
+        made, state = done, done.get("next")
 
     acc = jnp.zeros((8, 1024), F32)
     before = None
     rows_of = {name: [] for name in ROW_NAMES}
     for step in reversed(range(RECUR)):
-        back = backward_stage(kept[step], before, masks[step], lives[step], tables, gains, acc, weights, cotangent)
+        back = backward_stage(kept[step], before, masks[step], lives[step], tables, gains, acc, weights, cotangent.T)
         acc = back["acc_out"]
         for name in ("d_k", "d_v"):
             if before is not None:
@@ -1159,17 +1357,17 @@
         acc = lax.psum(acc, ("grp", "tok"))
     d_gate, d_up, d_down, d_q, d_k, d_v, d_o = spread_out(parts)
     return (
-        state.astype(BF),
-        back["grad"],
+        kept[-1]["output"].T,
+        back["grad"].T,
         acc[0, :width],
         d_q,
-        d_k,
-        d_v,
+        d_k.T,
+        d_v.T,
         d_o,
         acc[1, :width],
         d_gate,
         d_up,
-        d_down,
+        d_down.T,
         acc[2, :width],
     )
 

time: 696 us -> 547 us (0.79)
  waiting for transfers between devices: 151 us -> 0 us
  Pallas kernels: 416 us -> 511 us
  blocking collectives: 62.3 us -> 0 us
  local copies, waits for them, and re-layouts: 40.5 us -> 22.2 us
  between operations: 15.1 us -> 1.41 us
    all_gather x5 -> x0, waiting for transfers between devices: 148 us -> none  [gathered(): return lax.all_gather(shard, 'tok', axis=0, tiled=True)]
    pallas_call x0 -> x1, Pallas kernels: none -> 90.8 us  [gather_rows(): pl.pallas_call(gather_kernel, name='gather_rows', out_shape=tuple((jax.Sh...]
    all_gather x3 -> x0, blocking collectives: 43.4 us -> none  [the longest x2 33.4 us: gathered(): return lax.all_gather(shard, 'tok', axis=0, tiled=True)]
    unnamed x60 -> x26, local copies, waits for them, and re-layouts: 32.9 us -> 13.3 us
    unnamed x1 -> x0, blocking collectives: 18.8 us -> none
  transfers between devices with their start and end apart: 5 -> 0, of which waited for: 3 -> 0; matrix products, arithmetic and copies ran while one was open for 2% -> 0% of each run, Pallas kernels for 2% -> 0%
where the time goes in v3:
time: 547 us; the launch traced here: 542 us
  Pallas kernels  511 us (93%)
  local copies, waits for them, and re-layouts  22.2 us (4%)
  other arithmetic  6.9 us (1%)
    pallas_call x1, Pallas kernels, all_sum(): pl.pallas_call(reduce_kernel, name='all_sum', out_shape=(jax.ShapeDtypeSt...  190 us
    pallas_call x8, Pallas kernels, stage(): pl.pallas_call(body, name=name, out_shape=tuple(outputs.values()), in_spe...  114 us
    pallas_call x1, Pallas kernels, gather_rows(): pl.pallas_call(gather_kernel, name='gather_rows', out_shape=tuple((jax.Sh...  90.8 us
    pallas_call x3, Pallas kernels, exchange_home(): pl.pallas_call(lambda *refs: home_kernel(n_tok // 2, back, *refs), name='...  48.4 us
    pallas_call x3, Pallas kernels, exchange_keys(): pl.pallas_call(lambda *refs: keys_kernel(n_tok // 2, back, *refs), name='...  25.5 us
    pallas_call x1, Pallas kernels, weight_gradients(): pl.pallas_call(lambda *refs: grads_kernel(count, *refs), name='weight_gra...  21.7 us
    pallas_call x1, Pallas kernels, spread_out(): pl.pallas_call(spread_kernel, name='spread_out', out_shape=tuple((jax.Sha...  19.9 us
    unnamed x26, local copies, waits for them, and re-layouts  13.3 us

profile of v3, /device:TPU:0, one launch (start us, length us, event | category | flops | bytes accessed | tf_op | source)
XLA Modules:
  0.0 541.6 jit_solution(13417078494718572014)
XLA Ops:
  7.7 1.0 copy.45
  8.8 1.0 copy.46
  10.9 2.0 concatenate.14.refs_0_
  12.9 90.8 %gather_rows.1 = (bf16[8,120,2560]{2,1,0:T(8,128)(2,1)}, bf16[8,120,2560]{2,1,0:T(8,128)(2,1)}, bf16[8,120,2560]{2,1,0:T(8,128)(2,1)}, bf16[8,320,960]{2,1,0:T(8,128)(2,1)}, bf16[8,16,128]{2,1,0:T(8,128)(2,1)}) custom-call(bf16[120,2560]{1,0:T(8,128)(2,1)} %concatenate.14.refs_0_, bf16[120,2560]{1,0:T(8,128)(2,1)} %refs_1_.1, bf16[120,2560]{1,0:T(8,128)(2,1)} %refs_2_.1, ...), custom_call_target="tpu_custom_call" | custom-call | tf_op jit(solution)/shard_map/gather_rows/pallas_call | solution.py:982
  106.2 1.0 slice_bitcast_fusion
  107.2 5.2 first.1
  112.4 0.9 copy-done.11
  113.3 5.0 exchange_keys.3.refs_2_.refs_15_
  118.2 0.9 copy-done
  119.2 13.1 %forward.3 = (bf16[128,960]{1,0:T(8,128)(2,1)}, f32[8,384]{1,0:T(8,128)}, f32[128,960]{1,0:T(8,128)}, bf16[128,960]{1,0:T(8,128)(2,1)}, f32[128,2560]{1,0:T(8,12...) custom-call(f32[128,960]{1,0:T(8,128)} %get-tuple-element.97.refs_0_, ...), custom_call_target="tpu_custom_call" | custom-call | tf_op jit(solution)/shard_map/forward/pallas_call | solution.py:702
  132.3 0.9 copy-done.9
  133.2 9.1 %exchange_keys.4.refs_2_.refs_15_ = bf16[768,640]{1,0:T(8,128)(2,1)S(1)} custom-call(bf16[128,640]{1,0:T(8,128)(2,1)S(1)} %copy-done.9), custom_call_target="tpu_custom_call" | custom-call | tf_op jit(solution)/shard_map/exchange_keys/pallas_call | solution.py:1068
  142.3 1.0 copy-done.1
  143.3 13.1 %forward.4 = (bf16[128,960]{1,0:T(8,128)(2,1)}, f32[8,384]{1,0:T(8,128)}, f32[128,960]{1,0:T(8,128)}, bf16[128,960]{1,0:T(8,128)(2,1)}, f32[128,2560]{1,0:T(8,12...) custom-call(f32[128,960]{1,0:T(8,128)} %get-tuple-element.103.refs_0, ...), custom_call_target="tpu_custom_call" | custom-call | tf_op jit(solution)/shard_map/forward/pallas_call | solution.py:702
  156.5 0.9 copy-done.10
  157.4 11.4 %exchange_keys.5.refs_2_.refs_12_ = bf16[768,640]{1,0:T(8,128)(2,1)S(1)} custom-call(bf16[128,640]{1,0:T(8,128)(2,1)S(1)} %copy-done.10), custom_call_target="tpu_custom_call" | custom-call | tf_op jit(solution)/shard_map/exchange_keys/pallas_call | solution.py:1068
  168.8 0.9 copy-done.2
  169.8 12.7 %forward.5 = (bf16[128,960]{1,0:T(8,128)(2,1)}, f32[8,384]{1,0:T(8,128)}, f32[128,960]{1,0:T(8,128)}, bf16[128,960]{1,0:T(8,128)(2,1)}, f32[128,2560]{1,0:T(8,12...) custom-call(f32[128,960]{1,0:T(8,128)} %get-tuple-element.106.refs_0_.refs_, ...), custom_call_target="tpu_custom_call" | custom-call | tf_op jit(solution)/shard_map/forward/pallas_call | solution.py:702
  183.0 20.3 %backward.4 = (f32[8,1024]{1,0:T(8,128)}, bf16[128,960]{1,0:T(8,128)(2,1)}, bf16[128,2560]{1,0:T(8,128)(2,1)}, bf16[128,2560]{1,0:T(8,128)(2,1)}, bf16[128,960]{...) custom-call(f32[128,128]{1,0:T(8,128)} %get-tuple-element.190.refs_1_.refs_5_.refs_0_, ...), custom_call_target="tpu_custom_call" | custom-call | tf_op jit(solution)/shard_map/backward/pallas_call | solution.py:702
  203.4 1.2 copy-done.8
  204.6 21.8 %exchange_home.3.refs_4_ = f32[1,128,640]{2,1,0:T(8,128)S(1)} custom-call(bf16[768,640]{1,0:T(8,128)(2,1)S(1)} %copy-done.8), custom_call_target="tpu_custom_call" | custom-call | tf_op jit(solution)/shard_map/exchange_home/pallas_call | solution.py:1140
  227.1 21.9 %backward.5 = (f32[8,1024]{1,0:T(8,128)}, bf16[128,320]{1,0:T(8,128)(2,1)}, bf16[128,320]{1,0:T(8,128)(2,1)}, bf16[128,960]{1,0:T(8,128)(2,1)}, bf16[128,2560]{1...) custom-call(f32[128,128]{1,0:T(8,128)} %get-tuple-element.190.refs_1, ...), custom_call_target="tpu_custom_call" | custom-call | tf_op jit(solution)/shard_map/backward/pallas_call | solution.py:702
  249.1 1.2 copy-done.7
  250.3 14.1 %exchange_home.4.refs_4_ = f32[1,128,640]{2,1,0:T(8,128)S(1)} custom-call(bf16[768,640]{1,0:T(8,128)(2,1)S(1)} %copy-done.7), custom_call_target="tpu_custom_call" | custom-call | tf_op jit(solution)/shard_map/exchange_home/pallas_call | solution.py:1140
  265.1 21.9 %backward.6 = (f32[8,1024]{1,0:T(8,128)}, bf16[128,320]{1,0:T(8,128)(2,1)}, bf16[128,320]{1,0:T(8,128)(2,1)}, bf16[128,960]{1,0:T(8,128)(2,1)}, bf16[128,2560]{1...) custom-call(f32[128,128]{1,0:T(8,128)} %get-tuple-element.190.refs_1, ...), custom_call_target="tpu_custom_call" | custom-call | tf_op jit(solution)/shard_map/backward/pallas_call | solution.py:702
  287.0 1.2 copy-done.6
  288.2 12.5 %exchange_home.5.refs_4_ = f32[1,128,640]{2,1,0:T(8,128)S(1)} custom-call(bf16[768,640]{1,0:T(8,128)(2,1)S(1)} %copy-done.6), custom_call_target="tpu_custom_call" | custom-call | tf_op jit(solution)/shard_map/exchange_home/pallas_call | solution.py:1140
  301.4 6.1 %backward.7 = (f32[8,1024]{1,0:T(8,128)}, bf16[128,320]{1,0:T(8,128)(2,1)}, bf16[128,320]{1,0:T(8,128)(2,1)}, f32[960,128]{1,0:T(8,128)}) custom-call(f32[128,128]{1,0:T(8,128)} %get-tuple-element.190.refs_1_.refs_5_.refs_0_, f32[128,128]{1,0:T(8,128)} %get-tuple-element.191.refs_2_.refs_6_.refs_1_, f32[8,960]{1,0:T(8,128)} %pad_convert_fusion.refs_3_.refs_7_.refs_2_, ...), custom_call_target="tpu_custom_call" | custom-call | tf_op jit(solution)/shard_map/backward/pallas_call | solution.py:702
  307.6 21.7 %weight_gradients.1.g_ref = bf16[16,960,640]{2,1,0:T(8,128)(2,1)} custom-call(bf16[128,960]{1,0:T(8,128)(2,1)} %get-tuple-element.138.refs_0_, bf16[128,960]{1,0:T(8,128)(2,1)} %get-tuple-element.139.refs_1_, bf16[128,960]{1,0:T(8,128)(2,1)} %get-tuple-element.140.refs_2_, bf16[128,960]{1,0:T(8,128)(2,1)} %get-tuple-element.141.refs_3_, ...), custom_call_target="tpu_custom_call" | custom-call | tf_op jit(solution)/shard_map/weight_gradients/pallas_call | solution.py:1199
  329.2 190.5 %all_sum.1 = (bf16[16,960,640]{2,1,0:T(8,128)(2,1)}, f32[8,1024]{1,0:T(8,128)}) custom-call(bf16[16,960,640]{2,1,0:T(8,128)(2,1)} %weight_gradients.1.g_ref, f32[8,1024]{1,0:T(8,128)} %get-tuple-element.168.v_ref), custom_call_target="tpu_custom_call" | custom-call | tf_op jit(solution)/shard_map/all_sum/pallas_call | solution.py:454
  519.7 1.5 fusion.8
  521.2 19.9 %spread_out.1 = (f32[960,2560]{1,0:T(8,128)}, f32[960,2560]{1,0:T(8,128)}, f32[960,2560]{1,0:T(8,128)}, f32[960,960]{1,0:T(8,128)}, f32[320,960]{1,0:T(8,128)}, /*index=5*/f32[320,960]{1,0:T(8,128)}, f32[960,960]{1,0:T(8,128)}) custom-call(bf16[16,960,640]{2,1,0:T(8,128)(2,1)} %get-tuple-element.170.p_ref), custom_call_target="tpu_custom_call" | custom-call | tf_op jit(solution)/shard_map/spread_out/pallas_call | solution.py:1260
  (44 shorter events, 13.5 us)
Async XLA Ops:
  112.3 0.9 copy-start.11
  118.2 0.9 copy-start
  132.3 0.9 copy-start.9
  142.3 1.0 copy-start.1
  156.4 0.9 copy-start.10
  168.8 0.9 copy-start.2
  203.3 1.2 copy-start.8
  226.4 0.7 copy-start.5
  249.1 1.2 copy-start.7
  264.3 0.7 copy-start.4
  287.0 1.2 copy-start.6
  300.7 0.7 copy-start.3

commit v4 on v3

--- a/solution.py
+++ b/solution.py
@@ -40,436 +40,6 @@
     inverse = jnp.power(theta, -jnp.arange(half_dim, dtype=jnp.float32) * (2.0 / HD))
     angle = positions.astype(jnp.float32)[..., None] * inverse
     return (jnp.cos(angle), jnp.sin(angle))
-
-
-PARTS = 16
-HALF = 480
-COLS = 640
-STREAMS = (("x", True, 0, 160), ("y", True, 160, 160), ("x", False, 320, 80), ("y", False, 400, 80))
-
-
-def place():
-    g, t = lax.axis_index("grp"), lax.axis_index("tok")
-    return g // 2, lax.rem(g, 2), t // 2, lax.rem(t, 2)
-
-
-def dev(y, x, z, c):
-    return (y * 2 + x, z * 2 + c)
-
-
-def pick(z, values):
-    out = jnp.int32(values[3])
-    for i in (2, 1, 0):
-        out = jnp.where(z == i, jnp.int32(values[i]), out)
-    return out
-
-
-def copy_to(src, dst, send, recv, device):
-    return pltpu.make_async_remote_copy(src_ref=src, dst_ref=dst, send_sem=send, recv_sem=recv, device_id=device, device_id_type=MESH)
-
-
-def add_rows(dst, src, rows, step):
-    def body(i, _):
-        at = pl.ds(pl.multiple_of(i * step, step), step)
-        dst[at, :] = dst[at, :] + src[at, :]
-        return 0
-    lax.fori_loop(0, rows // step, body, 0)
-
-
-def reduce_kernel(g_ref, v_ref, o_ref, vo_ref, mine, other, ra0, ra1, ra2, ra3, rz0, rz1, rz2, rz3, rb0, rb1, rb2, rb3,
-                  vrecv, load_sem, core_s, core_r, as_, ar, zs, zr, bs, br, ob, obr, oz, ozr, oa, oar, oc, ocr, vs, vr, own_sem):
-    y, x, z, c = place()
-    ra, rz, rb = (ra0, ra1, ra2, ra3), (rz0, rz1, rz2, rz3), (rb0, rb1, rb2, rb3)
-    partner = dev(y, x, z, 1 - c)
-    across = {"x": dev(y, 1 - x, z, c), "y": dev(1 - y, x, z, c)}
-    left, right = dev(y, x, z - 1, c), dev(y, x, z + 1, c)
-    at_axis = {"x": x, "y": y}
-    order = (pick(z, (3, 3, 0, 0)), pick(z, (2, 0, 3, 1)), pick(z, (1, 2, 1, 2)), z)
-
-    bar = pltpu.get_barrier_semaphore()
-    for d in (partner, across["x"], across["y"]):
-        pl.semaphore_signal(bar, inc=1, device_id=d, device_id_type=MESH)
-
-    @pl.when(z > 0)
-    def _():
-        pl.semaphore_signal(bar, inc=1, device_id=left, device_id_type=MESH)
-
-    @pl.when(z < 3)
-    def _():
-        pl.semaphore_signal(bar, inc=1, device_id=right, device_id_type=MESH)
-    far = dev(y, x, jnp.where(z < 2, z + 2, z - 2), c)
-    pl.semaphore_signal(bar, inc=1, device_id=far, device_id_type=MESH)
-    pl.semaphore_wait(bar, 4 + (z > 0).astype(jnp.int32) + (z < 3).astype(jnp.int32))
-
-    def part_xy(px, py, pz):
-        return (px * 2 + py) * 4 + pz
-
-    def part_of(s, pa, pb, pz):
-        return part_xy(pa, pb, pz) if STREAMS[s][0] == "x" else part_xy(pb, pa, pz)
-
-    def ab(s):
-        a = STREAMS[s][0]
-        b = "y" if a == "x" else "x"
-        return at_axis[a], at_axis[b], across[a], across[b]
-
-    def core_copy(p):
-        return copy_to(g_ref.at[p, pl.ds(pl.multiple_of((1 - c) * HALF, HALF), HALF)], other.at[p], core_s.at[p], core_r.at[p], partner)
-
-    def load(p):
-        return pltpu.make_async_copy(g_ref.at[p, pl.ds(pl.multiple_of(c * HALF, HALF), HALF)], mine.at[p], load_sem.at[p])
-
-    waits = []
-    seq = [(k, px, py) for k in range(4) for px, py in ((1 - x, 1 - y), (1 - x, y), (x, 1 - y), (x, y))]
-    for k, px, py in seq:
-        p = part_xy(px, py, order[k])
-        core_copy(p).start()
-        load(p).start()
-
-    def a_copy(s, pb, pz):
-        a, b, to_a, _ = ab(s)
-        _, _, r0, n = STREAMS[s]
-        return copy_to(mine.at[part_of(s, 1 - a, pb, pz), pl.ds(r0, n)], ra[s].at[pb * 4 + pz], as_.at[s, pb * 4 + pz], ar.at[s, pb * 4 + pz], to_a)
-
-    def core_step(k):
-        for i, (px, py) in enumerate(((1 - x, 1 - y), (1 - x, y), (x, 1 - y), (x, y))):
-            p = part_xy(px, py, order[k])
-            load(p).wait()
-            core_copy(p).wait_recv()
-            add_rows(mine.at[p], other.at[p], HALF, 16)
-            for s in range(4):
-                a_axis = STREAMS[s][0]
-                if i == 0 or (i == 1 and a_axis == "x") or (i == 2 and a_axis == "y"):
-                    pb = py if a_axis == "x" else px
-                    cp = a_copy(s, pb, order[k])
-                    cp.start()
-                    waits.append(cp)
-
-    def z_copy(s, pb, pz, to_right):
-        a, b, _, _ = ab(s)
-        _, _, r0, n = STREAMS[s]
-        src = mine.at[part_of(s, a, pb, pz), pl.ds(r0, n)]
-        slot = pz if to_right else jnp.where(pz == z - 1, 4, pz)
-        i = pb * 5 + slot
-        return copy_to(src, rz[s].at[i], zs.at[s, i], zr.at[s, i], right if to_right else left)
-
-    def z_wait(s, pb, slot):
-        _, _, r0, n = STREAMS[s]
-        i = pb * 5 + slot
-        copy_to(mine.at[0, pl.ds(r0, n)], rz[s].at[i], zs.at[s, i], zr.at[s, i], left).wait_recv()
-
-    def z_step(s, pb, k):
-        a, b, _, _ = ab(s)
-        _, _, r0, n = STREAMS[s]
-        pz = order[k]
-        acc = mine.at[part_of(s, a, pb, pz), pl.ds(r0, n)]
-        if k < 3:
-            up = jnp.where(pz > z, (z > 0).astype(jnp.int32), (z < 3).astype(jnp.int32))
-
-            @pl.when(up == 1)
-            def _():
-                z_wait(s, pb, pz)
-                add_rows(acc, rz[s].at[pb * 5 + pz], n, 16)
-
-            @pl.when(pz > z)
-            def _():
-                z_copy(s, pb, pz, True).start()
-
-            @pl.when(pz < z)
-            def _():
-                z_copy(s, pb, pz, False).start()
-        else:
-            @pl.when(z > 0)
-            def _():
-                z_wait(s, pb, z)
-                add_rows(acc, rz[s].at[pb * 5 + z], n, 16)
-
-            @pl.when(z < 3)
-            def _():
-                z_wait(s, pb, 4)
-                add_rows(acc, rz[s].at[pb * 5 + 4], n, 16)
-
-    def z_drain(s, pb, k):
-        pz = order[k]
-
-        @pl.when(pz > z)
-        def _():
-            z_copy(s, pb, pz, True).wait_send()
-
-        @pl.when(pz < z)
-        def _():
-            z_copy(s, pb, pz, False).wait_send()
-
-    def a_step(s, pb, k):
-        a, b, to_a, _ = ab(s)
-        _, _, r0, n = STREAMS[s]
-        pz = order[k]
-        a_copy(s, pb, pz).wait_recv()
-        add_rows(mine.at[part_of(s, a, pb, pz), pl.ds(r0, n)], ra[s].at[pb * 4 + pz], n, 16)
-
-    def b_copy(s, pz):
-        a, b, _, to_b = ab(s)
-        _, second_z, r0, n = STREAMS[s]
-        i = 0 if second_z else pz
-        return copy_to(mine.at[part_of(s, a, 1 - b, pz), pl.ds(r0, n)], rb[s].at[i], bs.at[s, i], br.at[s, i], to_b)
-
-    def b_step(s, pz):
-        a, b, _, _ = ab(s)
-        _, second_z, r0, n = STREAMS[s]
-        i = 0 if second_z else pz
-        b_copy(s, pz).wait_recv()
-        add_rows(mine.at[part_of(s, a, b, pz), pl.ds(r0, n)], rb[s].at[i], n, 16)
-
-    def stream_step(k):
-        for s in range(4):
-            _, b, _, _ = ab(s)
-            if STREAMS[s][1]:
-                a_step(s, 1 - b, k)
-                z_step(s, 1 - b, k)
-                a_step(s, b, k)
-                z_step(s, b, k)
-                if k == 3:
-                    cp = b_copy(s, z)
-                    cp.start()
-                    waits.append(cp)
-            else:
-                a_step(s, 1 - b, k)
-                cp = b_copy(s, order[k])
-                cp.start()
-                waits.append(cp)
-                a_step(s, b, k)
-
-    def stream_step2(k):
-        for s in range(4):
-            _, b, _, _ = ab(s)
-            if not STREAMS[s][1]:
-                b_step(s, order[k])
-                z_step(s, b, k)
-            elif k == 3:
-                b_step(s, z)
-
-    def vec_to(i):
-        return (partner, across["x"], across["y"], dev(y, x, jnp.where(lax.rem(z, 2) == 0, z + 1, z - 1), c), far)[i]
-
-    def vec_copy(i):
-        return copy_to(vo_ref, vrecv.at[i], vs.at[i], vr.at[i], vec_to(i))
-
-    def vec_start(i):
-        vec_copy(i).start()
-
-    def vec_end(i):
-        vec_copy(i).wait()
-        vo_ref[...] = vo_ref[...] + vrecv[i]
-
-    vo_ref[...] = v_ref[...]
-    vec_start(0)
-    core_step(0)
-    vec_end(0)
-    vec_start(1)
-    core_step(1)
-    vec_end(1)
-    vec_start(2)
-    stream_step(0)
-    vec_end(2)
-    vec_start(3)
-    core_step(2)
-    stream_step2(0)
-    vec_end(3)
-    vec_start(4)
-    stream_step(1)
-    core_step(3)
-    stream_step2(1)
-    vec_end(4)
-    stream_step(2)
-    stream_step2(2)
-    stream_step(3)
-
-    half0 = c * HALF
-
-    def out_at(s, p):
-        _, _, r0, n = STREAMS[s]
-        return o_ref.at[p, pl.ds(pl.multiple_of(half0 + r0, 16), n)]
-
-    def mine_at(s, p):
-        _, _, r0, n = STREAMS[s]
-        return mine.at[p, pl.ds(r0, n)]
-
-    def go(cp):
-        cp.start()
-        waits.append(cp)
-
-    def to_core(s, p, src):
-        return copy_to(src, out_at(s, p), oc.at[s, p], ocr.at[s, p], partner)
-
-    def to_a(s, pb, pz, src):
-        a, b, na, _ = ab(s)
-        return copy_to(src, out_at(s, part_of(s, a, pb, pz)), oa.at[s, pb * 4 + pz], oar.at[s, pb * 4 + pz], na)
-
-    def to_b(s, pz, src):
-        a, b, _, nb = ab(s)
-        return copy_to(src, out_at(s, part_of(s, a, b, pz)), ob.at[s, pz], obr.at[s, pz], nb)
-
-    def to_z(s, pb, pz, src, to_right):
-        a, b, _, _ = ab(s)
-        i = pb * 8 + pz * 2 + (0 if to_right else 1)
-        return copy_to(src, out_at(s, part_of(s, a, pb, pz)), oz.at[s, i], ozr.at[s, pb * 4 + pz], right if to_right else left)
-
-    def spread_z(s, pb, pz, src, from_left=None):
-        if from_left is None:
-            @pl.when(z < 3)
-            def _():
-                to_z(s, pb, pz, src, True).start()
-
-            @pl.when(z > 0)
-            def _():
-                to_z(s, pb, pz, src, False).start()
-        elif from_left:
-            @pl.when(z < 3)
-            def _():
-                to_z(s, pb, pz, src, True).start()
-        else:
-            @pl.when(z > 0)
-            def _():
-                to_z(s, pb, pz, src, False).start()
-
-    for s in range(4):
-        a, b, _, _ = ab(s)
-        p = part_of(s, a, b, z)
-        if STREAMS[s][1]:
-            b_step(s, z)
-            src = mine_at(s, p)
-            go(to_b(s, z, src))
-            spread_z(s, b, z, src)
-            go(to_a(s, b, z, src))
-        else:
-            b_step(s, z)
-            z_step(s, b, 3)
-            src = mine_at(s, p)
-            spread_z(s, b, z, src)
-            go(to_b(s, z, src))
-            go(to_a(s, b, z, src))
-        go(to_core(s, p, src))
-        pltpu.make_async_copy(src, out_at(s, p), own_sem.at[s]).start()
-
-    def got_b(s, pz):
-        a, b, _, _ = ab(s)
-        p = part_of(s, a, 1 - b, pz)
-        src = out_at(s, p)
-        copy_to(src, src, ob.at[s, pz], obr.at[s, pz], partner).wait_recv()
-        if STREAMS[s][1]:
-            spread_z(s, 1 - b, pz, src)
-        to_a(s, 1 - b, pz, src).start()
-        to_core(s, p, src).start()
-
-    def got_z(s, pb, pz, from_left):
-        a, b, _, _ = ab(s)
-        p = part_of(s, a, pb, pz)
-        src = out_at(s, p)
-        copy_to(src, src, oz.at[s, 0], ozr.at[s, pb * 4 + pz], partner).wait_recv()
-        spread_z(s, pb, pz, src, from_left)
-        to_a(s, pb, pz, src).start()
-        to_core(s, p, src).start()
-        if not STREAMS[s][1]:
-            to_b(s, pz, src).start()
-
-    def got_a(s, pb, pz):
-        a, b, _, _ = ab(s)
-        p = part_of(s, 1 - a, pb, pz)
-        src = out_at(s, p)
-        copy_to(src, src, oa.at[s, pb * 4 + pz], oar.at[s, pb * 4 + pz], partner).wait_recv()
-        to_core(s, p, src).start()
-
-    for s in range(4):
-        got_b(s, z)
-    for s in range(4):
-        a, b, _, _ = ab(s)
-        got_a(s, b, z)
-        got_a(s, 1 - b, z)
-    for t in range(1, 4):
-        for lft in (True, False):
-            pz = z - t if lft else z + t
-            ok = (z >= t) if lft else (z + t <= 3)
-
-            @pl.when(ok)
-            def _():
-                for s in range(4):
-                    a, b, _, _ = ab(s)
-                    got_z(s, b, pz, lft)
-                    if STREAMS[s][1]:
-                        got_z(s, 1 - b, pz, lft)
-                for s in range(4):
-                    if not STREAMS[s][1]:
-                        got_b(s, pz)
-                for s in range(4):
-                    a, b, _, _ = ab(s)
-                    got_a(s, b, pz)
-                    got_a(s, 1 - b, pz)
-
-    for cp in waits:
-        cp.wait_send()
-    for k, px, py in seq:
-        core_copy(part_xy(px, py, order[k])).wait_send()
-    for s in range(4):
-        a, b, _, _ = ab(s)
-        pltpu.make_async_copy(mine_at(s, part_of(s, a, b, z)), out_at(s, part_of(s, a, b, z)), own_sem.at[s]).wait()
-        pbs = (b, 1 - b) if STREAMS[s][1] else (b,)
-        for pb in pbs:
-            for k in range(3):
-                z_drain(s, pb, k)
-        for pz in range(4):
-            for pb in pbs:
-                src = out_at(s, part_of(s, a, pb, pz))
-
-                @pl.when((z >= pz) & (z < 3))
-                def _():
-                    to_z(s, pb, pz, src, True).wait_send()
-
-                @pl.when((z <= pz) & (z > 0))
-                def _():
-                    to_z(s, pb, pz, src, False).wait_send()
-            for pb in (0, 1):
-                src = out_at(s, part_of(s, a, pb, pz))
-
-                @pl.when(((pb == b) & (pz == z)) == False)
-                def _():
-                    to_a(s, pb, pz, src).wait_send()
-            if not STREAMS[s][1]:
-                @pl.when(z != pz)
-                def _():
-                    to_b(s, pz, out_at(s, 0)).wait_send()
-        for p in range(16):
-            src = out_at(s, p)
-
-            @pl.when(p != part_of(s, a, b, z))
-            def _():
-                to_core(s, p, src).wait_send()
-            _, _, r0, n = STREAMS[s]
-            dst = o_ref.at[p, pl.ds(pl.multiple_of((1 - c) * HALF + r0, 16), n)]
-            copy_to(dst, dst, oc.at[s, p], ocr.at[s, p], partner).wait_recv()
-
-
-def all_sum(grads, vectors):
-    dma = pltpu.SemaphoreType.DMA
-    bf = jnp.bfloat16
-    rows = [s[3] for s in STREAMS]
-    return pl.pallas_call(
-        reduce_kernel,
-        name="all_sum",
-        out_shape=(jax.ShapeDtypeStruct(grads.shape, bf), jax.ShapeDtypeStruct(vectors.shape, jnp.float32)),
-        in_specs=[pl.BlockSpec(memory_space=pl.ANY), pl.BlockSpec(memory_space=pltpu.VMEM)],
-        out_specs=(pl.BlockSpec(memory_space=pl.ANY), pl.BlockSpec(memory_space=pltpu.VMEM)),
-        scratch_shapes=[
-            pltpu.VMEM((PARTS, HALF, COLS), bf), pltpu.VMEM((PARTS, HALF, COLS), bf),
-            *[pltpu.VMEM((8, n, COLS), bf) for n in rows],
-            *[pltpu.VMEM((10, n, COLS), bf) for n in rows],
-            *[pltpu.VMEM((1 if s[1] else 4, s[3], COLS), bf) for s in STREAMS],
-            pltpu.VMEM((5, *vectors.shape), jnp.float32),
-            dma((16,)), dma((16,)), dma((16,)),
-            dma((4, 8)), dma((4, 8)), dma((4, 10)), dma((4, 10)), dma((4, 4)), dma((4, 4)),
-            dma((4, 4)), dma((4, 4)), dma((4, 16)), dma((4, 8)), dma((4, 8)), dma((4, 8)), dma((4, 16)), dma((4, 16)),
-            dma((5,)), dma((5,)), dma((4,)),
-        ],
-        compiler_params=pltpu.CompilerParams(collective_id=1, has_side_effects=True, vmem_limit_bytes=56 * 2**20),
-    )(grads, vectors)
 
 
 F32 = jnp.float32
@@ -659,11 +229,10 @@
     padded = jnp.concatenate([total[:, :half], jnp.zeros((rows, half % (2 * HD)), F32)], axis=1)
     d_keys = rope_lanes(padded, r["cos"][...], r["sin"][...], -1.0)[:, :half].astype(BF)
     d_values = total[:, half:].astype(BF)
-    r["d_k"][...] = d_keys
-    r["d_v"][...] = d_values
     wait("wa")
-    both = jnp.concatenate([r["h_dq"][...], d_keys], axis=1)
-    d_normed = dot_nt(both, r["wa_v"][:, :QK]) + dot_nt(d_values, r["wa_v"][:, QKO:])
+    packed = jnp.concatenate([r["h_dq"][...], d_keys, r["h_d_attn"][...], d_values], axis=1)
+    r["d_packed"][...] = packed
+    d_normed = dot_nt(packed[:, :QK], r["wa_v"][:, :QK]) + dot_nt(d_values, r["wa_v"][:, QKO:])
     state = r["h_state"][...]
     width = state.shape[1]
     d_in, d_gain = norm_back(d_normed, state, r["gains"][0:1, :])
@@ -765,8 +334,8 @@
     ff = weights["wg"].shape[1]
     kvr = 2 * KVH * HD
     if before is not None:
-        ins |= {"home": before["home"], "h_dq": before["d_q"], "h_state": before["state"], "h_d_state": before["d_state"]}
-        outs |= {"d_k": shaped((rows, kvr // 2), BF), "d_v": shaped((rows, kvr // 2), BF)}
+        ins |= {"home": before["home"], "h_dq": before["d_q"], "h_state": before["state"], "h_d_state": before["d_state"], "h_d_attn": before["d_attn"]}
+        outs |= {"d_packed": shaped((rows, QKO + kvr // 2), BF)}
         needed += ("wa",)
     else:
         ins |= {"cot": cotangent}
@@ -789,6 +358,516 @@
             r["grad"][...] = grad.T
 
     return stage("backward", parts, needed, ins, outs, weights)
+
+
+PARTS = 16
+HALF = 480
+COLS = 640
+STREAMS = (
+    ("x", True, 0, 80, 0), ("y", True, 80, 80, 0), ("x", False, 160, 48, 0), ("y", False, 208, 32, 0),
+    ("x", True, 240, 80, 1), ("y", True, 320, 80, 1), ("x", False, 400, 32, 1), ("y", False, 432, 48, 1),
+)
+SLOTS = 4
+
+
+def place():
+    g, t = lax.axis_index("grp"), lax.axis_index("tok")
+    return g // 2, lax.rem(g, 2), t // 2, lax.rem(t, 2)
+
+
+def dev(y, x, z, c):
+    return (y * 2 + x, z * 2 + c)
+
+
+def pick(z, values):
+    out = jnp.int32(values[3])
+    for i in (2, 1, 0):
+        out = jnp.where(z == i, jnp.int32(values[i]), out)
+    return out
+
+
+def copy_to(src, dst, send, recv, device):
+    return pltpu.make_async_remote_copy(src_ref=src, dst_ref=dst, send_sem=send, recv_sem=recv, device_id=device, device_id_type=MESH)
+
+
+def add_rows(dst, src, rows, step):
+    def body(i, _):
+        at = pl.ds(pl.multiple_of(i * step, step), step)
+        dst[at, :] = dst[at, :] + src[at, :]
+        return 0
+
+    lax.fori_loop(0, rows // step, body, 0)
+
+
+def tail_kernel(count, *refs):
+    left_refs, refs = refs[: 4 * count], refs[4 * count :]
+    right_refs, refs = refs[: 4 * count], refs[4 * count :]
+    n_s = len(STREAMS)
+    v_ref, o_ref, vo_ref, left_t, right, theirs, mine, other = refs[:8]
+    ra, rz, rb = refs[8 : 8 + n_s], refs[8 + n_s : 8 + 2 * n_s], refs[8 + 2 * n_s : 8 + 3 * n_s]
+    vrecv, load_sem, core_s, core_r, as_, ar, zs, zr, bs, br, ob, obr, oz, ozr, oa, oar, oc, ocr, vs, vr, own_sem = refs[8 + 3 * n_s :]
+    y, x, z, c = place()
+    partner = dev(y, x, z, 1 - c)
+    across = {"x": dev(y, 1 - x, z, c), "y": dev(1 - y, x, z, c)}
+    left_dev, right_dev = dev(y, x, z - 1, c), dev(y, x, z + 1, c)
+    at_axis = {"x": x, "y": y}
+    order = (pick(z, (3, 3, 0, 0)), pick(z, (2, 0, 3, 1)), pick(z, (1, 2, 1, 2)), z)
+    far = dev(y, x, jnp.where(z < 2, z + 2, z - 2), c)
+    tokens = left_refs[0].shape[0]
+
+    loads = []
+    for p in range(PARTS):
+        for i in range(count):
+            src = right_refs[(p // 4) * count + i].at[:, pl.ds((p % 4) * COLS, COLS)]
+            loads.append(pltpu.make_async_copy(src, right.at[p, pl.ds(i * tokens, tokens)], load_sem.at[p * count + i]))
+    for cp in loads:
+        cp.start()
+
+    bar = pltpu.get_barrier_semaphore()
+    for d in (partner, across["x"], across["y"], far):
+        pl.semaphore_signal(bar, inc=1, device_id=d, device_id_type=MESH)
+
+    @pl.when(z > 0)
+    def _():
+        pl.semaphore_signal(bar, inc=1, device_id=left_dev, device_id_type=MESH)
+
+    @pl.when(z < 3)
+    def _():
+        pl.semaphore_signal(bar, inc=1, device_id=right_dev, device_id_type=MESH)
+
+    for j in range(4):
+        left_t[j] = jnp.concatenate([each[...].astype(F32).T.astype(BF) for each in left_refs[j * count : (j + 1) * count]], axis=1)
+    for cp in loads:
+        cp.wait()
+    pl.semaphore_wait(bar, 4 + (z > 0).astype(jnp.int32) + (z < 3).astype(jnp.int32))
+
+    def part_xy(px, py, pz):
+        return (px * 2 + py) * 4 + pz
+
+    def part_of(s, pa, pb, pz):
+        return part_xy(pa, pb, pz) if STREAMS[s][0] == "x" else part_xy(pb, pa, pz)
+
+    def ab(s):
+        a = STREAMS[s][0]
+        b = "y" if a == "x" else "x"
+        return at_axis[a], at_axis[b], across[a], across[b]
+
+    waits = []
+    seq = [(k, i, px, py) for k in range(4) for i, (px, py) in enumerate(((1 - x, 1 - y), (1 - x, y), (x, 1 - y), (x, y)))]
+
+    def core_copy(j):
+        k, _, px, py = seq[j]
+        p = part_xy(px, py, order[k])
+        return copy_to(theirs.at[j % SLOTS, pl.ds(pl.multiple_of((1 - c) * HALF, 16), HALF)], other.at[p], core_s.at[j], core_r.at[p], partner)
+
+    def core_make(j):
+        k, _, px, py = seq[j]
+        p = part_xy(px, py, order[k])
+        if j >= SLOTS:
+            core_copy(j - SLOTS).wait_send()
+        which = jnp.where(p < 8, 0, jnp.where(p < 12, 1, jnp.where(p < 14, 2, 3)))
+        split = 2 * COLS - 2 * HALF
+        theirs[j % SLOTS] = dot_nn(left_t[which], right[p]).astype(BF)
+
+        @pl.when(p == PARTS - 1)
+        def _():
+            theirs[j % SLOTS, :, COLS - split :] = dot_nn(left_t[2], right[p, :, COLS - split :]).astype(BF)
+
+        core_copy(j).start()
+
+    def core_add(j):
+        k, i, px, py = seq[j]
+        p = part_xy(px, py, order[k])
+        core_copy(j).wait_recv()
+        mine[p] = theirs[j % SLOTS, pl.ds(pl.multiple_of(c * HALF, 16), HALF), :] + other[p]
+
+    def a_copy(s, pb, pz):
+        a, b, to_a, _ = ab(s)
+        _, _, r0, n, _ = STREAMS[s]
+        return copy_to(mine.at[part_of(s, 1 - a, pb, pz), pl.ds(r0, n)], ra[s].at[pb * 4 + pz], as_.at[s, pb * 4 + pz], ar.at[s, pb * 4 + pz], to_a)
+
+    def a_send(j, batch):
+        k, i, px, py = seq[j]
+        for s in range(n_s):
+            a_axis = STREAMS[s][0]
+            if STREAMS[s][4] == batch and (i == 0 or (i == 1 and a_axis == "x") or (i == 2 and a_axis == "y")):
+                cp = a_copy(s, py if a_axis == "x" else px, order[k])
+                cp.start()
+                waits.append(cp)
+
+    def z_index(s, pb, slot):
+        return pb * 5 + slot if STREAMS[s][1] else slot
+
+    def z_copy(s, pb, pz, to_right):
+        a, b, _, _ = ab(s)
+        _, _, r0, n, _ = STREAMS[s]
+        src = mine.at[part_of(s, a, pb, pz), pl.ds(r0, n)]
+        i = z_index(s, pb, pz if to_right else jnp.where(pz == z - 1, 4, pz))
+        return copy_to(src, rz[s].at[i], zs.at[s, i], zr.at[s, i], right_dev if to_right else left_dev)
+
+    def z_take(s, pb, slot):
+        a, _, _, _ = ab(s)
+        _, _, r0, n, _ = STREAMS[s]
+        i = z_index(s, pb, slot)
+        copy_to(mine.at[0, pl.ds(r0, n)], rz[s].at[i], zs.at[s, i], zr.at[s, i], left_dev).wait_recv()
+        pz = z if slot is z or isinstance(slot, int) else slot
+        add_rows(mine.at[part_of(s, a, pb, pz), pl.ds(r0, n)], rz[s].at[i], n, 16)
+
+    def z_step(s, pb, k):
+        pz = order[k]
+        if k < 3:
+            up = jnp.where(pz > z, (z > 0).astype(jnp.int32), (z < 3).astype(jnp.int32))
+
+            @pl.when(up == 1)
+            def _():
+                z_take(s, pb, pz)
+
+            @pl.when(pz > z)
+            def _():
+                z_copy(s, pb, pz, True).start()
+
+            @pl.when(pz < z)
+            def _():
+                z_copy(s, pb, pz, False).start()
+        else:
+            @pl.when(z > 0)
+            def _():
+                z_take(s, pb, z)
+
+            @pl.when(z < 3)
+            def _():
+                z_take(s, pb, 4)
+
+    def z_drain(s, pb, k):
+        pz = order[k]
+
+        @pl.when(pz > z)
+        def _():
+            z_copy(s, pb, pz, True).wait_send()
+
+        @pl.when(pz < z)
+        def _():
+            z_copy(s, pb, pz, False).wait_send()
+
+    def a_step(s, pb, k):
+        a, b, to_a, _ = ab(s)
+        _, _, r0, n, _ = STREAMS[s]
+        pz = order[k]
+        a_copy(s, pb, pz).wait_recv()
+        add_rows(mine.at[part_of(s, a, pb, pz), pl.ds(r0, n)], ra[s].at[pb * 4 + pz], n, 16)
+
+    def b_copy(s, pz):
+        a, b, _, to_b = ab(s)
+        _, second_z, r0, n, _ = STREAMS[s]
+        i = 0 if second_z else pz
+        return copy_to(mine.at[part_of(s, a, 1 - b, pz), pl.ds(r0, n)], rb[s].at[i], bs.at[s, i], br.at[s, i], to_b)
+
+    def b_step(s, pz):
+        a, b, _, _ = ab(s)
+        _, second_z, r0, n, _ = STREAMS[s]
+        i = 0 if second_z else pz
+        b_copy(s, pz).wait_recv()
+        add_rows(mine.at[part_of(s, a, b, pz), pl.ds(r0, n)], rb[s].at[i], n, 16)
+
+    def of_batch(batch):
+        return [s for s in range(n_s) if STREAMS[s][4] == batch]
+
+    def first_step(batch, k):
+        for s in of_batch(batch):
+            _, b, _, _ = ab(s)
+            a_step(s, 1 - b, k)
+            if STREAMS[s][1]:
+                z_step(s, 1 - b, k)
+                a_step(s, b, k)
+                z_step(s, b, k)
+                if k == 3:
+                    cp = b_copy(s, z)
+                    cp.start()
+                    waits.append(cp)
+            else:
+                cp = b_copy(s, order[k])
+                cp.start()
+                waits.append(cp)
+                a_step(s, b, k)
+
+    def second_step(batch, k):
+        for s in of_batch(batch):
+            _, b, _, _ = ab(s)
+            if not STREAMS[s][1]:
+                b_step(s, order[k])
+                z_step(s, b, k)
+
+    def vec_copy(i):
+        to = (partner, across["x"], across["y"], dev(y, x, jnp.where(lax.rem(z, 2) == 0, z + 1, z - 1), c), far)[i]
+        return copy_to(vo_ref, vrecv.at[i], vs.at[i], vr.at[i], to)
+
+    def vec_end(i):
+        vec_copy(i).wait()
+        vo_ref[...] = vo_ref[...] + vrecv[i]
+
+    half0 = c * HALF
+
+    def out_at(s, p):
+        _, _, r0, n, _ = STREAMS[s]
+        return o_ref.at[p, pl.ds(pl.multiple_of(half0 + r0, 16), n)]
+
+    def mine_at(s, p):
+        _, _, r0, n, _ = STREAMS[s]
+        return mine.at[p, pl.ds(r0, n)]
+
+    def go(cp):
+        cp.start()
+        waits.append(cp)
+
+    def to_core(s, p, src):
+        return copy_to(src, out_at(s, p), oc.at[s, p], ocr.at[s, p], partner)
+
+    def to_a(s, pb, pz, src):
+        a, b, na, _ = ab(s)
+        return copy_to(src, out_at(s, part_of(s, a, pb, pz)), oa.at[s, pb * 4 + pz], oar.at[s, pb * 4 + pz], na)
+
+    def to_b(s, pz, src):
+        a, b, _, nb = ab(s)
+        return copy_to(src, out_at(s, part_of(s, a, b, pz)), ob.at[s, pz], obr.at[s, pz], nb)
+
+    def to_z(s, pb, pz, src, to_right):
+        a, b, _, _ = ab(s)
+        i = pb * 8 + pz * 2 + (0 if to_right else 1)
+        return copy_to(src, out_at(s, part_of(s, a, pb, pz)), oz.at[s, i], ozr.at[s, pb * 4 + pz], right_dev if to_right else left_dev)
+
+    def spread_z(s, pb, pz, src, sides):
+        if 0 in sides:
+            @pl.when(z < 3)
+            def _():
+                to_z(s, pb, pz, src, True).start()
+        if 1 in sides:
+            @pl.when(z > 0)
+            def _():
+                to_z(s, pb, pz, src, False).start()
+
+    def finish(batch):
+        for s in of_batch(batch):
+            a, b, _, _ = ab(s)
+            p = part_of(s, a, b, z)
+            b_step(s, z)
+            if not STREAMS[s][1]:
+                z_step(s, b, 3)
+            src = mine_at(s, p)
+            if STREAMS[s][1]:
+                go(to_b(s, z, src))
+                spread_z(s, b, z, src, (0, 1))
+            else:
+                spread_z(s, b, z, src, (0, 1))
+                go(to_b(s, z, src))
+            go(to_a(s, b, z, src))
+            go(to_core(s, p, src))
+            pltpu.make_async_copy(src, out_at(s, p), own_sem.at[s]).start()
+
+    def got_b(s, pz):
+        a, b, _, _ = ab(s)
+        p = part_of(s, a, 1 - b, pz)
+        src = out_at(s, p)
+        copy_to(src, src, ob.at[s, pz], obr.at[s, pz], partner).wait_recv()
+        if STREAMS[s][1]:
+            spread_z(s, 1 - b, pz, src, (0, 1))
+        to_a(s, 1 - b, pz, src).start()
+        to_core(s, p, src).start()
+
+    def got_z(s, pb, pz, from_left):
+        a, b, _, _ = ab(s)
+        p = part_of(s, a, pb, pz)
+        src = out_at(s, p)
+        copy_to(src, src, oz.at[s, 0], ozr.at[s, pb * 4 + pz], partner).wait_recv()
+        spread_z(s, pb, pz, src, (0,) if from_left else (1,))
+        to_a(s, pb, pz, src).start()
+        if not STREAMS[s][1]:
+            to_b(s, pz, src).start()
+        to_core(s, p, src).start()
+
+    def got_a(s, pb, pz):
+        a, b, _, _ = ab(s)
+        p = part_of(s, 1 - a, pb, pz)
+        src = out_at(s, p)
+        copy_to(src, src, oa.at[s, pb * 4 + pz], oar.at[s, pb * 4 + pz], partner).wait_recv()
+        to_core(s, p, src).start()
+
+    def gather_b(batch):
+        for s in of_batch(batch):
+            got_b(s, z)
+
+    def gather_a(batch):
+        for s in of_batch(batch):
+            _, b, _, _ = ab(s)
+            got_a(s, b, z)
+            got_a(s, 1 - b, z)
+
+    def from_side(t, side):
+        return (z - t, z >= t) if side == 0 else (z + t, z + t <= 3)
+
+    def gather_z(batch, t):
+        for side in (0, 1):
+            pz, there = from_side(t, side)
+
+            @pl.when(there)
+            def _():
+                for s in of_batch(batch):
+                    _, b, _, _ = ab(s)
+                    got_z(s, b, pz, side == 0)
+                    if STREAMS[s][1]:
+                        got_z(s, 1 - b, pz, side == 0)
+
+    def gather_rest(batch, t):
+        for side in (0, 1):
+            pz, there = from_side(t, side)
+
+            @pl.when(there)
+            def _():
+                for s in of_batch(batch):
+                    if not STREAMS[s][1]:
+                        got_b(s, pz)
+                for s in of_batch(batch):
+                    _, b, _, _ = ab(s)
+                    got_a(s, b, pz)
+                    got_a(s, 1 - b, pz)
+
+    vo_ref[...] = v_ref[...]
+    vec_copy(0).start()
+
+    def group(k, batches=(0,)):
+        for i in range(4):
+            j = k * 4 + i
+            core_make(j)
+            if j > 0:
+                core_add(j - 1)
+                a_send(j - 1, 0)
+        if k == 3:
+            core_add(15)
+            a_send(15, 0)
+
+    group(0)
+    vec_end(0)
+    vec_copy(1).start()
+    group(1)
+    vec_end(1)
+    vec_copy(2).start()
+    first_step(0, 0)
+    group(2)
+    vec_end(2)
+    vec_copy(3).start()
+    second_step(0, 0)
+    first_step(0, 1)
+    group(3)
+    vec_end(3)
+    vec_copy(4).start()
+    second_step(0, 1)
+    for j in range(0, 4):
+        a_send(j, 1)
+    first_step(0, 2)
+    vec_end(4)
+    second_step(0, 2)
+    for j in range(4, 8):
+        a_send(j, 1)
+    first_step(0, 3)
+    first_step(1, 0)
+    finish(0)
+    for j in range(8, 12):
+        a_send(j, 1)
+    second_step(1, 0)
+    gather_b(0)
+    first_step(1, 1)
+    second_step(1, 1)
+    gather_z(0, 1)
+    for j in range(12, 16):
+        a_send(j, 1)
+    gather_a(0)
+    first_step(1, 2)
+    second_step(1, 2)
+    gather_z(0, 2)
+    gather_rest(0, 1)
+    first_step(1, 3)
+    finish(1)
+    gather_z(0, 3)
+    gather_rest(0, 2)
+    gather_b(1)
+    gather_z(1, 1)
+    gather_rest(0, 3)
+    gather_a(1)
+    gather_z(1, 2)
+    gather_rest(1, 1)
+    gather_z(1, 3)
+    gather_rest(1, 2)
+    gather_rest(1, 3)
+
+    for cp in waits:
+        cp.wait_send()
+    for j in range(PARTS - SLOTS, PARTS):
+        core_copy(j).wait_send()
+    for s in range(n_s):
+        a, b, _, _ = ab(s)
+        pltpu.make_async_copy(mine_at(s, part_of(s, a, b, z)), out_at(s, part_of(s, a, b, z)), own_sem.at[s]).wait()
+        pbs = (b, 1 - b) if STREAMS[s][1] else (b,)
+        for pb in pbs:
+            for k in range(3):
+                z_drain(s, pb, k)
+        for pz in range(4):
+            for pb in pbs:
+                src = out_at(s, part_of(s, a, pb, pz))
+
+                @pl.when((z >= pz) & (z < 3))
+                def _():
+                    to_z(s, pb, pz, src, True).wait_send()
+
+                @pl.when((z <= pz) & (z > 0))
+                def _():
+                    to_z(s, pb, pz, src, False).wait_send()
+            for pb in (0, 1):
+                src = out_at(s, part_of(s, a, pb, pz))
+
+                @pl.when(jnp.logical_not((pb == b) & (pz == z)))
+                def _():
+                    to_a(s, pb, pz, src).wait_send()
+            if not STREAMS[s][1]:
+                @pl.when(z != pz)
+                def _():
+                    to_b(s, pz, out_at(s, 0)).wait_send()
+        for p in range(16):
+            src = out_at(s, p)
+
+            @pl.when(p != part_of(s, a, b, z))
+            def _():
+                to_core(s, p, src).wait_send()
+            _, _, r0, n, _ = STREAMS[s]
+            dst = o_ref.at[p, pl.ds(pl.multiple_of((1 - c) * HALF + r0, 16), n)]
+            copy_to(dst, dst, oc.at[s, p], ocr.at[s, p], partner).wait_recv()
+
+
+def summed_gradients(lefts, rights, vectors):
+    dma = pltpu.SemaphoreType.DMA
+    count = len(lefts[0])
+    tokens, width = lefts[0][0].shape
+    rows = count * tokens
+    n_s = len(STREAMS)
+    vm = pl.BlockSpec(memory_space=pltpu.VMEM)
+    return pl.pallas_call(
+        lambda *refs: tail_kernel(count, *refs),
+        name="summed_gradients",
+        out_shape=(jax.ShapeDtypeStruct((PARTS, width, COLS), BF), jax.ShapeDtypeStruct(vectors.shape, F32)),
+        in_specs=[vm] * (4 * count) + [pl.BlockSpec(memory_space=pl.ANY)] * (4 * count) + [vm],
+        out_specs=(pl.BlockSpec(memory_space=pl.ANY), vm),
+        scratch_shapes=[
+            pltpu.VMEM((4, width, rows), BF), pltpu.VMEM((PARTS, rows, COLS), BF), pltpu.VMEM((SLOTS, 2 * HALF, COLS), BF),
+            pltpu.VMEM((PARTS, HALF, COLS), BF), pltpu.VMEM((PARTS, HALF, COLS), BF),
+            *[pltpu.VMEM((8, s[3], COLS), BF) for s in STREAMS],
+            *[pltpu.VMEM((10 if s[1] else 5, s[3], COLS), BF) for s in STREAMS],
+            *[pltpu.VMEM((1 if s[1] else 4, s[3], COLS), BF) for s in STREAMS],
+            pltpu.VMEM((5, *vectors.shape), F32),
+            dma((PARTS * count,)), dma((16,)), dma((16,)),
+            dma((n_s, 8)), dma((n_s, 8)), dma((n_s, 10)), dma((n_s, 10)), dma((n_s, 4)), dma((n_s, 4)),
+            dma((n_s, 4)), dma((n_s, 4)), dma((n_s, 16)), dma((n_s, 8)), dma((n_s, 8)), dma((n_s, 8)), dma((n_s, 16)), dma((n_s, 16)),
+            dma((5,)), dma((5,)), dma((n_s,)),
+        ],
+        compiler_params=pltpu.CompilerParams(collective_id=1, has_side_effects=True, vmem_limit_bytes=60 * 2**20),
+    )(*[a for l in lefts for a in l], *[a for l in rights for a in l], vectors)
 
 
 QUARTERS = 4
@@ -1151,49 +1230,35 @@
     )(partial)
 
 
-ROW_NAMES = ("normed_two", "d_mlp", "normed", "mixed", "d_gate", "d_up", "hidden", "d_q", "d_k", "d_v", "d_attn")
+ROW_NAMES = ("normed_two", "d_mlp", "normed", "mixed", "d_gate", "d_up", "hidden", "d_packed")
 
 
 def grads_kernel(count, *refs):
-    n = len(ROW_NAMES)
     r = {name: refs[i * count : (i + 1) * count] for i, name in enumerate(ROW_NAMES)}
-    g_ref, left_t, slots, sems = refs[n * count :]
+    g_ref, left_t, slots, sems = refs[len(ROW_NAMES) * count :]
     for i, name in enumerate(ROW_NAMES[:4]):
         left_t[i] = jnp.concatenate([each[...].astype(F32).T.astype(BF) for each in r[name]], axis=1)
 
-    def rows_of(name, low, high):
-        return jnp.concatenate([each[:, low:high] for each in r[name]], axis=0)
-
     def out_copy(p):
         return pltpu.make_async_copy(slots.at[p % 2], g_ref.at[p], sems.at[p % 2])
 
-    width = left_t.shape[1]
+    split = 2 * COLS - left_t.shape[1]
     for p in range(PARTS):
         if p >= 2:
             out_copy(p - 2).wait()
-        slot = slots.at[p % 2]
-        if p < 12:
-            name, left = (("d_gate", 0), ("d_up", 0), ("hidden", 1))[p // 4]
-            low = (p % 4) * COLS
-            slot[...] = dot_nn(left_t[left], rows_of(name, low, low + COLS)).astype(BF)
-        elif p == 12:
-            slot[...] = dot_nn(left_t[2], rows_of("d_q", 0, COLS)).astype(BF)
-        elif p == 13:
-            right = jnp.concatenate([rows_of("d_q", COLS, width), rows_of("d_k", 0, 2 * COLS - width)], axis=1)
-            slot[...] = dot_nn(left_t[2], right).astype(BF)
-        elif p == 14:
-            slot[...] = dot_nn(left_t[3], rows_of("d_attn", 0, COLS)).astype(BF)
-        else:
-            one = dot_nn(left_t[3], rows_of("d_attn", COLS, width))
-            two = dot_nn(left_t[2], rows_of("d_v", 0, 2 * COLS - width))
-            slot[...] = jnp.concatenate([one, two], axis=1).astype(BF)
+        low = (p % 4) * COLS
+        right = jnp.concatenate([each[:, low : low + COLS] for each in r[ROW_NAMES[4 + p // 4]]], axis=0)
+        result = dot_nn(left_t[((0,) * 8 + (1,) * 4 + (2, 2, 3, 3))[p]], right)
+        if p == PARTS - 1:
+            result = jnp.concatenate([result[:, : COLS - split], dot_nn(left_t[2], right[:, COLS - split :])], axis=1)
+        slots[p % 2] = result.astype(BF)
         out_copy(p).start()
     out_copy(PARTS - 2).wait()
     out_copy(PARTS - 1).wait()
 
 
 def weight_gradients(rows):
-    count = len(rows["d_q"])
+    count = len(rows["d_mlp"])
     flat = [each for name in ROW_NAMES for each in rows[name]]
     tokens, width = rows["normed"][0].shape
     return pl.pallas_call(
@@ -1336,23 +1401,22 @@
     for step in reversed(range(RECUR)):
         back = backward_stage(kept[step], before, masks[step], lives[step], tables, gains, acc, weights, cotangent.T)
         acc = back["acc_out"]
-        for name in ("d_k", "d_v"):
-            if before is not None:
-                rows_of[name].append(back[name])
-        for name in ("d_mlp", "d_gate", "d_up", "d_q", "d_attn"):
+        if before is not None:
+            rows_of["d_packed"].append(back["d_packed"])
+        for name in ("d_mlp", "d_gate", "d_up"):
             rows_of[name].append(back[name])
         for name in ("normed_two", "mixed", "hidden"):
             rows_of[name].append(kept[step][name])
         rows_of["normed"].append(kept[step]["normed_r"])
-        before = {"home": exchange_home(back["dkv"], n_tok, nback), "d_q": back["d_q"], "state": kept[step]["state"], "d_state": back["d_state"]}
+        before = {"home": exchange_home(back["dkv"], n_tok, nback), "d_q": back["d_q"], "state": kept[step]["state"], "d_state": back["d_state"], "d_attn": back["d_attn"]}
     back = backward_stage(None, before, None, None, tables, gains, acc, weights, None)
-    for name in ("d_k", "d_v"):
-        rows_of[name].append(back[name])
+    rows_of["d_packed"].append(back["d_packed"])
     acc = back["acc_out"]
-    parts = weight_gradients(rows_of)
     if (n_grp, n_tok) == (4, 8):
-        parts, acc = all_sum(parts, acc)
+        lefts, rights = ([rows_of[name] for name in names] for names in (ROW_NAMES[:4], ROW_NAMES[4:]))
+        parts, acc = summed_gradients(lefts, rights, acc)
     else:
+        parts = weight_gradients(rows_of)
         parts = lax.psum(parts.astype(F32), ("grp", "tok")).astype(BF)
         acc = lax.psum(acc, ("grp", "tok"))
     d_gate, d_up, d_down, d_q, d_k, d_v, d_o = spread_out(parts)

time: 547 us -> 520 us (0.951)
  Pallas kernels: 511 us -> 483 us
    pallas_call x2 -> x1, Pallas kernels: 212 us -> 185 us  [summed_gradients(): pl.pallas_call(lambda *refs: tail_kernel(count, *refs), name='summed_grad...]
where the time goes in v4:
time: 520 us; the launch traced here: 514 us
  Pallas kernels  483 us (93%)
  local copies, waits for them, and re-layouts  22.2 us (4%)
  other arithmetic  6.9 us (1%)
    pallas_call x1, Pallas kernels, summed_gradients(): pl.pallas_call(lambda *refs: tail_kernel(count, *refs), name='summed_grad...  185 us
    pallas_call x8, Pallas kernels, stage(): pl.pallas_call(body, name=name, out_shape=tuple(outputs.values()), in_spe...  114 us
    pallas_call x1, Pallas kernels, gather_rows(): pl.pallas_call(gather_kernel, name='gather_rows', out_shape=tuple((jax.Sh...  90.8 us
    pallas_call x3, Pallas kernels, exchange_home(): pl.pallas_call(lambda *refs: home_kernel(n_tok // 2, back, *refs), name='...  48.2 us
    pallas_call x3, Pallas kernels, exchange_keys(): pl.pallas_call(lambda *refs: keys_kernel(n_tok // 2, back, *refs), name='...  25.1 us
    pallas_call x1, Pallas kernels, spread_out(): pl.pallas_call(spread_kernel, name='spread_out', out_shape=tuple((jax.Sha...  19.9 us
    unnamed x26, local copies, waits for them, and re-layouts  13.3 us

profile of v4, /device:TPU:0, one launch (start us, length us, event | category | flops | bytes accessed | tf_op | source)
XLA Modules:
  0.0 513.7 jit_solution(4224873330812059902)
XLA Ops:
  7.7 1.0 copy.45
  8.7 1.0 copy.46
  10.1 0.8 pad_maximum_fusion
  10.9 2.0 concatenate.14.refs_0_
  12.9 90.8 %gather_rows.1 = (bf16[8,120,2560]{2,1,0:T(8,128)(2,1)}, bf16[8,120,2560]{2,1,0:T(8,128)(2,1)}, bf16[8,120,2560]{2,1,0:T(8,128)(2,1)}, bf16[8,320,960]{2,1,0:T(8,128)(2,1)}, bf16[8,16,128]{2,1,0:T(8,128)(2,1)}) custom-call(bf16[120,2560]{1,0:T(8,128)(2,1)} %concatenate.14.refs_0_, bf16[120,2560]{1,0:T(8,128)(2,1)} %refs_1_.1, bf16[120,2560]{1,0:T(8,128)(2,1)} %refs_2_.1, ...), custom_call_target="tpu_custom_call" | custom-call | tf_op jit(solution)/shard_map/gather_rows/pallas_call | solution.py:1061
  106.2 1.0 slice_bitcast_fusion
  107.2 5.1 %first.1 = (bf16[128,960]{1,0:T(8,128)(2,1)}, bf16[128,960]{1,0:T(8,128)(2,1)}, bf16[128,640]{1,0:T(8,128)(2,1)}, f32[128,960]{1,0:T(8,128)}) custom-call(bf16[960,128]{1,0:T(8,128)(2,1)} %bitcast.68, f32[128,128]{1,0:T(8,128)} %get-tuple-element.184.refs_1_.refs_5_.refs_0_, f32[128,128]{1,0:T(8,128)} %get-tuple-element.185.refs_2_.refs_6_.refs_1_, ...), custom_call_target="tpu_custom_call" | custom-call | tf_op jit(solution)/shard_map/first/pallas_call | solution.py:271
  112.3 0.9 copy-done.11
  113.3 4.6 exchange_keys.3.refs_2_.refs_16_
  117.9 0.9 copy-done
  118.8 13.1 %forward.3 = (bf16[128,960]{1,0:T(8,128)(2,1)}, f32[8,384]{1,0:T(8,128)}, f32[128,960]{1,0:T(8,128)}, bf16[128,960]{1,0:T(8,128)(2,1)}, f32[128,2560]{1,0:T(8,12...) custom-call(f32[128,960]{1,0:T(8,128)} %get-tuple-element.94.refs_0_, ...), custom_call_target="tpu_custom_call" | custom-call | tf_op jit(solution)/shard_map/forward/pallas_call | solution.py:271
  132.0 0.9 copy-done.9
  132.9 9.1 %exchange_keys.4.refs_2_.refs_16_ = bf16[768,640]{1,0:T(8,128)(2,1)S(1)} custom-call(bf16[128,640]{1,0:T(8,128)(2,1)S(1)} %copy-done.9), custom_call_target="tpu_custom_call" | custom-call | tf_op jit(solution)/shard_map/exchange_keys/pallas_call | solution.py:1147
  141.9 1.0 copy-done.1
  142.9 13.1 %forward.4 = (bf16[128,960]{1,0:T(8,128)(2,1)}, f32[8,384]{1,0:T(8,128)}, f32[128,960]{1,0:T(8,128)}, bf16[128,960]{1,0:T(8,128)(2,1)}, f32[128,2560]{1,0:T(8,12...) custom-call(f32[128,960]{1,0:T(8,128)} %get-tuple-element.100.refs_0, ...), custom_call_target="tpu_custom_call" | custom-call | tf_op jit(solution)/shard_map/forward/pallas_call | solution.py:271
  156.1 0.9 copy-done.10
  157.0 11.4 %exchange_keys.5.refs_2_.refs_12_ = bf16[768,640]{1,0:T(8,128)(2,1)S(1)} custom-call(bf16[128,640]{1,0:T(8,128)(2,1)S(1)} %copy-done.10), custom_call_target="tpu_custom_call" | custom-call | tf_op jit(solution)/shard_map/exchange_keys/pallas_call | solution.py:1147
  168.4 0.9 copy-done.2
  169.4 12.7 %forward.5 = (bf16[128,960]{1,0:T(8,128)(2,1)}, f32[8,384]{1,0:T(8,128)}, f32[128,960]{1,0:T(8,128)}, bf16[128,960]{1,0:T(8,128)(2,1)}, f32[128,2560]{1,0:T(8,12...) custom-call(f32[128,960]{1,0:T(8,128)} %get-tuple-element.103.refs_0_.refs_, ...), custom_call_target="tpu_custom_call" | custom-call | tf_op jit(solution)/shard_map/forward/pallas_call | solution.py:271
  182.6 20.1 %backward.4 = (f32[8,1024]{1,0:T(8,128)}, bf16[128,960]{1,0:T(8,128)(2,1)}, bf16[128,2560]{1,0:T(8,128)(2,1)}, bf16[128,2560]{1,0:T(8,128)(2,1)}, bf16[128,960]{...) custom-call(f32[128,128]{1,0:T(8,128)} %get-tuple-element.184.refs_1_.refs_5_.refs_0_, ...), custom_call_target="tpu_custom_call" | custom-call | tf_op jit(solution)/shard_map/backward/pallas_call | solution.py:271
  202.7 1.2 copy-done.8
  203.9 21.8 %exchange_home.3.refs_4_ = f32[1,128,640]{2,1,0:T(8,128)S(1)} custom-call(bf16[768,640]{1,0:T(8,128)(2,1)S(1)} %copy-done.8), custom_call_target="tpu_custom_call" | custom-call | tf_op jit(solution)/shard_map/exchange_home/pallas_call | solution.py:1219
  226.5 21.9 %backward.5 = (f32[8,1024]{1,0:T(8,128)}, bf16[128,2560]{1,0:T(8,128)(2,1)}, bf16[128,960]{1,0:T(8,128)(2,1)}, bf16[128,2560]{1,0:T(8,128)(2,1)}, bf16[128,2560]...) custom-call(f32[128,128]{1,0:T(8,128)} %get-tuple-element.184.refs_1, ...), custom_call_target="tpu_custom_call" | custom-call | tf_op jit(solution)/shard_map/backward/pallas_call | solution.py:271
  248.5 1.2 copy-done.7
  249.7 14.1 %exchange_home.4.refs_4_ = f32[1,128,640]{2,1,0:T(8,128)S(1)} custom-call(bf16[768,640]{1,0:T(8,128)(2,1)S(1)} %copy-done.7), custom_call_target="tpu_custom_call" | custom-call | tf_op jit(solution)/shard_map/exchange_home/pallas_call | solution.py:1219
  264.5 21.9 %backward.6 = (f32[8,1024]{1,0:T(8,128)}, bf16[128,2560]{1,0:T(8,128)(2,1)}, bf16[128,960]{1,0:T(8,128)(2,1)}, bf16[128,2560]{1,0:T(8,128)(2,1)}, bf16[128,2560]...) custom-call(f32[128,128]{1,0:T(8,128)} %get-tuple-element.184.refs_1, ...), custom_call_target="tpu_custom_call" | custom-call | tf_op jit(solution)/shard_map/backward/pallas_call | solution.py:271
  286.4 1.2 copy-done.6
  287.6 12.3 %exchange_home.5.refs_4_ = f32[1,128,640]{2,1,0:T(8,128)S(1)} custom-call(bf16[768,640]{1,0:T(8,128)(2,1)S(1)} %copy-done.6), custom_call_target="tpu_custom_call" | custom-call | tf_op jit(solution)/shard_map/exchange_home/pallas_call | solution.py:1219
  300.6 6.3 %backward.7 = (f32[8,1024]{1,0:T(8,128)}, bf16[128,2560]{1,0:T(8,128)(2,1)}, f32[960,128]{1,0:T(8,128)}) custom-call(f32[128,128]{1,0:T(8,128)} %get-tuple-element.184.refs_1_.refs_5_.refs_0_, f32[128,128]{1,0:T(8,128)} %get-tuple-element.185.refs_2_.refs_6_.refs_1_, f32[8,960]{1,0:T(8,128)} %pad_convert_fusion.refs_3_.refs_7_.refs_2_, ...), custom_call_target="tpu_custom_call" | custom-call | tf_op jit(solution)/shard_map/backward/pallas_call | solution.py:271
  307.0 185.0 %summed_gradients.1 = (bf16[16,960,640]{2,1,0:T(8,128)(2,1)}, f32[8,1024]{1,0:T(8,128)}) custom-call(bf16[128,960]{1,0:T(8,128)(2,1)} %get-tuple-element.138.refs_0_, bf16[128,960]{1,0:T(8,128)(2,1)} %get-tuple-element.139.refs_1_, bf16[128,960]{1,0:T(8,128)(2,1)} %get-tuple-element.140.refs_2_, bf16[128,960]{1,0:T(8,128)(2,1)} %get-tuple-element.141.refs_3_, ...), custom_call_target="tpu_custom_call" | custom-call | tf_op jit(solution)/shard_map/summed_gradients/pallas_call | solution.py:851
  492.0 1.5 fusion.8
  493.5 19.9 %spread_out.1 = (f32[960,2560]{1,0:T(8,128)}, f32[960,2560]{1,0:T(8,128)}, f32[960,2560]{1,0:T(8,128)}, f32[960,960]{1,0:T(8,128)}, f32[320,960]{1,0:T(8,128)}, /*index=5*/f32[320,960]{1,0:T(8,128)}, f32[960,960]{1,0:T(8,128)}) custom-call(bf16[16,960,640]{2,1,0:T(8,128)(2,1)} %get-tuple-element.164.p_ref), custom_call_target="tpu_custom_call" | custom-call | tf_op jit(solution)/shard_map/spread_out/pallas_call | solution.py:1325
  (43 shorter events, 12.7 us)
Async XLA Ops:
  112.3 0.9 copy-start.11
  117.9 0.9 copy-start
  131.9 0.9 copy-start.9
  141.9 1.0 copy-start.1
  156.1 0.9 copy-start.10
  168.4 0.9 copy-start.2
  202.7 1.2 copy-start.8
  225.8 0.7 copy-start.5
  248.4 1.2 copy-start.7
  263.8 0.7 copy-start.4
  286.4 1.2 copy-start.6
  299.9 0.7 copy-start.3

commit v5 on v4

--- a/solution.py
+++ b/solution.py
@@ -247,35 +247,20 @@
     def body(*refs):
         it = iter(refs)
         r = {n: next(it) for n in in_names}
-        src = {n: next(it) for n in w_names}
+        for n in w_names:
+            r[n + "_v"] = next(it)
         for n in out_names:
             r[n] = next(it)
-        for n in w_names:
-            r[n + "_v"] = next(it)
-        sems = next(it)
-        copies = {n: pltpu.make_async_copy(src[n], r[n + "_v"], sems.at[i]) for i, n in enumerate(w_names)}
-        for n in w_names:
-            copies[n].start()
-        done = set()
-
-        def wait(n):
-            if n not in done:
-                copies[n].wait()
-                done.add(n)
-
-        parts(r, wait)
-        for n in w_names:
-            wait(n)
+        parts(r, lambda n: None)
 
     vm = pl.BlockSpec(memory_space=pltpu.VMEM)
     out = pl.pallas_call(
         body,
         name=name,
         out_shape=tuple(outputs.values()),
-        in_specs=[vm] * len(in_names) + [pl.BlockSpec(memory_space=pl.ANY)] * len(w_names),
+        in_specs=[vm] * (len(in_names) + len(w_names)),
         out_specs=tuple([vm] * len(out_names)),
-        scratch_shapes=[pltpu.VMEM(weights[n].shape, BF) for n in w_names] + [pltpu.SemaphoreType.DMA((len(w_names),))],
-        compiler_params=pltpu.CompilerParams(vmem_limit_bytes=60 * 2**20),
+        compiler_params=pltpu.CompilerParams(vmem_limit_bytes=20 * 2**20),
     )(*inputs.values(), *[weights[n] for n in w_names])
     return dict(zip(out_names, out))
 
@@ -1151,7 +1136,7 @@
         in_specs=[pl.BlockSpec(memory_space=pltpu.VMEM)],
         out_specs=pl.BlockSpec(memory_space=pltpu.VMEM),
         scratch_shapes=[dma((back,)), dma((back,)), dma((back + 1,)), dma((back + 1,))],
-        compiler_params=pltpu.CompilerParams(collective_id=2, has_side_effects=True, vmem_limit_bytes=32 * 2**20),
+        compiler_params=pltpu.CompilerParams(collective_id=2, has_side_effects=True, vmem_limit_bytes=12 * 2**20),
     )(kv)
 
 
@@ -1226,7 +1211,7 @@
             pltpu.VMEM((back + 1, rows, width), BF), pltpu.VMEM((back, rows, width), BF), pltpu.VMEM((back, rows, width), BF),
             dma((back,)), dma((back,)), dma((back + 1,)), dma((back + 1,)),
         ],
-        compiler_params=pltpu.CompilerParams(collective_id=3, has_side_effects=True, vmem_limit_bytes=32 * 2**20),
+        compiler_params=pltpu.CompilerParams(collective_id=3, has_side_effects=True, vmem_limit_bytes=12 * 2**20),
     )(partial)
 
 

time: 520 us -> 465 us (0.89)
  Pallas kernels: 483 us -> 429 us
    pallas_call x8, Pallas kernels: 114 us -> 60.1 us  [stage(): pl.pallas_call(body, name=name, out_shape=tuple(outputs.values()), in_spe...]
    unnamed x26 -> x64, local copies, waits for them, and re-layouts: 13.3 us -> 17.7 us
where the time goes in v5:
time: 465 us; the launch traced here: 459 us
  Pallas kernels  429 us (92%)
  local copies, waits for them, and re-layouts  23.2 us (5%)
  other arithmetic  5.63 us (1%)
    pallas_call x1, Pallas kernels, summed_gradients(): pl.pallas_call(lambda *refs: tail_kernel(count, *refs), name='summed_grad...  185 us
    pallas_call x1, Pallas kernels, gather_rows(): pl.pallas_call(gather_kernel, name='gather_rows', out_shape=tuple((jax.Sh...  90.8 us
    pallas_call x8, Pallas kernels, stage(): pl.pallas_call(body, name=name, out_shape=tuple(outputs.values()), in_spe...  60.1 us
    pallas_call x3, Pallas kernels, exchange_home(): pl.pallas_call(lambda *refs: home_kernel(n_tok // 2, back, *refs), name='...  48.3 us
    pallas_call x3, Pallas kernels, exchange_keys(): pl.pallas_call(lambda *refs: keys_kernel(n_tok // 2, back, *refs), name='...  25.2 us
    pallas_call x1, Pallas kernels, spread_out(): pl.pallas_call(spread_kernel, name='spread_out', out_shape=tuple((jax.Sha...  19.9 us
    unnamed x64, local copies, waits for them, and re-layouts  17.7 us

profile of v5, /device:TPU:0, one launch (start us, length us, event | category | flops | bytes accessed | tf_op | source)
XLA Modules:
  0.0 459.4 jit_solution(17300950457091974607)
XLA Ops:
  0.6 0.8 select_reduce_fusion.1
  4.4 0.8 convert_bitcast_fusion
  5.9 1.0 copy.45
  6.9 1.0 copy.46
  8.4 2.0 concatenate.14.refs_0_
  10.4 90.8 %gather_rows.1 = (bf16[8,120,2560]{2,1,0:T(8,128)(2,1)}, bf16[8,120,2560]{2,1,0:T(8,128)(2,1)}, bf16[8,120,2560]{2,1,0:T(8,128)(2,1)}, bf16[8,320,960]{2,1,0:T(8,128)(2,1)}, bf16[8,16,128]{2,1,0:T(8,128)(2,1)}) custom-call(bf16[120,2560]{1,0:T(8,128)(2,1)} %concatenate.14.refs_0_, bf16[120,2560]{1,0:T(8,128)(2,1)} %refs_1_.1, bf16[120,2560]{1,0:T(8,128)(2,1)} %refs_2_.1, ...), custom_call_target="tpu_custom_call" | custom-call | tf_op jit(solution)/shard_map/gather_rows/pallas_call | solution.py:1046
  103.3 2.4 copy-done
  105.6 1.3 first.1
  107.7 4.6 %exchange_keys.3.refs_2_.refs_16_ = bf16[768,640]{1,0:T(8,128)(2,1)S(1)} custom-call(bf16[128,640]{1,0:T(8,128)(2,1)S(1)} %get-tuple-element.96.refs_0_), custom_call_target="tpu_custom_call" | custom-call | tf_op jit(solution)/shard_map/exchange_keys/pallas_call | solution.py:1132
  112.3 2.4 copy-done.2
  114.7 2.4 copy-done.3
  117.1 7.3 %forward.3 = (bf16[128,960]{1,0:T(8,128)(2,1)S(1)}, f32[8,384]{1,0:T(8,128)S(1)}, f32[128,960]{1,0:T(8,128)S(1)}, bf16[128,960]{1,0:T(8,128)(2,1)S(1)}, f32[128,...) custom-call(f32[128,960]{1,0:T(8,128)S(1)} %get-tuple-element.94.ref, ...), custom_call_target="tpu_custom_call" | custom-call | tf_op jit(solution)/shard_map/forward/pallas_call | solution.py:257
  124.4 9.1 %exchange_keys.4.refs_2_.refs_16_ = bf16[768,640]{1,0:T(8,128)(2,1)S(1)} custom-call(bf16[128,640]{1,0:T(8,128)(2,1)S(1)} %get-tuple-element.102.refs_0_), custom_call_target="tpu_custom_call" | custom-call | tf_op jit(solution)/shard_map/exchange_keys/pallas_call | solution.py:1132
  133.6 7.4 %forward.4 = (bf16[128,960]{1,0:T(8,128)(2,1)S(1)}, f32[8,384]{1,0:T(8,128)S(1)}, f32[128,960]{1,0:T(8,128)S(1)}, bf16[128,960]{1,0:T(8,128)(2,1)S(1)}, f32[128,...) custom-call(f32[128,960]{1,0:T(8,128)S(1)} %get-tuple-element.100.re, ...), custom_call_target="tpu_custom_call" | custom-call | tf_op jit(solution)/shard_map/forward/pallas_call | solution.py:257
  141.7 11.4 %exchange_keys.5.refs_2_.refs_12_ = bf16[768,640]{1,0:T(8,128)(2,1)S(1)} custom-call(bf16[128,640]{1,0:T(8,128)(2,1)S(1)} %get-tuple-element.105.refs_0_), custom_call_target="tpu_custom_call" | custom-call | tf_op jit(solution)/shard_map/exchange_keys/pallas_call | solution.py:1132
  153.2 7.0 %forward.5 = (bf16[128,960]{1,0:T(8,128)(2,1)S(1)}, f32[8,384]{1,0:T(8,128)S(1)}, f32[128,960]{1,0:T(8,128)S(1)}, bf16[128,960]{1,0:T(8,128)(2,1)S(1)}, f32[128,...) custom-call(f32[128,960]{1,0:T(8,128)S(1)} %get-tuple-element.103.re, ...), custom_call_target="tpu_custom_call" | custom-call | tf_op jit(solution)/shard_map/forward/pallas_call | solution.py:257
  160.9 10.9 %backward.4 = (f32[8,1024]{1,0:T(8,128)S(1)}, bf16[128,960]{1,0:T(8,128)(2,1)S(1)}, bf16[128,2560]{1,0:T(8,128)(2,1)S(1)}, bf16[128,2560]{1,0:T(8,128)(2,1)S(1)}...) custom-call(f32[128,128]{1,0:T(8,128)S(1)} %get-tuple-element.184.re, ...), custom_call_target="tpu_custom_call" | custom-call | tf_op jit(solution)/shard_map/backward/pallas_call | solution.py:257
  171.9 0.8 copy-done.7
  172.7 0.8 copy-done.8
  174.2 21.8 %exchange_home.3.refs_4_ = f32[1,128,640]{2,1,0:T(8,128)S(1)} custom-call(bf16[768,640]{1,0:T(8,128)(2,1)S(1)} %get-tuple-element.113.refs_0_), custom_call_target="tpu_custom_call" | custom-call | tf_op jit(solution)/shard_map/exchange_home/pallas_call | solution.py:1204
  196.1 11.9 %backward.5 = (f32[8,1024]{1,0:T(8,128)S(1)}, bf16[128,2560]{1,0:T(8,128)(2,1)S(1)}, bf16[128,960]{1,0:T(8,128)(2,1)S(1)}, bf16[128,2560]{1,0:T(8,128)(2,1)S(1)}...) custom-call(f32[128,128]{1,0:T(8,128)S(1)} %get-tuple-element.184.re, ...), custom_call_target="tpu_custom_call" | custom-call | tf_op jit(solution)/shard_map/backward/pallas_call | solution.py:257
  208.0 0.8 copy-done.9
  208.9 0.8 copy-done.10
  209.7 0.8 copy-done.11
  210.6 14.1 %exchange_home.4.refs_4_ = f32[1,128,640]{2,1,0:T(8,128)S(1)} custom-call(bf16[768,640]{1,0:T(8,128)(2,1)S(1)} %get-tuple-element.123.refs_0_), custom_call_target="tpu_custom_call" | custom-call | tf_op jit(solution)/shard_map/exchange_home/pallas_call | solution.py:1204
  224.7 11.9 %backward.6 = (f32[8,1024]{1,0:T(8,128)S(1)}, bf16[128,2560]{1,0:T(8,128)(2,1)S(1)}, bf16[128,960]{1,0:T(8,128)(2,1)S(1)}, bf16[128,2560]{1,0:T(8,128)(2,1)S(1)}...) custom-call(f32[128,128]{1,0:T(8,128)S(1)} %get-tuple-element.184.re, ...), custom_call_target="tpu_custom_call" | custom-call | tf_op jit(solution)/shard_map/backward/pallas_call | solution.py:257
  236.6 12.4 %exchange_home.5.refs_4_ = f32[1,128,640]{2,1,0:T(8,128)S(1)} custom-call(bf16[768,640]{1,0:T(8,128)(2,1)S(1)} %get-tuple-element.133.refs_0_), custom_call_target="tpu_custom_call" | custom-call | tf_op jit(solution)/shard_map/exchange_home/pallas_call | solution.py:1204
  249.0 2.3 backward.7
  251.3 0.8 copy-done.15
  252.8 185.0 %summed_gradients.1 = (bf16[16,960,640]{2,1,0:T(8,128)(2,1)}, f32[8,1024]{1,0:T(8,128)}) custom-call(bf16[128,960]{1,0:T(8,128)(2,1)} %copy-done.24, bf16[128,960]{1,0:T(8,128)(2,1)} %copy-done.21, bf16[128,960]{1,0:T(8,128)(2,1)} %copy-done.18, bf16[128,960]{1,0:T(8,128)(2,1)} %copy-done.25, bf16[128,960]{1,0:T(8,128)(2,1)} %copy-done.26, ...), custom_call_target="tpu_custom_call" | custom-call | tf_op jit(solution)/shard_map/summed_gradients/pallas_call | solution.py:836
  437.7 1.5 fusion.8
  439.2 19.9 %spread_out.1 = (f32[960,2560]{1,0:T(8,128)}, f32[960,2560]{1,0:T(8,128)}, f32[960,2560]{1,0:T(8,128)}, f32[960,960]{1,0:T(8,128)}, f32[320,960]{1,0:T(8,128)}, /*index=5*/f32[320,960]{1,0:T(8,128)}, f32[960,960]{1,0:T(8,128)}) custom-call(bf16[16,960,640]{2,1,0:T(8,128)(2,1)} %get-tuple-element.164.p_ref), custom_call_target="tpu_custom_call" | custom-call | tf_op jit(solution)/shard_map/spread_out/pallas_call | solution.py:1310
  (81 shorter events, 9.6 us)
Async XLA Ops:
  5.9 97.3 %copy-start.28 = (bf16[128,960]{0,1:T(8,128)(2,1)S(1)}, bf16[128,960]{0,1:T(8,128)(2,1)}, u32[]{:S(2)}) copy-start(bf16[128,960]{0,1:T(8,128)(2,1)} %param.14) | copy-start | bytes 737284
  103.2 2.4 copy-start
  105.6 6.6 %copy-start.1 = (bf16[8,320,960]{2,1,0:T(8,128)(2,1)S(1)}, bf16[8,320,960]{2,1,0:T(8,128)(2,1)}, u32[]{:S(2)}) copy-start(bf16[8,320,960]{2,1,0:T(8,128)(2,1)} %get-tuple-element.99) | copy-start | bytes 14745604
  107.0 0.7 copy-start.16
  112.3 2.4 copy-start.2
  114.7 2.4 copy-start.3
  124.4 16.5 %copy-start.4 = (bf16[128,2560]{1,0:T(8,128)(2,1)}, bf16[128,2560]{1,0:T(8,128)(2,1)S(1)}, u32[]{:S(2)}) copy-start(bf16[128,2560]{1,0:T(8,128)(2,1)S(1)} %get-tuple-element.158.refs_20_) | copy-start | bytes 1966084
  124.4 16.5 %copy-start.17 = (bf16[128,960]{1,0:T(8,128)(2,1)}, bf16[128,960]{1,0:T(8,128)(2,1)S(1)}, u32[]{:S(2)}) copy-start(bf16[128,960]{1,0:T(8,128)(2,1)S(1)} %get-tuple-element.149.refs_11_) | copy-start | bytes 737284
  124.4 16.5 %copy-start.18 = (bf16[128,960]{1,0:T(8,128)(2,1)}, bf16[128,960]{1,0:T(8,128)(2,1)S(1)}, u32[]{:S(2)}) copy-start(bf16[128,960]{1,0:T(8,128)(2,1)S(1)} %get-tuple-element.140.refs_2_) | copy-start | bytes 737284
  124.4 16.5 %copy-start.19 = (bf16[128,960]{1,0:T(8,128)(2,1)}, bf16[128,960]{1,0:T(8,128)(2,1)S(1)}, u32[]{:S(2)}) copy-start(bf16[128,960]{1,0:T(8,128)(2,1)S(1)} %get-tuple-element.145.refs_7_) | copy-start | bytes 737284
  141.0 0.7 copy-start.22
  141.7 18.5 %copy-start.5 = (bf16[128,2560]{1,0:T(8,128)(2,1)}, bf16[128,2560]{1,0:T(8,128)(2,1)S(1)}, u32[]{:S(2)}) copy-start(bf16[128,2560]{1,0:T(8,128)(2,1)S(1)} %get-tuple-element.157.refs_19_) | copy-start | bytes 1966084
  141.7 18.5 %copy-start.20 = (bf16[128,960]{1,0:T(8,128)(2,1)}, bf16[128,960]{1,0:T(8,128)(2,1)S(1)}, u32[]{:S(2)}) copy-start(bf16[128,960]{1,0:T(8,128)(2,1)S(1)} %get-tuple-element.148.refs_10_) | copy-start | bytes 737284
  141.7 18.5 %copy-start.21 = (bf16[128,960]{1,0:T(8,128)(2,1)}, bf16[128,960]{1,0:T(8,128)(2,1)S(1)}, u32[]{:S(2)}) copy-start(bf16[128,960]{1,0:T(8,128)(2,1)S(1)} %get-tuple-element.139.refs_1_) | copy-start | bytes 737284
  153.1 7.8 %copy-start.29 = (bf16[128,960]{0,1:T(8,128)(2,1)S(1)}, bf16[128,960]{0,1:T(8,128)(2,1)}, u32[]{:S(2)}) copy-start(bf16[128,960]{0,1:T(8,128)(2,1)} %param.15) | copy-start | bytes 737284
  160.2 0.7 copy-start.23
  160.9 10.9 %copy-start.6 = (bf16[128,2560]{1,0:T(8,128)(2,1)}, bf16[128,2560]{1,0:T(8,128)(2,1)S(1)}, u32[]{:S(2)}) copy-start(bf16[128,2560]{1,0:T(8,128)(2,1)S(1)} %get-tuple-element.156.refs_18_) | copy-start | bytes 1966084
  160.9 10.9 %copy-start.24 = (bf16[128,960]{1,0:T(8,128)(2,1)}, bf16[128,960]{1,0:T(8,128)(2,1)S(1)}, u32[]{:S(2)}) copy-start(bf16[128,960]{1,0:T(8,128)(2,1)S(1)} %get-tuple-element.138.refs_0_) | copy-start | bytes 737284
  171.9 0.8 copy-start.7
  172.7 0.8 copy-start.8
  173.5 0.7 copy-start.25
  208.0 0.9 copy-start.9
  208.9 0.8 copy-start.10
  209.7 0.8 copy-start.11
  210.6 26.0 %copy-start.26 = (bf16[128,960]{1,0:T(8,128)(2,1)}, bf16[128,960]{1,0:T(8,128)(2,1)S(1)}, u32[]{:S(2)}) copy-start(bf16[128,960]{1,0:T(8,128)(2,1)S(1)} %get-tuple-element.142.refs_4_) | copy-start | bytes 737284
  236.6 14.7 %copy-start.12 = (bf16[128,2560]{1,0:T(8,128)(2,1)}, bf16[128,2560]{1,0:T(8,128)(2,1)S(1)}, u32[]{:S(2)}) copy-start(bf16[128,2560]{1,0:T(8,128)(2,1)S(1)} %get-tuple-element.160.refs_22_) | copy-start | bytes 1966084
  236.6 14.7 %copy-start.13 = (bf16[128,2560]{1,0:T(8,128)(2,1)}, bf16[128,2560]{1,0:T(8,128)(2,1)S(1)}, u32[]{:S(2)}) copy-start(bf16[128,2560]{1,0:T(8,128)(2,1)S(1)} %get-tuple-element.155.refs_17_) | copy-start | bytes 1966084
  236.6 14.7 %copy-start.14 = (bf16[128,2560]{1,0:T(8,128)(2,1)}, bf16[128,2560]{1,0:T(8,128)(2,1)S(1)}, u32[]{:S(2)}) copy-start(bf16[128,2560]{1,0:T(8,128)(2,1)S(1)} %get-tuple-element.152.refs_14_) | copy-start | bytes 1966084
  236.6 14.7 %copy-start.27 = (bf16[128,960]{1,0:T(8,128)(2,1)}, bf16[128,960]{1,0:T(8,128)(2,1)S(1)}, u32[]{:S(2)}) copy-start(bf16[128,960]{1,0:T(8,128)(2,1)S(1)} %get-tuple-element.143.refs_5_) | copy-start | bytes 737284
  251.3 0.8 copy-start.15
  252.2 0.6 copy-start.30

commit v6 on v5

--- a/solution.py
+++ b/solution.py
@@ -74,16 +74,20 @@
     return lax.rsqrt(jnp.mean(rows * rows, axis=1, keepdims=True) + epsilon)
 
 
-def front_part(r, wait, state):
+def front_part(r, wait, state, ready=None):
     gain = r["gains"][0:1, :]
     normed = (state * inverse_of(state) * gain).astype(BF)
     r["normed"][...] = normed
     wait("wa")
-    values = dot_nn(normed, r["wa_v"][:, QKO:])
-    turned = rope_lanes(dot_nn(normed, r["wa_v"][:, :QK]), r["cos"][...], r["sin"][...], 1.0).astype(BF)
+    values = dot_nn(normed, r["wa_v"][:, QKO:]).astype(BF)
     qw = H * HD
-    r["q"][...] = turned[:, :qw]
-    r["kv"][...] = jnp.concatenate([turned[:, qw:], values.astype(BF)], axis=1)
+    even = qw // (2 * HD) * (2 * HD)
+    tail = rope_lanes(dot_nn(normed, r["wa_v"][:, even:QK]), r["cos"][...], r["sin"][...], 1.0).astype(BF)
+    r["kv"][...] = jnp.concatenate([tail[:, qw - even :], values], axis=1)
+    if ready is not None:
+        ready()
+    queries = rope_lanes(dot_nn(normed, r["wa_v"][:, :even]), r["cos"][...], r["sin"][...], 1.0).astype(BF)
+    r["q"][...] = jnp.concatenate([queries, tail[:, : qw - even]], axis=1)
 
 
 def head_rows(tensor, g):
@@ -271,6 +275,205 @@
 
 def front_outs(rows, width):
     return {"normed": shaped((rows, width), BF), "q": shaped((rows, H * HD), BF), "kv": shaped((rows, 2 * KVH * HD), BF)}
+
+
+def recursion_kernel(chips, back, in_names, out_names, scratch_names, *refs):
+    names = in_names + list(WEIGHTS) + out_names + scratch_names
+    r = dict(zip(names, refs, strict=True))
+    g, t = lax.axis_index("grp"), lax.axis_index("tok")
+    z, c = t // 2, lax.rem(t, 2)
+    rows = r["hidden_in"].shape[1]
+    partner, left, right = (g, z * 2 + 1 - c), (g, t - 2), (g, t + 2)
+
+    copies = {n: pltpu.make_async_copy(r[n], r[n + "_v"], r["w_sem"].at[i]) for i, n in enumerate(WEIGHTS)}
+    for n in WEIGHTS:
+        copies[n].start()
+    done = set()
+
+    def wait(n):
+        if n not in done:
+            copies[n].wait()
+            done.add(n)
+
+    bar = pltpu.get_barrier_semaphore()
+    pl.semaphore_signal(bar, inc=1, device_id=partner, device_id_type=MESH)
+
+    @pl.when(z > 0)
+    def _():
+        pl.semaphore_signal(bar, inc=1, device_id=left, device_id_type=MESH)
+
+    @pl.when(z < chips - 1)
+    def _():
+        pl.semaphore_signal(bar, inc=1, device_id=right, device_id_type=MESH)
+
+    def at(d, core):
+        return pl.ds(pl.multiple_of(((back - d) * 2 + core) * rows, 128), rows)
+
+    r["acc_out"][...] = jnp.zeros(r["acc_out"].shape, F32)
+    for step in range(RECUR):
+        for d in range(1, back + 1):
+            @pl.when(z < d)
+            def _():
+                for core in (0, 1):
+                    r["kvw"][step, at(d, core), :] = jnp.zeros((rows, r["kvw"].shape[2]), BF)
+
+    def of_step(step):
+        every = {n: r[n] for n in ("gains", "cos", "sin", "acc_out", "d_state", "d_q", "d_attn", "dkv", "home")}
+        every |= {n + "_v": r[n + "_v"] for n in WEIGHTS}
+        for n in ("normed", "mixed", "normed_two", "hidden", "d_mlp", "d_gate", "d_up", "d_packed"):
+            every[n] = r[n + str(step)]
+        for n in ("q", "kvw", "mask", "live", "state", "lse", "middle", "branch", "gate", "up"):
+            every[n] = r[n].at[step]
+        every |= {"q_in": every["q"], "kv": r["kvw"].at[step, at(0, c)], "acc": r["acc_out"]}
+        every |= {"b_" + n: every[n] for n in ("state", "live", "branch", "gate", "up", "middle", "lse")}
+        every |= {"h_dq": r["d_q"], "h_state": every["state"], "h_d_state": r["d_state"], "h_d_attn": r["d_attn"]}
+        return every
+
+    def k_along(step, d):
+        here = r["kvw"].at[step, at(d - 1, c)]
+        return copy_to(here, r["kvw"].at[step, at(d, c)], r["k_s"].at[step, d - 1], r["k_r"].at[step, d - 1], right)
+
+    def k_beside(step, d):
+        here = r["kvw"].at[step, at(d, c)]
+        return copy_to(here, here, r["kc_s"].at[step, d], r["kc_r"].at[step, d], partner)
+
+    def keys_start(step):
+        @pl.when(z < chips - 1)
+        def _():
+            k_along(step, 1).start()
+
+        k_beside(step, 0).start()
+
+    def keys_end(step):
+        for d in range(1, back + 1):
+            @pl.when(z >= d)
+            def _():
+                k_along(step, d).wait_recv()
+                if d < back:
+                    @pl.when(z < chips - 1)
+                    def _():
+                        k_along(step, d + 1).start()
+                k_beside(step, d).start()
+
+        k_beside(step, 0).wait_recv()
+        for d in range(1, back + 1):
+            @pl.when(z >= d)
+            def _():
+                k_beside(step, d).wait_recv()
+
+    def keys_drain(step):
+        k_beside(step, 0).wait_send()
+        for d in range(1, back + 1):
+            @pl.when(z >= d)
+            def _():
+                k_beside(step, d).wait_send()
+
+            @pl.when((z >= d - 1) & (z < chips - 1))
+            def _():
+                k_along(step, d).wait_send()
+
+    def h_beside(step, d):
+        return copy_to(r["dkv"].at[at(d, 1 - c)], r["beside_in"].at[step, d], r["hc_s"].at[step, d], r["hc_r"].at[step, d], partner)
+
+    def h_along(step, d):
+        return copy_to(r["sums"].at[d - 1], r["after_in"].at[step, d - 1], r["h_s"].at[step, d - 1], r["h_r"].at[step, d - 1], left)
+
+    def home_start(step):
+        for d in range(back, 0, -1):
+            @pl.when(z >= d)
+            def _():
+                h_beside(step, d).start()
+        h_beside(step, 0).start()
+
+    def home_end(step):
+        for d in range(back, 0, -1):
+            @pl.when(z >= d)
+            def _():
+                h_beside(step, d).wait_recv()
+                r["sums"][d - 1] = (r["dkv"][at(d, c), :].astype(F32) + r["beside_in"][step, d].astype(F32)).astype(BF)
+                if d < back:
+                    @pl.when(z < chips - 1)
+                    def _():
+                        h_along(step, d + 1).wait_recv()
+                        r["sums"][d - 1] = (r["sums"][d - 1].astype(F32) + r["after_in"][step, d].astype(F32)).astype(BF)
+                h_along(step, d).start()
+        h_beside(step, 0).wait_recv()
+        r["home"][0] = r["dkv"][at(0, c), :].astype(F32) + r["beside_in"][step, 0].astype(F32)
+
+        @pl.when(z < chips - 1)
+        def _():
+            h_along(step, 1).wait_recv()
+            r["home"][0] = r["home"][0] + r["after_in"][step, 0].astype(F32)
+
+        h_beside(step, 0).wait_send()
+        for d in range(1, back + 1):
+            @pl.when(z >= d)
+            def _():
+                h_beside(step, d).wait_send()
+                h_along(step, d).wait_send()
+
+    r["state"][0] = r["hidden_in"][...].astype(F32).T
+    met = False
+    for step in range(RECUR):
+        here = of_step(step)
+
+        def ready(step=step, first=step == 0):
+            if first:
+                pl.semaphore_wait(bar, 1 + (z < chips - 1).astype(jnp.int32) + (z > 0).astype(jnp.int32))
+            keys_start(step)
+
+        front_part(here, wait, here["state"][...], ready)
+        keys_end(step)
+        after = rest_part(here, wait)
+        keys_drain(step)
+        if step < RECUR - 1:
+            r["state"][step + 1] = after
+        else:
+            r["output"][...] = after.T.astype(BF)
+    grad = r["cot"][...].astype(F32).T
+    for step in reversed(range(RECUR)):
+        here = of_step(step)
+        back_part(here, wait, grad)
+        home_start(step)
+        home_end(step)
+        grad = home_part(here, wait)
+    r["grad"][...] = grad.T
+
+
+def all_recursions(hidden_in, cotangent, masks, lives, tables, gains, weights, n_tok, nback):
+    back = nback // 2
+    width, rows = hidden_in.shape
+    ff = weights["wg"].shape[1]
+    kvr = 2 * KVH * HD
+    slots = (2 * back + 2) * rows
+    ins = {"hidden_in": hidden_in, "cot": cotangent, "mask": masks, "live": lives, "cos": tables[0], "sin": tables[1], "gains": gains}
+    outs = {"output": shaped((width, rows), BF), "grad": shaped((width, rows), F32), "acc_out": shaped((8, 1024), F32)}
+    sizes = {"normed": width, "d_mlp": width, "mixed": H * HD, "normed_two": width, "hidden": ff, "d_gate": ff, "d_up": ff, "d_packed": QKO + kvr // 2}
+    for name, size in sizes.items():
+        for step in range(RECUR):
+            outs[name + str(step)] = shaped((rows, size), BF)
+    dma, vm = pltpu.SemaphoreType.DMA, pltpu.VMEM
+    scratch = {n + "_v": vm(weights[n].shape, BF) for n in WEIGHTS}
+    scratch |= {
+        "state": vm((RECUR, rows, width), F32), "middle": vm((RECUR, rows, width), F32), "branch": vm((RECUR, rows, width), F32),
+        "gate": vm((RECUR, rows, ff), F32), "up": vm((RECUR, rows, ff), F32), "lse": vm((RECUR, 8, (H // KVH) * rows), F32),
+        "q": vm((RECUR, rows, H * HD), BF), "kvw": vm((RECUR, slots, kvr), BF), "d_state": vm((rows, width), F32),
+        "d_q": vm((rows, H * HD), BF), "d_attn": vm((rows, width), BF), "dkv": vm((slots, kvr), BF), "home": vm((1, rows, kvr), F32),
+        "beside_in": vm((RECUR, back + 1, rows, kvr), BF), "after_in": vm((RECUR, back, rows, kvr), BF), "sums": vm((back, rows, kvr), BF),
+        "w_sem": dma((len(WEIGHTS),)), "k_s": dma((RECUR, back)), "k_r": dma((RECUR, back)), "kc_s": dma((RECUR, back + 1)),
+        "kc_r": dma((RECUR, back + 1)), "h_s": dma((RECUR, back)), "h_r": dma((RECUR, back)), "hc_s": dma((RECUR, back + 1)), "hc_r": dma((RECUR, back + 1)),
+    }
+    spec = pl.BlockSpec(memory_space=pltpu.VMEM)
+    got = pl.pallas_call(
+        lambda *refs: recursion_kernel(n_tok // 2, back, list(ins), list(outs), list(scratch), *refs),
+        name="all_recursions",
+        out_shape=tuple(outs.values()),
+        in_specs=[spec] * len(ins) + [pl.BlockSpec(memory_space=pl.ANY)] * len(WEIGHTS),
+        out_specs=tuple([spec] * len(outs)),
+        scratch_shapes=list(scratch.values()),
+        compiler_params=pltpu.CompilerParams(collective_id=5, has_side_effects=True, vmem_limit_bytes=62 * 2**20),
+    )(*ins.values(), *[weights[n] for n in WEIGHTS])
+    return dict(zip(outs, got))
 
 
 def forward_stage(state, q, kvw, mask, live, tables, gains, weights, last):
@@ -974,17 +1177,24 @@
 
     for t, side in steps:
         small_step(t, side)
-    for turn in range(4 + 2):
-        for t, side in steps:
-            if turn < 4:
-                each(0, turn, t, side)
-            if 1 <= turn < 5:
-                m = turn - 1
-                relay, leaf = (1, 2) if m % 2 == 0 else (2, 1)
-                each(relay, m, t, side)
-                each(leaf, m, t, side)
-            if turn >= 2:
-                each(3, turn - 2, t, side)
+    turns = [(t, m) for t in (1, 2, 3) for m in range(4)]
+    for i in range(len(turns) + 3):
+        if i < len(turns):
+            t, m = turns[i]
+            for side in (0, 1):
+                each(0, m, t, side)
+        if 0 <= i - 1 < len(turns):
+            t, m = turns[i - 1]
+            for side in (0, 1):
+                each(1 if m % 2 == 0 else 2, m, t, side)
+        if 0 <= i - 2 < len(turns):
+            t, m = turns[i - 2]
+            for side in (0, 1):
+                each(2 if m % 2 == 0 else 1, m, t, side)
+        if i - 3 >= 0:
+            t, m = turns[i - 3]
+            for side in (0, 1):
+                each(3, m, t, side)
 
     for cp, when in lasting:
         if not isinstance(cp, tuple):
@@ -1370,44 +1580,47 @@
     masks = jnp.where(reachable[None] & (live_keys[:, :, None] > 0), 1.0, 0.0).astype(F32)
     lives = [active[i].astype(F32)[:, None] for i in range(RECUR)]
 
-    kept = []
-    made = first_stage(hidden_in.T, tables, gains, weights)
-    state = made["state"]
-    for step in range(RECUR):
-        kvw = exchange_keys(made["kv"], n_tok, nback)
-        last = step == RECUR - 1
-        done = forward_stage(state, made["q"], kvw, masks[step], lives[step], tables, gains, weights, last)
-        kept.append({**done, "state": state, "q": made["q"], "kvw": kvw, "normed_r": made["normed"]})
-        made, state = done, done.get("next")
-
-    acc = jnp.zeros((8, 1024), F32)
-    before = None
-    rows_of = {name: [] for name in ROW_NAMES}
-    for step in reversed(range(RECUR)):
-        back = backward_stage(kept[step], before, masks[step], lives[step], tables, gains, acc, weights, cotangent.T)
+    if (n_grp, n_tok) == (4, 8):
+        done = all_recursions(hidden_in.T, cotangent.T, masks, jnp.stack(lives), tables, gains, weights, n_tok, nback)
+        lefts, rights = ([[done[name + str(step)] for step in reversed(range(RECUR))] for name in names] for names in (ROW_NAMES[:4], ROW_NAMES[4:]))
+        parts, acc = summed_gradients(lefts, rights, done["acc_out"])
+        output, grad = done["output"], done["grad"]
+    else:
+        kept = []
+        made = first_stage(hidden_in.T, tables, gains, weights)
+        state = made["state"]
+        for step in range(RECUR):
+            kvw = exchange_keys(made["kv"], n_tok, nback)
+            last = step == RECUR - 1
+            done = forward_stage(state, made["q"], kvw, masks[step], lives[step], tables, gains, weights, last)
+            kept.append({**done, "state": state, "q": made["q"], "kvw": kvw, "normed_r": made["normed"]})
+            made, state = done, done.get("next")
+
+        acc = jnp.zeros((8, 1024), F32)
+        before = None
+        rows_of = {name: [] for name in ROW_NAMES}
+        for step in reversed(range(RECUR)):
+            back = backward_stage(kept[step], before, masks[step], lives[step], tables, gains, acc, weights, cotangent.T)
+            acc = back["acc_out"]
+            if before is not None:
+                rows_of["d_packed"].append(back["d_packed"])
+            for name in ("d_mlp", "d_gate", "d_up"):
+                rows_of[name].append(back[name])
+            for name in ("normed_two", "mixed", "hidden"):
+                rows_of[name].append(kept[step][name])
+            rows_of["normed"].append(kept[step]["normed_r"])
+            before = {"home": exchange_home(back["dkv"], n_tok, nback), "d_q": back["d_q"], "state": kept[step]["state"], "d_state": back["d_state"], "d_attn": back["d_attn"]}
+        back = backward_stage(None, before, None, None, tables, gains, acc, weights, None)
+        rows_of["d_packed"].append(back["d_packed"])
         acc = back["acc_out"]
-        if before is not None:
-            rows_of["d_packed"].append(back["d_packed"])
-        for name in ("d_mlp", "d_gate", "d_up"):
-            rows_of[name].append(back[name])
-        for name in ("normed_two", "mixed", "hidden"):
-            rows_of[name].append(kept[step][name])
-        rows_of["normed"].append(kept[step]["normed_r"])
-        before = {"home": exchange_home(back["dkv"], n_tok, nback), "d_q": back["d_q"], "state": kept[step]["state"], "d_state": back["d_state"], "d_attn": back["d_attn"]}
-    back = backward_stage(None, before, None, None, tables, gains, acc, weights, None)
-    rows_of["d_packed"].append(back["d_packed"])
-    acc = back["acc_out"]
-    if (n_grp, n_tok) == (4, 8):
-        lefts, rights = ([rows_of[name] for name in names] for names in (ROW_NAMES[:4], ROW_NAMES[4:]))
-        parts, acc = summed_gradients(lefts, rights, acc)
-    else:
         parts = weight_gradients(rows_of)
         parts = lax.psum(parts.astype(F32), ("grp", "tok")).astype(BF)
         acc = lax.psum(acc, ("grp", "tok"))
+        output, grad = kept[-1]["output"], back["grad"]
     d_gate, d_up, d_down, d_q, d_k, d_v, d_o = spread_out(parts)
     return (
-        kept[-1]["output"].T,
-        back["grad"].T,
+        output.T,
+        grad.T,
         acc[0, :width],
         d_q,
         d_k.T,

time: 465 us -> 442 us (0.951)
  local copies, waits for them, and re-layouts: 23.2 us -> 9.36 us
  Pallas kernels: 429 us -> 419 us
    unnamed x64 -> x8, local copies, waits for them, and re-layouts: 17.7 us -> 3.48 us
    pallas_call x14 -> x1, Pallas kernels: 134 us -> 124 us  [all_recursions(): pl.pallas_call(lambda *refs: recursion_kernel(n_tok // 2, back, list(ins)...]
where the time goes in v6:
time: 442 us; the launch traced here: 437 us
  Pallas kernels  419 us (95%)
  local copies, waits for them, and re-layouts  9.36 us (2%)
  other arithmetic  7.85 us (2%)
    pallas_call x1, Pallas kernels, summed_gradients(): pl.pallas_call(lambda *refs: tail_kernel(count, *refs), name='summed_grad...  184 us
    pallas_call x1, Pallas kernels, all_recursions(): pl.pallas_call(lambda *refs: recursion_kernel(n_tok // 2, back, list(ins)...  124 us
    pallas_call x1, Pallas kernels, gather_rows(): pl.pallas_call(gather_kernel, name='gather_rows', out_shape=tuple((jax.Sh...  90.8 us
    pallas_call x1, Pallas kernels, spread_out(): pl.pallas_call(spread_kernel, name='spread_out', out_shape=tuple((jax.Sha...  20 us

profile of v6, /device:TPU:0, one launch (start us, length us, event | category | flops | bytes accessed | tf_op | source)
XLA Modules:
  0.0 436.7 jit_solution(13904236723143975936)
XLA Ops:
  0.6 0.8 select_reduce_fusion.1
  1.4 0.1 convert_reduce_fusion.1
  1.5 0.7 fusion.7
  2.2 0.1 select_reduce_fusion
  2.3 0.1 pad.31.clone
  2.4 0.7 fusion.6
  3.1 0.7 convert_element_type.70
  3.8 0.7 maximum_maximum_fusion.refs_4_
  4.4 0.8 convert_bitcast_fusion.2
  5.2 0.1 convert_reduce_fusion
  5.3 0.2 compare_and_fusion
  5.6 1.0 copy.40
  6.6 1.0 copy.41
  7.6 0.8 copy.44.refs_3_
  8.4 0.3 fusion
  8.7 0.8 pad_maximum_fusion
  9.5 2.0 concatenate.12.refs_0_
  11.5 90.8 %gather_rows.1 = (bf16[8,120,2560]{2,1,0:T(8,128)(2,1)}, bf16[8,120,2560]{2,1,0:T(8,128)(2,1)}, bf16[8,120,2560]{2,1,0:T(8,128)(2,1)}, bf16[8,320,960]{2,1,0:T(8,128)(2,1)}, bf16[8,16,128]{2,1,0:T(8,128)(2,1)}) custom-call(bf16[120,2560]{1,0:T(8,128)(2,1)} %concatenate.12.refs_0_, bf16[120,2560]{1,0:T(8,128)(2,1)} %refs_1_.1, bf16[120,2560]{1,0:T(8,128)(2,1)} %refs_2_.1, ...), custom_call_target="tpu_custom_call" | custom-call | tf_op jit(solution)/shard_map/gather_rows/pallas_call | solution.py:1256
  102.3 0.7 slice_bitcast_fusion
  103.0 0.7 slice_bitcast_fusion.1
  103.8 0.1 convert_element_type.79
  103.9 0.6 pad_convert_fusion.refs_6_
  104.5 1.3 and_select_fusion.refs_2_
  105.8 123.6 %all_recursions.1 = (bf16[960,128]{1,0:T(8,128)(2,1)}, f32[960,128]{1,0:T(8,128)}, f32[8,1024]{1,0:T(8,128)}, bf16[128,960]{1,0:T(8,128)(2,1)}, bf16[128,960]{1,...) custom-call(bf16[960,128]{1,0:T(8,128)(2,1)} %bitcast.42, ...), custom_call_target="tpu_custom_call" | custom-call | tf_op jit(solution)/shard_map/all_recursions/pallas_call | solution.py:467
  229.4 184.1 %summed_gradients.1 = (bf16[16,960,640]{2,1,0:T(8,128)(2,1)}, f32[8,1024]{1,0:T(8,128)}) custom-call(bf16[128,960]{1,0:T(8,128)(2,1)} %get-tuple-element.60.refs_0_, bf16[128,960]{1,0:T(8,128)(2,1)} %get-tuple-element.61.refs_1_, bf16[128,960]{1,0:T(8,128)(2,1)} %get-tuple-element.62.refs_2_, bf16[128,960]{1,0:T(8,128)(2,1)} %get-tuple-element.63.refs_3_, ...), custom_call_target="tpu_custom_call" | custom-call | tf_op jit(solution)/shard_map/summed_gradients/pallas_call | solution.py:1039
  413.5 1.5 fusion.8
  415.0 0.0 copy-start.1
  415.0 20.0 %spread_out.1 = (f32[960,2560]{1,0:T(8,128)}, f32[960,2560]{1,0:T(8,128)}, f32[960,2560]{1,0:T(8,128)}, f32[960,960]{1,0:T(8,128)}, f32[320,960]{1,0:T(8,128)}, /*index=5*/f32[320,960]{1,0:T(8,128)}, f32[960,960]{1,0:T(8,128)}) custom-call(bf16[16,960,640]{2,1,0:T(8,128)(2,1)} %get-tuple-element.86.p_ref), custom_call_target="tpu_custom_call" | custom-call | tf_op jit(solution)/shard_map/spread_out/pallas_call | solution.py:1520
  435.0 0.0 copy-done.1
  435.0 0.7 copy.47
  435.7 0.0 copy-done
  435.7 0.8 copy.48
  (9 shorter events, 0.1 us)
Async XLA Ops:
  415.0 20.0 %copy-start.1 = (bf16[960,128]{1,0:T(8,128)(2,1)S(1)}, bf16[960,128]{1,0:T(8,128)(2,1)}, u32[]{:S(2)}) copy-start(bf16[960,128]{1,0:T(8,128)(2,1)} %get-tuple-element.58) | copy-start | bytes 737284
  415.0 20.7 %copy-start = (f32[960,128]{1,0:T(8,128)S(1)}, f32[960,128]{1,0:T(8,128)}, u32[]{:S(2)}) copy-start(f32[960,128]{1,0:T(8,128)} %get-tuple-element.59) | copy-start | bytes 1474564

commit v7 on v6

--- a/solution.py
+++ b/solution.py
@@ -552,8 +552,26 @@
 HALF = 480
 COLS = 640
 STREAMS = (
-    ("x", True, 0, 80, 0), ("y", True, 80, 80, 0), ("x", False, 160, 48, 0), ("y", False, 208, 32, 0),
-    ("x", True, 240, 80, 1), ("y", True, 320, 80, 1), ("x", False, 400, 32, 1), ("y", False, 432, 48, 1),
+    ("x", True, 0, 80, 0),
+    ("y", True, 80, 80, 0),
+    ("x", True, 160, 80, 1),
+    ("y", True, 240, 80, 1),
+    ("x", True, 320, 80, 2),
+    ("y", True, 400, 80, 2),
+)
+SCHEDULE = (
+    (0, 0), (0, 1), (1, 0, 0), (0, 2), (1, 1, 0), (8, 0), (0, 3), (0, 4), (0, 5), (0, 6), (1, 5, 0), (1, 4, 0), (1, 2, 0), (0, 7),
+    (1, 3, 0), (8, 1), (2, 0, 0), (0, 8), (0, 9), (1, 2, 1), (1, 8, 0), (1, 6, 0), (1, 7, 0), (2, 1, 0), (0, 10), (0, 11), (1, 10, 0),
+    (8, 2), (2, 0, 1), (1, 1, 1), (0, 12), (0, 13), (1, 7, 1), (1, 9, 0), (1, 12, 0), (0, 14), (2, 1, 1), (1, 0, 1), (0, 15), (1, 11, 0),
+    (0, 16), (8, 3), (1, 15, 0), (2, 0, 2), (1, 13, 0), (1, 14, 0), (2, 1, 2), (8, 4), (1, 11, 2), (1, 4, 1), (1, 3, 1), (1, 5, 1),
+    (1, 6, 1), (2, 0, 3), (1, 8, 1), (2, 1, 3), (1, 10, 1), (2, 3, 0), (1, 9, 1), (2, 2, 0), (3, 0), (2, 3, 1), (3, 1), (1, 12, 1),
+    (1, 14, 1), (4, 0), (1, 13, 1), (4, 1), (1, 15, 1), (1, 11, 1), (1, 4, 2), (2, 2, 1), (5, 1), (1, 1, 2), (2, 3, 2), (1, 6, 2),
+    (6, 0, 1), (1, 0, 2), (2, 2, 2), (6, 1, 1), (1, 3, 2), (2, 3, 3), (1, 2, 2), (6, 0, 2), (1, 5, 2), (2, 2, 3), (6, 1, 2), (3, 2),
+    (2, 5, 0), (3, 3), (1, 7, 2), (1, 9, 2), (7, 0, 1), (2, 4, 0), (6, 0, 3), (6, 1, 3), (2, 5, 1), (7, 1, 1), (1, 14, 2), (4, 2),
+    (1, 13, 2), (1, 10, 2), (4, 3), (2, 4, 1), (7, 1, 3), (7, 1, 2), (6, 3, 1), (1, 8, 2), (5, 0), (1, 15, 2), (7, 0, 2), (6, 2, 1),
+    (2, 4, 2), (1, 12, 2), (6, 2, 2), (2, 5, 2), (5, 3), (2, 4, 3), (6, 3, 2), (2, 5, 3), (3, 4), (6, 3, 3), (3, 5), (7, 3, 3), (7, 3, 1),
+    (7, 0, 3), (4, 4), (4, 5), (6, 2, 3), (6, 4, 1), (6, 5, 1), (7, 5, 1), (6, 4, 2), (7, 4, 1), (7, 2, 3), (7, 2, 1), (5, 2), (7, 4, 2),
+    (6, 5, 2), (6, 4, 3), (5, 5), (7, 5, 2), (7, 2, 2), (5, 4), (7, 3, 2), (6, 5, 3), (7, 4, 3), (7, 5, 3),
 )
 SLOTS = 4
 
@@ -760,8 +778,8 @@
     def of_batch(batch):
         return [s for s in range(n_s) if STREAMS[s][4] == batch]
 
-    def first_step(batch, k):
-        for s in of_batch(batch):
+    def first_step(only, k):
+        for s in (only,):
             _, b, _, _ = ab(s)
             a_step(s, 1 - b, k)
             if STREAMS[s][1]:
@@ -833,8 +851,8 @@
             def _():
                 to_z(s, pb, pz, src, False).start()
 
-    def finish(batch):
-        for s in of_batch(batch):
+    def finish(only):
+        for s in (only,):
             a, b, _, _ = ab(s)
             p = part_of(s, a, b, z)
             b_step(s, z)
@@ -879,12 +897,12 @@
         copy_to(src, src, oa.at[s, pb * 4 + pz], oar.at[s, pb * 4 + pz], partner).wait_recv()
         to_core(s, p, src).start()
 
-    def gather_b(batch):
-        for s in of_batch(batch):
+    def gather_b(only):
+        for s in (only,):
             got_b(s, z)
 
-    def gather_a(batch):
-        for s in of_batch(batch):
+    def gather_a(only):
+        for s in (only,):
             _, b, _, _ = ab(s)
             got_a(s, b, z)
             got_a(s, 1 - b, z)
@@ -892,99 +910,43 @@
     def from_side(t, side):
         return (z - t, z >= t) if side == 0 else (z + t, z + t <= 3)
 
-    def gather_z(batch, t):
+    def gather_z(only, t):
         for side in (0, 1):
             pz, there = from_side(t, side)
 
             @pl.when(there)
             def _():
-                for s in of_batch(batch):
-                    _, b, _, _ = ab(s)
-                    got_z(s, b, pz, side == 0)
-                    if STREAMS[s][1]:
-                        got_z(s, 1 - b, pz, side == 0)
-
-    def gather_rest(batch, t):
+                _, b, _, _ = ab(only)
+                got_z(only, b, pz, side == 0)
+                got_z(only, 1 - b, pz, side == 0)
+
+    def gather_rest(only, t):
         for side in (0, 1):
             pz, there = from_side(t, side)
 
             @pl.when(there)
             def _():
-                for s in of_batch(batch):
-                    if not STREAMS[s][1]:
-                        got_b(s, pz)
-                for s in of_batch(batch):
-                    _, b, _, _ = ab(s)
-                    got_a(s, b, pz)
-                    got_a(s, 1 - b, pz)
+                _, b, _, _ = ab(only)
+                got_a(only, b, pz)
+                got_a(only, 1 - b, pz)
+
+    def make(j):
+        if j < PARTS:
+            core_make(j)
+        if j > 0:
+            core_add(j - 1)
+
+    def vec_end_start(i):
+        vec_end(i)
+        if i < 4:
+            vec_copy(i + 1).start()
 
     vo_ref[...] = v_ref[...]
     vec_copy(0).start()
 
-    def group(k, batches=(0,)):
-        for i in range(4):
-            j = k * 4 + i
-            core_make(j)
-            if j > 0:
-                core_add(j - 1)
-                a_send(j - 1, 0)
-        if k == 3:
-            core_add(15)
-            a_send(15, 0)
-
-    group(0)
-    vec_end(0)
-    vec_copy(1).start()
-    group(1)
-    vec_end(1)
-    vec_copy(2).start()
-    first_step(0, 0)
-    group(2)
-    vec_end(2)
-    vec_copy(3).start()
-    second_step(0, 0)
-    first_step(0, 1)
-    group(3)
-    vec_end(3)
-    vec_copy(4).start()
-    second_step(0, 1)
-    for j in range(0, 4):
-        a_send(j, 1)
-    first_step(0, 2)
-    vec_end(4)
-    second_step(0, 2)
-    for j in range(4, 8):
-        a_send(j, 1)
-    first_step(0, 3)
-    first_step(1, 0)
-    finish(0)
-    for j in range(8, 12):
-        a_send(j, 1)
-    second_step(1, 0)
-    gather_b(0)
-    first_step(1, 1)
-    second_step(1, 1)
-    gather_z(0, 1)
-    for j in range(12, 16):
-        a_send(j, 1)
-    gather_a(0)
-    first_step(1, 2)
-    second_step(1, 2)
-    gather_z(0, 2)
-    gather_rest(0, 1)
-    first_step(1, 3)
-    finish(1)
-    gather_z(0, 3)
-    gather_rest(0, 2)
-    gather_b(1)
-    gather_z(1, 1)
-    gather_rest(0, 3)
-    gather_a(1)
-    gather_z(1, 2)
-    gather_rest(1, 1)
-    gather_z(1, 3)
-    gather_rest(1, 2)
-    gather_rest(1, 3)
+    actions = (make, a_send, first_step, finish, gather_b, gather_a, gather_z, gather_rest, vec_end_start)
+    for kind, *which in SCHEDULE:
+        actions[kind](*which)
 
     for cp in waits:
         cp.wait_send()
@@ -1059,11 +1021,17 @@
 
 
 QUARTERS = 4
+UNITS = ((0, 0, 1536, True, True), (0, 1536, 1024, False, True), (1, 0, 2560, True, False), (2, 0, 2560, True, True), (3, 0, 320, True, False))
+FIRST = (0, 2, 3, 4, 1)
+SMALL_AT = (5, 10, 15)
 
 
 def gather_kernel(*refs):
-    ins, outs = refs[:5], refs[5:10]
-    zs, xs, ys, cs, got, cgot, own_s, own_c, own_r, ss, sr, sc, scr = refs[10:]
+    q_ref, k_ref, o_ref, v_ref = refs[:4]
+    ins, outs, packed = (refs[17], *refs[4:8]), refs[8:13], refs[17]
+    turned = [each[...].astype(F32).T.astype(BF) for each in (k_ref, v_ref)]
+    packed[...] = jnp.concatenate([q_ref[...], turned[0], o_ref[...], turned[1]], axis=1)
+    zs, xs, ys, cs, got, cgot, own_s, own_c, own_r, ss, sr, sc, scr = (*refs[13:17], *refs[18:])
     y, x, z, c = place()
     partner, to_x, to_y = dev(y, x, z, 1 - c), dev(y, 1 - x, z, c), dev(1 - y, x, z, c)
     left, right = dev(y, x, z - 1, c), dev(y, x, z + 1, c)
@@ -1079,15 +1047,16 @@
                 cp.start()
         lasting.append((cp, when))
 
-    def cut(ref, m, q):
+    def cut(ref, u, q):
+        m, first, size, shared, _ = UNITS[u]
+        n = size // QUARTERS if shared else size
+        begin = first + q * n if shared else first
         if m < 3:
-            n = ref.shape[1] // QUARTERS
-            return ref.at[:, pl.ds(pl.multiple_of(q * n, 128), n)]
-        n = ref.shape[0] // QUARTERS
-        return ref.at[pl.ds(pl.multiple_of(q * n, 16), n), :]
-
-    def out_piece(m, kind, zz, core):
-        return cut(outs[m].at[zz * 2 + core], m, quarter[kind])
+            return ref.at[:, pl.ds(pl.multiple_of(begin, 128), n)]
+        return ref.at[pl.ds(pl.multiple_of(begin, 16), n), :]
+
+    def out_piece(u, kind, zz, core):
+        return cut(outs[UNITS[u][0]].at[zz * 2 + core], u, quarter[kind])
 
     bar = pltpu.get_barrier_semaphore()
     for d in (partner, to_x, to_y):
@@ -1109,10 +1078,10 @@
     go(small_copy(z, c, ins[4], right, (ss.at[z, 0], sr.at[z])), z < 3)
     go(small_copy(z, c, ins[4], left, (ss.at[z, 1], sr.at[z])), z > 0)
     go(small_copy(z, c, ins[4], partner, (sc.at[z], scr.at[z])))
-    for m in range(4):
-        src, dst = cut(ins[m], m, quarter[0]), out_piece(m, 0, z, c)
-        go(copy_to(src, dst, zs.at[m, z, 0], got.at[0, m, z], right), z < 3)
-        go(copy_to(src, dst, zs.at[m, z, 1], got.at[0, m, z], left), z > 0)
+    for u in FIRST:
+        src, dst = cut(ins[UNITS[u][0]], u, quarter[0]), out_piece(u, 0, z, c)
+        go(copy_to(src, dst, zs.at[u, z, 0], got.at[0, u, z], right), z < 3)
+        go(copy_to(src, dst, zs.at[u, z, 1], got.at[0, u, z], left), z > 0)
     for m in range(4):
         go(copy_to(ins[m], outs[m].at[z * 2 + c], own_c.at[m], own_r.at[m], partner))
     local = [pltpu.make_async_copy(ins[m], outs[m].at[z * 2 + c], own_s.at[m]) for m in range(5)]
@@ -1124,40 +1093,43 @@
     def source(t, side):
         return (z - t, z >= t) if side == 0 else (z + t, z + t <= 3)
 
-    def wait_for(kind, m, zz):
-        piece = out_piece(m, kind, zz, c)
-        copy_to(piece, piece, cs.at[kind, m, zz], got.at[kind, m, zz], partner).wait_recv()
+    def wait_for(kind, u, zz):
+        piece = out_piece(u, kind, zz, c)
+        copy_to(piece, piece, cs.at[kind, u, zz], got.at[kind, u, zz], partner).wait_recv()
         return piece
 
-    def each(kind, m, t, side):
+    def sends(kind, u, zz, piece):
+        shared, first_x = UNITS[u][3], UNITS[u][4]
+        out = []
+        if shared and (kind == 0 or (kind == 2 and not first_x)):
+            out.append(copy_to(piece, piece, xs.at[min(kind, 1), u, zz], got.at[1 if kind == 0 else 3, u, zz], to_x))
+        if shared and (kind == 0 or (kind == 1 and first_x)):
+            out.append(copy_to(piece, piece, ys.at[min(kind, 1), u, zz], got.at[2 if kind == 0 else 3, u, zz], to_y))
+        out.append(copy_to(piece, piece, cs.at[kind, u, zz], cgot.at[kind, u, zz], partner))
+        return out
+
+    def each(kind, u, t, side):
+        if kind and not UNITS[u][3]:
+            return
         zz, there = source(t, side)
         onward = (z < 3) if side == 0 else (z > 0)
 
         @pl.when(there)
         def _():
-            piece = wait_for(kind, m, zz)
-            first_x = m % 2 == 0
-            sends = []
+            piece = wait_for(kind, u, zz)
             if kind == 0:
-                on = copy_to(piece, piece, zs.at[m, zz, side], got.at[0, m, zz], right if side == 0 else left)
+                on = copy_to(piece, piece, zs.at[u, zz, side], got.at[0, u, zz], right if side == 0 else left)
 
                 @pl.when(onward)
                 def _():
                     on.start()
 
-                sends.append(copy_to(piece, piece, xs.at[0, m, zz], got.at[1, m, zz], to_x))
-                sends.append(copy_to(piece, piece, ys.at[0, m, zz], got.at[2, m, zz], to_y))
-            elif kind == 1 and first_x:
-                sends.append(copy_to(piece, piece, ys.at[1, m, zz], got.at[3, m, zz], to_y))
-            elif kind == 2 and not first_x:
-                sends.append(copy_to(piece, piece, xs.at[1, m, zz], got.at[3, m, zz], to_x))
-            sends.append(copy_to(piece, piece, cs.at[kind, m, zz], cgot.at[kind, m, zz], partner))
-            for cp in sends:
+            for cp in sends(kind, u, zz, piece):
                 cp.start()
 
-        lasting.append((("s", kind, m, t, side), there))
+        lasting.append((("s", kind, u, t, side), there))
         if kind == 0:
-            lasting.append((("z", m, t, side), there & onward))
+            lasting.append((("z", u, t, side), there & onward))
 
     def small_step(t, side):
         zz, there = source(t, side)
@@ -1175,26 +1147,27 @@
 
         lasting.append((("m", t, side), there))
 
-    for t, side in steps:
-        small_step(t, side)
-    turns = [(t, m) for t in (1, 2, 3) for m in range(4)]
+    turns = [(t, u) for t in (1, 2, 3) for u in FIRST]
     for i in range(len(turns) + 3):
         if i < len(turns):
-            t, m = turns[i]
+            t, u = turns[i]
             for side in (0, 1):
-                each(0, m, t, side)
+                each(0, u, t, side)
         if 0 <= i - 1 < len(turns):
-            t, m = turns[i - 1]
+            t, u = turns[i - 1]
             for side in (0, 1):
-                each(1 if m % 2 == 0 else 2, m, t, side)
+                each(1 if UNITS[u][4] else 2, u, t, side)
         if 0 <= i - 2 < len(turns):
-            t, m = turns[i - 2]
+            t, u = turns[i - 2]
             for side in (0, 1):
-                each(2 if m % 2 == 0 else 1, m, t, side)
+                each(2 if UNITS[u][4] else 1, u, t, side)
         if i - 3 >= 0:
-            t, m = turns[i - 3]
+            t, u = turns[i - 3]
             for side in (0, 1):
-                each(3, m, t, side)
+                each(3, u, t, side)
+        if i in SMALL_AT:
+            for side in (0, 1):
+                small_step(SMALL_AT.index(i) + 1, side)
 
     for cp, when in lasting:
         if not isinstance(cp, tuple):
@@ -1205,13 +1178,13 @@
                 def _():
                     cp.wait_send()
         elif cp[0] == "z":
-            _, m, t, side = cp
+            _, u, t, side = cp
             zz, _ = source(t, side)
-            piece = out_piece(m, 0, zz, c)
+            piece = out_piece(u, 0, zz, c)
 
             @pl.when(when)
             def _():
-                copy_to(piece, piece, zs.at[m, zz, side], got.at[0, m, zz], partner).wait_send()
+                copy_to(piece, piece, zs.at[u, zz, side], got.at[0, u, zz], partner).wait_send()
         elif cp[0] == "m":
             _, t, side = cp
             zz, _ = source(t, side)
@@ -1227,20 +1200,16 @@
                 other = outs[4].at[zz * 2 + 1 - c]
                 copy_to(other, other, sc.at[zz], scr.at[zz], partner).wait_recv()
         else:
-            _, kind, m, t, side = cp
+            _, kind, u, t, side = cp
             zz, _ = source(t, side)
-            piece = out_piece(m, kind, zz, c)
-            other = out_piece(m, kind, zz, 1 - c)
-            first_x = m % 2 == 0
+            piece = out_piece(u, kind, zz, c)
+            other = out_piece(u, kind, zz, 1 - c)
 
             @pl.when(when)
             def _():
-                if kind == 0 or (kind == 2 and not first_x):
-                    copy_to(piece, piece, xs.at[min(kind, 1), m, zz], got.at[1, m, zz], partner).wait_send()
-                if kind == 0 or (kind == 1 and first_x):
-                    copy_to(piece, piece, ys.at[min(kind, 1), m, zz], got.at[1, m, zz], partner).wait_send()
-                copy_to(piece, piece, cs.at[kind, m, zz], cgot.at[kind, m, zz], partner).wait_send()
-                copy_to(other, other, cs.at[kind, m, zz], cgot.at[kind, m, zz], partner).wait_recv()
+                for cp in sends(kind, u, zz, piece):
+                    cp.wait_send()
+                copy_to(other, other, cs.at[kind, u, zz], cgot.at[kind, u, zz], partner).wait_recv()
 
     for m in range(4):
         other = outs[m].at[z * 2 + 1 - c]
@@ -1251,20 +1220,24 @@
         cp.wait()
 
 
-def gather_rows(shards):
+def gather_rows(w_query, w_key_t, w_out, w_value_t, others):
     dma = pltpu.SemaphoreType.DMA
+    rows, width = w_query.shape
+    packed = (rows, 2 * (width + w_key_t.shape[0]))
+    shapes = [packed] + [each.shape for each in others]
+    n = len(UNITS)
     return pl.pallas_call(
         gather_kernel,
         name="gather_rows",
-        out_shape=tuple(jax.ShapeDtypeStruct((8, *s.shape), s.dtype) for s in shards),
-        in_specs=[pl.BlockSpec(memory_space=pl.ANY)] * 5,
+        out_shape=tuple(jax.ShapeDtypeStruct((8, *each), BF) for each in shapes),
+        in_specs=[pl.BlockSpec(memory_space=pltpu.VMEM)] * 4 + [pl.BlockSpec(memory_space=pl.ANY)] * 4,
         out_specs=tuple([pl.BlockSpec(memory_space=pl.ANY)] * 5),
         scratch_shapes=[
-            dma((4, 4, 2)), dma((2, 4, 4)), dma((2, 4, 4)), dma((4, 4, 4)), dma((4, 4, 4)), dma((4, 4, 4)),
+            dma((n, 4, 2)), dma((2, n, 4)), dma((2, n, 4)), dma((4, n, 4)), pltpu.VMEM(packed, BF), dma((4, n, 4)), dma((4, n, 4)),
             dma((5,)), dma((4,)), dma((4,)), dma((4, 2)), dma((4,)), dma((4,)), dma((4,)),
         ],
         compiler_params=pltpu.CompilerParams(collective_id=4, has_side_effects=True),
-    )(*shards)
+    )(w_query, w_key_t, w_out, w_value_t, *others)
 
 
 def keys_kernel(chips, back, kv_ref, w_ref, s_right, r_left, s_core, r_core):
@@ -1557,8 +1530,12 @@
     share = norm_attn.shape[0]
     vectors = jnp.pad(jnp.stack([norm_attn, norm_mlp, w_router]), ((0, 0), (0, 128 - share)))
     small = jnp.concatenate([vectors, active.astype(BF), jnp.zeros((10, 128), BF)], axis=0)
-    shards = (jnp.concatenate([w_query, w_key, w_out, w_value], axis=1), w_gate, w_up, w_down, small)
-    whole = gather_rows(shards) if (n_grp, n_tok) == (4, 8) else [lax.all_gather(each, "tok", axis=0) for each in shards]
+    others = (w_gate, w_up, w_down, small)
+    if (n_grp, n_tok) == (4, 8):
+        whole = gather_rows(w_query, w_key.T, w_out, w_value.T, others)
+    else:
+        packed = jnp.concatenate([w_query, w_key, w_out, w_value], axis=1)
+        whole = [lax.all_gather(each, "tok", axis=0) for each in (packed, *others)]
     weights = {name: each.reshape(-1, each.shape[-1]) for name, each in zip(WEIGHTS, whole)}
     gains = jnp.transpose(whole[4][:, :3, :share], (1, 0, 2)).reshape(3, width).astype(F32)
     gains = jnp.pad(gains, ((0, 5), (0, 0)))

time: 442 us -> 414 us (0.937)
  Pallas kernels: 419 us -> 394 us
    pallas_call x1, Pallas kernels: 90.8 us -> 76.3 us  [gather_rows(): pl.pallas_call(gather_kernel, name='gather_rows', out_shape=tuple((jax.Sh...]
    pallas_call x1, Pallas kernels: 184 us -> 174 us  [summed_gradients(): pl.pallas_call(lambda *refs: tail_kernel(count, *refs), name='summed_grad...]
where the time goes in v7:
time: 414 us; the launch traced here: 408 us
  Pallas kernels  394 us (95%)
  other arithmetic  7.85 us (2%)
  local copies, waits for them, and re-layouts  5.41 us (1%)
    pallas_call x1, Pallas kernels, summed_gradients(): pl.pallas_call(lambda *refs: tail_kernel(count, *refs), name='summed_grad...  174 us
    pallas_call x1, Pallas kernels, all_recursions(): pl.pallas_call(lambda *refs: recursion_kernel(n_tok // 2, back, list(ins)...  124 us
    pallas_call x1, Pallas kernels, gather_rows(): pl.pallas_call(gather_kernel, name='gather_rows', out_shape=tuple((jax.Sh...  76.3 us
    pallas_call x1, Pallas kernels, spread_out(): pl.pallas_call(spread_kernel, name='spread_out', out_shape=tuple((jax.Sha...  20 us

profile of v7, /device:TPU:0, one launch (start us, length us, event | category | flops | bytes accessed | tf_op | source)
XLA Modules:
  0.0 408.5 jit_solution(16686742212243161387)
XLA Ops:
  0.6 0.8 select_reduce_fusion.1
  1.4 0.1 convert_reduce_fusion.1
  1.5 0.7 fusion.7
  2.2 0.1 select_reduce_fusion
  2.3 0.1 pad.31.clone
  2.4 0.7 fusion.6
  3.1 0.7 convert_element_type.70
  3.8 0.7 maximum_maximum_fusion.refs_7_
  4.4 0.8 convert_bitcast_fusion.2
  5.2 0.1 convert_reduce_fusion
  5.3 0.2 compare_and_fusion
  5.6 0.8 copy.36.refs_3_
  6.4 0.3 fusion
  6.7 0.8 pad_maximum_fusion
  7.5 76.3 %gather_rows.1 = (bf16[8,120,2560]{2,1,0:T(8,128)(2,1)}, bf16[8,120,2560]{2,1,0:T(8,128)(2,1)}, bf16[8,120,2560]{2,1,0:T(8,128)(2,1)}, bf16[8,320,960]{2,1,0:T(8,128)(2,1)}, bf16[8,16,128]{2,1,0:T(8,128)(2,1)}) custom-call(bf16[120,960]{1,0:T(8,128)(2,1)} %refs_0_.1, bf16[320,120]{1,0:T(8,128)(2,1)} %bitcast.46, bf16[120,960]{1,0:T(8,128)(2,1)} %refs_2_.1, ...), custom_call_target="tpu_custom_call" | custom-call | tf_op jit(solution)/shard_map/gather_rows/pallas_call | solution.py:1229
  83.8 0.7 slice_bitcast_fusion
  84.6 0.7 slice_bitcast_fusion.1
  85.3 0.1 convert_element_type.79
  85.4 0.6 pad_convert_fusion.refs_6_
  86.0 1.3 and_select_fusion.refs_2_
  87.3 123.6 %all_recursions.1 = (bf16[960,128]{1,0:T(8,128)(2,1)}, f32[960,128]{1,0:T(8,128)}, f32[8,1024]{1,0:T(8,128)}, bf16[128,960]{1,0:T(8,128)(2,1)}, bf16[128,960]{1,...) custom-call(bf16[960,128]{1,0:T(8,128)(2,1)} %bitcast.44, ...), custom_call_target="tpu_custom_call" | custom-call | tf_op jit(solution)/shard_map/all_recursions/pallas_call | solution.py:467
  210.9 174.4 %summed_gradients.1 = (bf16[16,960,640]{2,1,0:T(8,128)(2,1)}, f32[8,1024]{1,0:T(8,128)}) custom-call(bf16[128,960]{1,0:T(8,128)(2,1)} %get-tuple-element.60.refs_0_, bf16[128,960]{1,0:T(8,128)(2,1)} %get-tuple-element.61.refs_1_, bf16[128,960]{1,0:T(8,128)(2,1)} %get-tuple-element.62.refs_2_, bf16[128,960]{1,0:T(8,128)(2,1)} %get-tuple-element.63.refs_3_, ...), custom_call_target="tpu_custom_call" | custom-call | tf_op jit(solution)/shard_map/summed_gradients/pallas_call | solution.py:1001
  385.3 1.5 fusion.8
  386.8 0.0 copy-start.1
  386.8 0.0 copy-start
  386.8 20.0 %spread_out.1 = (f32[960,2560]{1,0:T(8,128)}, f32[960,2560]{1,0:T(8,128)}, f32[960,2560]{1,0:T(8,128)}, f32[960,960]{1,0:T(8,128)}, f32[320,960]{1,0:T(8,128)}, /*index=5*/f32[320,960]{1,0:T(8,128)}, f32[960,960]{1,0:T(8,128)}) custom-call(bf16[16,960,640]{2,1,0:T(8,128)(2,1)} %get-tuple-element.86.p_ref), custom_call_target="tpu_custom_call" | custom-call | tf_op jit(solution)/shard_map/spread_out/pallas_call | solution.py:1493
  406.8 0.0 copy-done.1
  406.8 0.7 copy.39
  407.5 0.0 copy-done
  407.5 0.8 copy.40
  (8 shorter events, 0.1 us)
Async XLA Ops:
  386.8 20.0 %copy-start.1 = (bf16[960,128]{1,0:T(8,128)(2,1)S(1)}, bf16[960,128]{1,0:T(8,128)(2,1)}, u32[]{:S(2)}) copy-start(bf16[960,128]{1,0:T(8,128)(2,1)} %get-tuple-element.58) | copy-start | bytes 737284
  386.8 20.7 %copy-start = (f32[960,128]{1,0:T(8,128)S(1)}, f32[960,128]{1,0:T(8,128)}, u32[]{:S(2)}) copy-start(f32[960,128]{1,0:T(8,128)} %get-tuple-element.59) | copy-start | bytes 1474564

commit v8 on v7

--- a/solution.py
+++ b/solution.py
@@ -45,6 +45,7 @@
 F32 = jnp.float32
 BF = jnp.bfloat16
 CHUNK = 512
+ROW_NAMES = ("normed_two", "d_mlp", "normed", "mixed", "d_gate", "d_up", "hidden", "d_packed")
 WEIGHTS = ("wa", "wg", "wu", "wd")
 QK = (H + KVH) * HD
 QKO = QK + H * HD
@@ -83,7 +84,8 @@
     qw = H * HD
     even = qw // (2 * HD) * (2 * HD)
     tail = rope_lanes(dot_nn(normed, r["wa_v"][:, even:QK]), r["cos"][...], r["sin"][...], 1.0).astype(BF)
-    r["kv"][...] = jnp.concatenate([tail[:, qw - even :], values], axis=1)
+    keys = tail[:, qw - even :]
+    r["kv"][...] = jnp.concatenate([each[:, g * HD : (g + 1) * HD] for g in range(KVH) for each in (keys, values)], axis=1)
     if ready is not None:
         ready()
     queries = rope_lanes(dot_nn(normed, r["wa_v"][:, :even]), r["cos"][...], r["sin"][...], 1.0).astype(BF)
@@ -95,37 +97,36 @@
     return jnp.concatenate([tensor[:, (g * per + i) * HD : (g * per + i + 1) * HD] for i in range(per)], axis=0)
 
 
-def window(r):
-    rows = r["mask"].shape[0]
+def key_rows(r):
     start = lax.rem(lax.axis_index("tok"), 2) * r["q_in"].shape[0]
-    return r["kvw"][pl.ds(pl.multiple_of(start, 128), rows), :]
-
-
-def attention_part(r):
+    return pl.ds(pl.multiple_of(start, 128), r["mask"].shape[0])
+
+
+def attention_part(r, arrived=None):
     per = H // KVH
-    kv = window(r)
     q = r["q_in"][...]
     rows = q.shape[0]
     allowed = jnp.concatenate([r["mask"][...]] * per, axis=1) > 0
     mixed_t, logs = [], []
     for g in range(KVH):
-        k_g = kv[:, g * HD : (g + 1) * HD]
-        v_g = kv[:, (KVH + g) * HD : (KVH + g + 1) * HD]
-        scores = jnp.where(allowed, dot_nt(k_g, head_rows(q, g)) * HD**-0.5, masked)
+        if arrived is not None:
+            arrived(g)
+        kv = r["kvw"][key_rows(r), 2 * g * HD : 2 * (g + 1) * HD]
+        scores = jnp.where(allowed, dot_nt(kv[:, :HD], head_rows(q, g)) * HD**-0.5, masked)
         largest = jnp.max(scores, axis=0, keepdims=True)
         exponent = jnp.exp(scores - largest)
         total = jnp.sum(exponent, axis=0, keepdims=True)
         probs = (exponent * (1.0 / total)).astype(BF)
-        mix = dot_nn(v_g.T, probs)
+        mix = dot_nn(kv[:, HD:].T, probs)
         mixed_t += [mix[:, i * rows : (i + 1) * rows] for i in range(per)]
         logs.append(largest + jnp.log(total))
     r["lse"][...] = jnp.concatenate(logs + [logs[0]] * (r["lse"].shape[0] - KVH), axis=0)
     return jnp.concatenate(mixed_t, axis=0).T.astype(BF)
 
 
-def rest_part(r, wait):
+def rest_part(r, wait, arrived=None):
     state = r["state"][...]
-    mixed = attention_part(r)
+    mixed = attention_part(r, arrived)
     r["mixed"][...] = mixed
     wait("wa")
     attn_out = dot_nn(mixed, r["wa_v"][:, QK:QKO])
@@ -161,7 +162,7 @@
     return inverse * (weighted - scaled * inner), jnp.sum(grad * scaled, axis=0, keepdims=True)
 
 
-def back_part(r, wait, grad_after):
+def back_part(r, wait, grad_after, made=None):
     state, live = r["b_state"][...], r["b_live"][:, 0:1]
     width = state.shape[1]
     router_vec = r["gains"][2:3, :]
@@ -197,42 +198,41 @@
     d_mixed = dot_nt(d_attn, r["wa_v"][:, QK:QKO]).astype(BF)
 
     per = H // KVH
-    kv = window(r)
     q = r["q_in"][...]
     rows = q.shape[0]
     allowed = jnp.concatenate([r["mask"][...]] * per, axis=1) > 0
-    d_keys, d_values, dq_t = [], [], []
+    partial, reach = r["dkv"], r["mask"].shape[0]
+    keep = partial.shape[0] - reach
+    unused = (1 - lax.rem(lax.axis_index("tok"), 2)) * reach
+    partial[pl.ds(pl.multiple_of(unused, 128), keep), :] = jnp.zeros((keep, partial.shape[1]), BF)
+    dq_t = []
     for g in range(KVH):
-        k_g = kv[:, g * HD : (g + 1) * HD]
-        v_g = kv[:, (KVH + g) * HD : (KVH + g + 1) * HD]
+        lanes = slice(2 * g * HD, 2 * (g + 1) * HD)
+        kv = r["kvw"][key_rows(r), lanes]
+        k_g, v_g = kv[:, :HD], kv[:, HD:]
         q_g, do_g = head_rows(q, g), head_rows(d_mixed, g)
         scores = jnp.where(allowed, dot_nt(k_g, q_g) * HD**-0.5, masked)
         probs = jnp.exp(scores - r["b_lse"][g : g + 1, :])
-        d_values.append(dot_nn(probs.astype(BF), do_g))
+        d_values = dot_nn(probs.astype(BF), do_g)
         d_probs = dot_nt(v_g, do_g)
         d_scores = (probs * (d_probs - jnp.sum(probs * d_probs, axis=0, keepdims=True))).astype(BF)
-        d_keys.append(dot_nn(d_scores, q_g) * HD**-0.5)
+        d_keys = dot_nn(d_scores, q_g) * HD**-0.5
+        partial[key_rows(r), lanes] = jnp.concatenate([d_keys, d_values], axis=1).astype(BF)
         dq = dot_nn(k_g.T, d_scores) * HD**-0.5
         dq_t += [dq[:, i * rows : (i + 1) * rows] for i in range(per)]
+        if made is not None:
+            made(g)
     d_queries = jnp.concatenate(dq_t + [jnp.zeros((HD, rows), F32)], axis=0).T
     d_queries = rope_lanes(d_queries, r["cos"][...], r["sin"][...], -1.0)
     r["d_q"][...] = d_queries[:, : H * HD].astype(BF)
-    start = lax.rem(lax.axis_index("tok"), 2) * rows
-    partial = r["dkv"]
-    keep = partial.shape[0] - kv.shape[0]
-    partial[pl.ds(pl.multiple_of((1 - lax.rem(lax.axis_index("tok"), 2)) * kv.shape[0], 128), keep), :] = jnp.zeros((keep, kv.shape[1]), BF)
-    partial[pl.ds(pl.multiple_of(start, 128), kv.shape[0]), :] = jnp.concatenate(d_keys + d_values, axis=1).astype(BF)
 
 
 def home_part(r, wait):
-    half = KVH * HD
-    total = r["home"][0].astype(F32)
-    for i in range(1, r["home"].shape[0]):
-        total = total + r["home"][i].astype(F32)
-    rows = total.shape[0]
-    padded = jnp.concatenate([total[:, :half], jnp.zeros((rows, half % (2 * HD)), F32)], axis=1)
-    d_keys = rope_lanes(padded, r["cos"][...], r["sin"][...], -1.0)[:, :half].astype(BF)
-    d_values = total[:, half:].astype(BF)
+    total = r["home"][0]
+    turned = rope_lanes(total, r["cos"][...], r["sin"][...], -1.0).astype(BF)
+    low = total.astype(BF)
+    d_keys = jnp.concatenate([turned[:, 2 * g * HD : (2 * g + 1) * HD] for g in range(KVH)], axis=1)
+    d_values = jnp.concatenate([low[:, (2 * g + 1) * HD : 2 * (g + 1) * HD] for g in range(KVH)], axis=1)
     wait("wa")
     packed = jnp.concatenate([r["h_dq"][...], d_keys, r["h_d_attn"][...], d_values], axis=1)
     r["d_packed"][...] = packed
@@ -277,6 +277,10 @@
     return {"normed": shaped((rows, width), BF), "q": shaped((rows, H * HD), BF), "kv": shaped((rows, 2 * KVH * HD), BF)}
 
 
+FIRST_HEADS = (KVH + 1) // 2
+PIECES = ((0, 2 * HD * FIRST_HEADS), (2 * HD * FIRST_HEADS, 2 * HD * (KVH - FIRST_HEADS)))
+
+
 def recursion_kernel(chips, back, in_names, out_names, scratch_names, *refs):
     names = in_names + list(WEIGHTS) + out_names + scratch_names
     r = dict(zip(names, refs, strict=True))
@@ -320,8 +324,8 @@
     def of_step(step):
         every = {n: r[n] for n in ("gains", "cos", "sin", "acc_out", "d_state", "d_q", "d_attn", "dkv", "home")}
         every |= {n + "_v": r[n + "_v"] for n in WEIGHTS}
-        for n in ("normed", "mixed", "normed_two", "hidden", "d_mlp", "d_gate", "d_up", "d_packed"):
-            every[n] = r[n + str(step)]
+        every |= {n: r[n] for n in ROW_NAMES[:4]}
+        every |= {n: r[n + str(step)] for n in ROW_NAMES[4:]}
         for n in ("q", "kvw", "mask", "live", "state", "lse", "middle", "branch", "gate", "up"):
             every[n] = r[n].at[step]
         every |= {"q_in": every["q"], "kv": r["kvw"].at[step, at(0, c)], "acc": r["acc_out"]}
@@ -329,88 +333,126 @@
         every |= {"h_dq": r["d_q"], "h_state": every["state"], "h_d_state": r["d_state"], "h_d_attn": r["d_attn"]}
         return every
 
-    def k_along(step, d):
-        here = r["kvw"].at[step, at(d - 1, c)]
-        return copy_to(here, r["kvw"].at[step, at(d, c)], r["k_s"].at[step, d - 1], r["k_r"].at[step, d - 1], right)
-
-    def k_beside(step, d):
-        here = r["kvw"].at[step, at(d, c)]
-        return copy_to(here, here, r["kc_s"].at[step, d], r["kc_r"].at[step, d], partner)
+    def k_along(step, d, j):
+        src, dst = (r["kvw"].at[step, at(e, c), pl.ds(*PIECES[j])] for e in (d - 1, d))
+        return copy_to(src, dst, r["k_s"].at[step, j, d - 1], r["k_r"].at[step, j, d - 1], right)
+
+    def k_beside(step, d, j):
+        here = r["kvw"].at[step, at(d, c), pl.ds(*PIECES[j])]
+        return copy_to(here, here, r["kc_s"].at[step, j, d], r["kc_r"].at[step, j, d], partner)
 
     def keys_start(step):
+        for j in (0, 1):
+            @pl.when(z < chips - 1)
+            def _():
+                k_along(step, 1, j).start()
+
+            k_beside(step, 0, j).start()
+
+    def keys_pass(step, d, j):
+        @pl.when(z >= d)
+        def _():
+            k_along(step, d, j).wait_recv()
+            if d < back:
+                @pl.when(z < chips - 1)
+                def _():
+                    k_along(step, d + 1, j).start()
+            k_beside(step, d, j).start()
+
+    def keys_end(step, j):
+        k_beside(step, 0, j).wait_recv()
+        for d in range(1, back + 1):
+            @pl.when(z >= d)
+            def _():
+                k_beside(step, d, j).wait_recv()
+
+    def keys_arrived(step, g):
+        if g == 0:
+            for d in range(1, back):
+                keys_pass(step, d, 0)
+                keys_pass(step, d, 1)
+            keys_pass(step, back, 0)
+            keys_end(step, 0)
+        if g == FIRST_HEADS:
+            keys_pass(step, back, 1)
+            keys_end(step, 1)
+
+    def keys_drain(step):
+        for j in (0, 1):
+            k_beside(step, 0, j).wait_send()
+            for d in range(1, back + 1):
+                @pl.when(z >= d)
+                def _():
+                    k_beside(step, d, j).wait_send()
+
+                @pl.when((z >= d - 1) & (z < chips - 1))
+                def _():
+                    k_along(step, d, j).wait_send()
+
+    def h_beside(step, d, j):
+        piece = pl.ds(*PIECES[j])
+        return copy_to(r["dkv"].at[at(d, 1 - c), piece], r["beside_in"].at[step, d, :, piece], r["hc_s"].at[step, j, d], r["hc_r"].at[step, j, d], partner)
+
+    def h_along(step, d, j):
+        piece = pl.ds(*PIECES[j])
+        return copy_to(r["sums"].at[d - 1, :, piece], r["after_in"].at[step, d - 1, :, piece], r["h_s"].at[step, j, d - 1], r["h_r"].at[step, j, d - 1], left)
+
+    def home_start(step, j):
+        for d in range(back, 0, -1):
+            @pl.when(z >= d)
+            def _():
+                h_beside(step, d, j).start()
+        h_beside(step, 0, j).start()
+
+    def home_pass(step, d, j):
+        lanes = slice(PIECES[j][0], sum(PIECES[j]))
+
+        @pl.when(z >= d)
+        def _():
+            h_beside(step, d, j).wait_recv()
+            total = r["dkv"][at(d, c), lanes].astype(F32) + r["beside_in"][step, d, :, lanes].astype(F32)
+            r["sums"][d - 1, :, lanes] = total.astype(BF)
+            if d < back:
+                @pl.when(z < chips - 1)
+                def _():
+                    h_along(step, d + 1, j).wait_recv()
+                    more = r["sums"][d - 1, :, lanes].astype(F32) + r["after_in"][step, d, :, lanes].astype(F32)
+                    r["sums"][d - 1, :, lanes] = more.astype(BF)
+            h_along(step, d, j).start()
+
+    def home_made(step, g):
+        if g == FIRST_HEADS - 1:
+            home_start(step, 0)
+        if g == FIRST_HEADS:
+            home_pass(step, back, 0)
+        if g == KVH - 1:
+            home_start(step, 1)
+
+    def home_end(step):
+        home_pass(step, back, 1)
+        for d in range(back - 1, 0, -1):
+            for j in (0, 1):
+                home_pass(step, d, j)
+        for j in (0, 1):
+            h_beside(step, 0, j).wait_recv()
+        r["home"][0] = r["dkv"][at(0, c), :].astype(F32) + r["beside_in"][step, 0].astype(F32)
+
         @pl.when(z < chips - 1)
         def _():
-            k_along(step, 1).start()
-
-        k_beside(step, 0).start()
-
-    def keys_end(step):
-        for d in range(1, back + 1):
-            @pl.when(z >= d)
-            def _():
-                k_along(step, d).wait_recv()
-                if d < back:
-                    @pl.when(z < chips - 1)
-                    def _():
-                        k_along(step, d + 1).start()
-                k_beside(step, d).start()
-
-        k_beside(step, 0).wait_recv()
-        for d in range(1, back + 1):
-            @pl.when(z >= d)
-            def _():
-                k_beside(step, d).wait_recv()
-
-    def keys_drain(step):
-        k_beside(step, 0).wait_send()
-        for d in range(1, back + 1):
-            @pl.when(z >= d)
-            def _():
-                k_beside(step, d).wait_send()
-
-            @pl.when((z >= d - 1) & (z < chips - 1))
-            def _():
-                k_along(step, d).wait_send()
-
-    def h_beside(step, d):
-        return copy_to(r["dkv"].at[at(d, 1 - c)], r["beside_in"].at[step, d], r["hc_s"].at[step, d], r["hc_r"].at[step, d], partner)
-
-    def h_along(step, d):
-        return copy_to(r["sums"].at[d - 1], r["after_in"].at[step, d - 1], r["h_s"].at[step, d - 1], r["h_r"].at[step, d - 1], left)
-
-    def home_start(step):
-        for d in range(back, 0, -1):
-            @pl.when(z >= d)
-            def _():
-                h_beside(step, d).start()
-        h_beside(step, 0).start()
-
-    def home_end(step):
-        for d in range(back, 0, -1):
-            @pl.when(z >= d)
-            def _():
-                h_beside(step, d).wait_recv()
-                r["sums"][d - 1] = (r["dkv"][at(d, c), :].astype(F32) + r["beside_in"][step, d].astype(F32)).astype(BF)
-                if d < back:
-                    @pl.when(z < chips - 1)
-                    def _():
-                        h_along(step, d + 1).wait_recv()
-                        r["sums"][d - 1] = (r["sums"][d - 1].astype(F32) + r["after_in"][step, d].astype(F32)).astype(BF)
-                h_along(step, d).start()
-        h_beside(step, 0).wait_recv()
-        r["home"][0] = r["dkv"][at(0, c), :].astype(F32) + r["beside_in"][step, 0].astype(F32)
-
-        @pl.when(z < chips - 1)
-        def _():
-            h_along(step, 1).wait_recv()
+            for j in (0, 1):
+                h_along(step, 1, j).wait_recv()
             r["home"][0] = r["home"][0] + r["after_in"][step, 0].astype(F32)
 
-        h_beside(step, 0).wait_send()
-        for d in range(1, back + 1):
-            @pl.when(z >= d)
-            def _():
-                h_beside(step, d).wait_send()
-                h_along(step, d).wait_send()
+        for j in (0, 1):
+            h_beside(step, 0, j).wait_send()
+            for d in range(1, back + 1):
+                @pl.when(z >= d)
+                def _():
+                    h_beside(step, d, j).wait_send()
+                    h_along(step, d, j).wait_send()
+
+    def turn(name, step):
+        r[name + "_t" + str(step)][...] = r[name][...].astype(F32).T.astype(BF)
 
     r["state"][0] = r["hidden_in"][...].astype(F32).T
     met = False
@@ -423,8 +465,11 @@
             keys_start(step)
 
         front_part(here, wait, here["state"][...], ready)
-        keys_end(step)
-        after = rest_part(here, wait)
+        turn("normed", step)
+        if step > 0:
+            turn("mixed", step - 1)
+            turn("normed_two", step - 1)
+        after = rest_part(here, wait, lambda g, step=step: keys_arrived(step, g))
         keys_drain(step)
         if step < RECUR - 1:
             r["state"][step + 1] = after
@@ -433,8 +478,11 @@
     grad = r["cot"][...].astype(F32).T
     for step in reversed(range(RECUR)):
         here = of_step(step)
-        back_part(here, wait, grad)
-        home_start(step)
+        back_part(here, wait, grad, lambda g, step=step: home_made(step, g))
+        turn("d_mlp", step)
+        if step == RECUR - 1:
+            turn("mixed", step)
+            turn("normed_two", step)
         home_end(step)
         grad = home_part(here, wait)
     r["grad"][...] = grad.T
@@ -448,10 +496,9 @@
     slots = (2 * back + 2) * rows
     ins = {"hidden_in": hidden_in, "cot": cotangent, "mask": masks, "live": lives, "cos": tables[0], "sin": tables[1], "gains": gains}
     outs = {"output": shaped((width, rows), BF), "grad": shaped((width, rows), F32), "acc_out": shaped((8, 1024), F32)}
-    sizes = {"normed": width, "d_mlp": width, "mixed": H * HD, "normed_two": width, "hidden": ff, "d_gate": ff, "d_up": ff, "d_packed": QKO + kvr // 2}
-    for name, size in sizes.items():
-        for step in range(RECUR):
-            outs[name + str(step)] = shaped((rows, size), BF)
+    for step in range(RECUR):
+        outs |= {name + "_t" + str(step): shaped((width, rows), BF) for name in ROW_NAMES[:4]}
+        outs |= {name + str(step): shaped((rows, ff), BF) for name in ROW_NAMES[4:]}
     dma, vm = pltpu.SemaphoreType.DMA, pltpu.VMEM
     scratch = {n + "_v": vm(weights[n].shape, BF) for n in WEIGHTS}
     scratch |= {
@@ -460,9 +507,11 @@
         "q": vm((RECUR, rows, H * HD), BF), "kvw": vm((RECUR, slots, kvr), BF), "d_state": vm((rows, width), F32),
         "d_q": vm((rows, H * HD), BF), "d_attn": vm((rows, width), BF), "dkv": vm((slots, kvr), BF), "home": vm((1, rows, kvr), F32),
         "beside_in": vm((RECUR, back + 1, rows, kvr), BF), "after_in": vm((RECUR, back, rows, kvr), BF), "sums": vm((back, rows, kvr), BF),
-        "w_sem": dma((len(WEIGHTS),)), "k_s": dma((RECUR, back)), "k_r": dma((RECUR, back)), "kc_s": dma((RECUR, back + 1)),
-        "kc_r": dma((RECUR, back + 1)), "h_s": dma((RECUR, back)), "h_r": dma((RECUR, back)), "hc_s": dma((RECUR, back + 1)), "hc_r": dma((RECUR, back + 1)),
+        "w_sem": dma((len(WEIGHTS),)),
     }
+    scratch |= {name: vm((rows, width), BF) for name in ROW_NAMES[:4]}
+    scratch |= {name: dma((RECUR, 2, back)) for name in ("k_s", "k_r", "h_s", "h_r")}
+    scratch |= {name: dma((RECUR, 2, back + 1)) for name in ("kc_s", "kc_r", "hc_s", "hc_r")}
     spec = pl.BlockSpec(memory_space=pltpu.VMEM)
     got = pl.pallas_call(
         lambda *refs: recursion_kernel(n_tok // 2, back, list(ins), list(outs), list(scratch), *refs),
@@ -611,7 +660,7 @@
     n_s = len(STREAMS)
     v_ref, o_ref, vo_ref, left_t, right, theirs, mine, other = refs[:8]
     ra, rz, rb = refs[8 : 8 + n_s], refs[8 + n_s : 8 + 2 * n_s], refs[8 + 2 * n_s : 8 + 3 * n_s]
-    vrecv, load_sem, core_s, core_r, as_, ar, zs, zr, bs, br, ob, obr, oz, ozr, oa, oar, oc, ocr, vs, vr, own_sem = refs[8 + 3 * n_s :]
+    vrecv, left_sem, load_sem, core_s, core_r, as_, ar, zs, zr, bs, br, ob, obr, oz, ozr, oa, oar, oc, ocr, vs, vr, own_sem = refs[8 + 3 * n_s :]
     y, x, z, c = place()
     partner = dev(y, x, z, 1 - c)
     across = {"x": dev(y, 1 - x, z, c), "y": dev(1 - y, x, z, c)}
@@ -619,15 +668,19 @@
     at_axis = {"x": x, "y": y}
     order = (pick(z, (3, 3, 0, 0)), pick(z, (2, 0, 3, 1)), pick(z, (1, 2, 1, 2)), z)
     far = dev(y, x, jnp.where(z < 2, z + 2, z - 2), c)
-    tokens = left_refs[0].shape[0]
-
-    loads = []
-    for p in range(PARTS):
-        for i in range(count):
-            src = right_refs[(p // 4) * count + i].at[:, pl.ds((p % 4) * COLS, COLS)]
-            loads.append(pltpu.make_async_copy(src, right.at[p, pl.ds(i * tokens, tokens)], load_sem.at[p * count + i]))
-    for cp in loads:
-        cp.start()
+    tokens = left_refs[0].shape[1]
+    lefts = [pltpu.make_async_copy(each, left_t.at[i // count, :, pl.ds(i % count * tokens, tokens)], left_sem.at[i]) for i, each in enumerate(left_refs)]
+
+    def load(p, src, i):
+        return pltpu.make_async_copy(src, right.at[p, pl.ds(i * tokens, tokens)], load_sem.at[p * count + i])
+
+    for k in range(4):
+        for j in range(4):
+            for i in range(count):
+                if k == 0:
+                    lefts[j * count + i].start()
+                columns = pl.ds(pl.multiple_of(order[k] * COLS, COLS), COLS)
+                load(j * 4 + order[k], right_refs[j * count + i].at[:, columns], i).start()
 
     bar = pltpu.get_barrier_semaphore()
     for d in (partner, across["x"], across["y"], far):
@@ -641,9 +694,7 @@
     def _():
         pl.semaphore_signal(bar, inc=1, device_id=right_dev, device_id_type=MESH)
 
-    for j in range(4):
-        left_t[j] = jnp.concatenate([each[...].astype(F32).T.astype(BF) for each in left_refs[j * count : (j + 1) * count]], axis=1)
-    for cp in loads:
+    for cp in lefts:
         cp.wait()
     pl.semaphore_wait(bar, 4 + (z > 0).astype(jnp.int32) + (z < 3).astype(jnp.int32))
 
@@ -669,6 +720,8 @@
     def core_make(j):
         k, _, px, py = seq[j]
         p = part_xy(px, py, order[k])
+        for i in range(count):
+            load(p, right_refs[0].at[:, pl.ds(0, COLS)], i).wait()
         if j >= SLOTS:
             core_copy(j - SLOTS).wait_send()
         which = jnp.where(p < 8, 0, jnp.where(p < 12, 1, jnp.where(p < 14, 2, 3)))
@@ -994,7 +1047,7 @@
 def summed_gradients(lefts, rights, vectors):
     dma = pltpu.SemaphoreType.DMA
     count = len(lefts[0])
-    tokens, width = lefts[0][0].shape
+    width, tokens = lefts[0][0].shape
     rows = count * tokens
     n_s = len(STREAMS)
     vm = pl.BlockSpec(memory_space=pltpu.VMEM)
@@ -1002,7 +1055,7 @@
         lambda *refs: tail_kernel(count, *refs),
         name="summed_gradients",
         out_shape=(jax.ShapeDtypeStruct((PARTS, width, COLS), BF), jax.ShapeDtypeStruct(vectors.shape, F32)),
-        in_specs=[vm] * (4 * count) + [pl.BlockSpec(memory_space=pl.ANY)] * (4 * count) + [vm],
+        in_specs=[pl.BlockSpec(memory_space=pl.ANY)] * (8 * count) + [vm],
         out_specs=(pl.BlockSpec(memory_space=pl.ANY), vm),
         scratch_shapes=[
             pltpu.VMEM((4, width, rows), BF), pltpu.VMEM((PARTS, rows, COLS), BF), pltpu.VMEM((SLOTS, 2 * HALF, COLS), BF),
@@ -1011,7 +1064,7 @@
             *[pltpu.VMEM((10 if s[1] else 5, s[3], COLS), BF) for s in STREAMS],
             *[pltpu.VMEM((1 if s[1] else 4, s[3], COLS), BF) for s in STREAMS],
             pltpu.VMEM((5, *vectors.shape), F32),
-            dma((PARTS * count,)), dma((16,)), dma((16,)),
+            dma((4 * count,)), dma((PARTS * count,)), dma((16,)), dma((16,)),
             dma((n_s, 8)), dma((n_s, 8)), dma((n_s, 10)), dma((n_s, 10)), dma((n_s, 4)), dma((n_s, 4)),
             dma((n_s, 4)), dma((n_s, 4)), dma((n_s, 16)), dma((n_s, 8)), dma((n_s, 8)), dma((n_s, 8)), dma((n_s, 16)), dma((n_s, 16)),
             dma((5,)), dma((5,)), dma((n_s,)),
@@ -1396,9 +1449,6 @@
         ],
         compiler_params=pltpu.CompilerParams(collective_id=3, has_side_effects=True, vmem_limit_bytes=12 * 2**20),
     )(partial)
-
-
-ROW_NAMES = ("normed_two", "d_mlp", "normed", "mixed", "d_gate", "d_up", "hidden", "d_packed")
 
 
 def grads_kernel(count, *refs):
@@ -1559,7 +1609,9 @@
 
     if (n_grp, n_tok) == (4, 8):
         done = all_recursions(hidden_in.T, cotangent.T, masks, jnp.stack(lives), tables, gains, weights, n_tok, nback)
-        lefts, rights = ([[done[name + str(step)] for step in reversed(range(RECUR))] for name in names] for names in (ROW_NAMES[:4], ROW_NAMES[4:]))
+        names = [name + "_t" for name in ROW_NAMES[:4]] + list(ROW_NAMES[4:])
+        rows_of = [[done[name + str(step)] for step in reversed(range(RECUR))] for name in names]
+        lefts, rights = rows_of[:4], rows_of[4:]
         parts, acc = summed_gradients(lefts, rights, done["acc_out"])
         output, grad = done["output"], done["grad"]
     else:

time: 414 us -> 407 us (0.983)
  Pallas kernels: 394 us -> 387 us
    pallas_call x1, Pallas kernels: 124 us -> 116 us  [all_recursions(): pl.pallas_call(lambda *refs: recursion_kernel(n_tok // 2, back, list(ins)...]
where the time goes in v8:
time: 407 us; the launch traced here: 401 us
  Pallas kernels  387 us (95%)
  other arithmetic  7.85 us (2%)
  local copies, waits for them, and re-layouts  5.41 us (1%)
    pallas_call x1, Pallas kernels, summed_gradients(): pl.pallas_call(lambda *refs: tail_kernel(count, *refs), name='summed_grad...  175 us
    pallas_call x1, Pallas kernels, all_recursions(): pl.pallas_call(lambda *refs: recursion_kernel(n_tok // 2, back, list(ins)...  116 us
    pallas_call x1, Pallas kernels, gather_rows(): pl.pallas_call(gather_kernel, name='gather_rows', out_shape=tuple((jax.Sh...  76.3 us
    pallas_call x1, Pallas kernels, spread_out(): pl.pallas_call(spread_kernel, name='spread_out', out_shape=tuple((jax.Sha...  20 us

profile of v8, /device:TPU:0, one launch (start us, length us, event | category | flops | bytes accessed | tf_op | source)
XLA Modules:
  0.0 401.3 jit_solution(17487893239047432378)
XLA Ops:
  0.6 0.8 select_reduce_fusion.1
  1.4 0.1 convert_reduce_fusion.1
  1.5 0.7 fusion.7
  2.2 0.1 select_reduce_fusion
  2.3 0.1 pad.31.clone
  2.4 0.7 fusion.6
  3.1 0.7 convert_element_type.70
  3.8 0.7 maximum_maximum_fusion.refs_7_
  4.4 0.8 convert_bitcast_fusion.2
  5.2 0.1 convert_reduce_fusion
  5.3 0.2 compare_and_fusion
  5.6 0.8 copy.36.refs_3_
  6.4 0.3 fusion
  6.7 0.8 pad_maximum_fusion
  7.5 76.3 %gather_rows.1 = (bf16[8,120,2560]{2,1,0:T(8,128)(2,1)}, bf16[8,120,2560]{2,1,0:T(8,128)(2,1)}, bf16[8,120,2560]{2,1,0:T(8,128)(2,1)}, bf16[8,320,960]{2,1,0:T(8,128)(2,1)}, bf16[8,16,128]{2,1,0:T(8,128)(2,1)}) custom-call(bf16[120,960]{1,0:T(8,128)(2,1)} %refs_0_.1, bf16[320,120]{1,0:T(8,128)(2,1)} %bitcast.46, bf16[120,960]{1,0:T(8,128)(2,1)} %refs_2_.1, ...), custom_call_target="tpu_custom_call" | custom-call | tf_op jit(solution)/shard_map/gather_rows/pallas_call | solution.py:1282
  83.8 0.7 slice_bitcast_fusion
  84.6 0.7 slice_bitcast_fusion.1
  85.3 0.1 convert_element_type.79
  85.4 0.6 pad_convert_fusion.refs_6_
  86.0 1.3 and_select_fusion.refs_2_
  87.3 116.2 %all_recursions.1 = (bf16[960,128]{1,0:T(8,128)(2,1)}, f32[960,128]{1,0:T(8,128)}, f32[8,1024]{1,0:T(8,128)}, bf16[960,128]{1,0:T(8,128)(2,1)}, bf16[960,128]{1,...) custom-call(bf16[960,128]{1,0:T(8,128)(2,1)} %bitcast.44, ...), custom_call_target="tpu_custom_call" | custom-call | tf_op jit(solution)/shard_map/all_recursions/pallas_call | solution.py:516
  203.5 174.5 %summed_gradients.1 = (bf16[16,960,640]{2,1,0:T(8,128)(2,1)}, f32[8,1024]{1,0:T(8,128)}) custom-call(bf16[960,128]{1,0:T(8,128)(2,1)} %get-tuple-element.60.refs_0_, bf16[960,128]{1,0:T(8,128)(2,1)} %get-tuple-element.61.refs_1_, bf16[960,128]{1,0:T(8,128)(2,1)} %get-tuple-element.62.refs_2_, bf16[960,128]{1,0:T(8,128)(2,1)} %get-tuple-element.63.refs_3_, ...), custom_call_target="tpu_custom_call" | custom-call | tf_op jit(solution)/shard_map/summed_gradients/pallas_call | solution.py:1054
  378.0 1.5 fusion.8
  379.5 0.0 copy-start.1
  379.5 0.0 copy-start
  379.5 20.0 %spread_out.1 = (f32[960,2560]{1,0:T(8,128)}, f32[960,2560]{1,0:T(8,128)}, f32[960,2560]{1,0:T(8,128)}, f32[960,960]{1,0:T(8,128)}, f32[320,960]{1,0:T(8,128)}, /*index=5*/f32[320,960]{1,0:T(8,128)}, f32[960,960]{1,0:T(8,128)}) custom-call(bf16[16,960,640]{2,1,0:T(8,128)(2,1)} %get-tuple-element.86.p_ref), custom_call_target="tpu_custom_call" | custom-call | tf_op jit(solution)/shard_map/spread_out/pallas_call | solution.py:1543
  399.5 0.0 copy-done.1
  399.5 0.7 copy.39
  400.2 0.0 copy-done
  400.2 0.8 copy.40
  (8 shorter events, 0.1 us)
Async XLA Ops:
  379.5 20.0 %copy-start.1 = (bf16[960,128]{1,0:T(8,128)(2,1)S(1)}, bf16[960,128]{1,0:T(8,128)(2,1)}, u32[]{:S(2)}) copy-start(bf16[960,128]{1,0:T(8,128)(2,1)} %get-tuple-element.58) | copy-start | bytes 737284
  379.5 20.7 %copy-start = (f32[960,128]{1,0:T(8,128)S(1)}, f32[960,128]{1,0:T(8,128)}, u32[]{:S(2)}) copy-start(f32[960,128]{1,0:T(8,128)} %get-tuple-element.59) | copy-start | bytes 1474564

commit v9 on v8

--- a/solution.py
+++ b/solution.py
@@ -1490,7 +1490,7 @@
     )(*flat)
 
 
-def spread_kernel(p_ref, gate, up, down, d_q, d_k, d_v, d_o, came, wide, q_full, k_full, o_full, v_full, sem_in, sem_out, sem_full):
+def spread_kernel(p_ref, out_in, grad_in, acc_in, gate, up, down, d_q, d_k, d_v, d_o, out_ref, grad_ref, one, two, three, came, wide, q_full, k_full, o_full, v_full, sem_in, sem_out, sem_full):
     width = q_full.shape[0]
     order = [12, 13, 14, 15] + list(range(12))
 
@@ -1508,6 +1508,10 @@
 
     fetch(0).start()
     fetch(1).start()
+    out_ref[...] = out_in[...]
+    grad_ref[...] = grad_in[...]
+    for i, each in enumerate((one, two, three)):
+        each[...] = acc_in[i, :width]
     for i, p in enumerate(order):
         if i + 2 < len(order):
             fetch(i + 2).start()
@@ -1534,7 +1538,7 @@
         put_full(j).wait()
 
 
-def spread_out(parts):
+def spread_out(parts, output, grad, acc):
     n, width, cols = parts.shape
     kv = 2 * cols - width
     ff = 4 * cols
@@ -1543,16 +1547,16 @@
     return pl.pallas_call(
         spread_kernel,
         name="spread_out",
-        out_shape=tuple(jax.ShapeDtypeStruct(s, F32) for s in shapes),
-        in_specs=[pl.BlockSpec(memory_space=pl.ANY)],
-        out_specs=tuple([pl.BlockSpec(memory_space=pl.ANY)] * 7),
+        out_shape=tuple(shaped(s, F32) for s in shapes) + (shaped(output.shape, BF), shaped(grad.shape, F32)) + (shaped((width,), F32),) * 3,
+        in_specs=[pl.BlockSpec(memory_space=pl.ANY)] + [pl.BlockSpec(memory_space=vm)] * 3,
+        out_specs=tuple([pl.BlockSpec(memory_space=pl.ANY)] * 7 + [pl.BlockSpec(memory_space=vm)] * 5),
         scratch_shapes=[
             vm((3, width, cols), BF), vm((2, width, cols), F32),
             vm((width, width), F32), vm((kv, width), F32), vm((width, width), F32), vm((kv, width), F32),
             pltpu.SemaphoreType.DMA((3,)), pltpu.SemaphoreType.DMA((2,)), pltpu.SemaphoreType.DMA((4,)),
         ],
         compiler_params=pltpu.CompilerParams(vmem_limit_bytes=60 * 2**20),
-    )(parts)
+    )(parts, output, grad, acc)
 
 
 def on_device(
@@ -1646,20 +1650,20 @@
         parts = lax.psum(parts.astype(F32), ("grp", "tok")).astype(BF)
         acc = lax.psum(acc, ("grp", "tok"))
         output, grad = kept[-1]["output"], back["grad"]
-    d_gate, d_up, d_down, d_q, d_k, d_v, d_o = spread_out(parts)
+    d_gate, d_up, d_down, d_q, d_k, d_v, d_o, output, grad, *small_grads = spread_out(parts, output, grad, acc)
     return (
         output.T,
         grad.T,
-        acc[0, :width],
+        small_grads[0],
         d_q,
         d_k.T,
         d_v.T,
         d_o,
-        acc[1, :width],
+        small_grads[1],
         d_gate,
         d_up,
         d_down.T,
-        acc[2, :width],
+        small_grads[2],
     )
 
 

time: 407 us -> 406 us (level)
  no operation moved by 1% of the time
where the time goes in v9:
time: 406 us; the launch traced here: 400 us
  Pallas kernels  389 us (96%)
  other arithmetic  7.85 us (2%)
    pallas_call x1, Pallas kernels, summed_gradients(): pl.pallas_call(lambda *refs: tail_kernel(count, *refs), name='summed_grad...  175 us
    pallas_call x1, Pallas kernels, all_recursions(): pl.pallas_call(lambda *refs: recursion_kernel(n_tok // 2, back, list(ins)...  116 us
    pallas_call x1, Pallas kernels, gather_rows(): pl.pallas_call(gather_kernel, name='gather_rows', out_shape=tuple((jax.Sh...  76.3 us
    pallas_call x1, Pallas kernels, spread_out(): pl.pallas_call(spread_kernel, name='spread_out', out_shape=tuple((shaped(...  21.9 us

profile of v9, /device:TPU:0, one launch (start us, length us, event | category | flops | bytes accessed | tf_op | source)
XLA Modules:
  0.0 400.2 jit_solution(7618460329210686606)
XLA Ops:
  0.6 0.8 select_reduce_fusion.1
  1.4 0.1 convert_reduce_fusion.1
  1.5 0.7 fusion.7
  2.2 0.1 select_reduce_fusion
  2.3 0.1 pad.31.clone
  2.4 0.7 fusion.6
  3.1 0.7 convert_element_type.70
  3.8 0.7 maximum_maximum_fusion.refs_7_
  4.4 0.8 convert_bitcast_fusion.2
  5.2 0.1 convert_reduce_fusion
  5.3 0.2 compare_and_fusion
  5.6 0.8 copy.36.refs_3_
  6.4 0.3 fusion
  6.7 0.8 pad_maximum_fusion
  7.5 76.3 %gather_rows.1 = (bf16[8,120,2560]{2,1,0:T(8,128)(2,1)}, bf16[8,120,2560]{2,1,0:T(8,128)(2,1)}, bf16[8,120,2560]{2,1,0:T(8,128)(2,1)}, bf16[8,320,960]{2,1,0:T(8,128)(2,1)}, bf16[8,16,128]{2,1,0:T(8,128)(2,1)}) custom-call(bf16[120,960]{1,0:T(8,128)(2,1)} %refs_0_.1, bf16[320,120]{1,0:T(8,128)(2,1)} %bitcast.41, bf16[120,960]{1,0:T(8,128)(2,1)} %refs_2_.1, ...), custom_call_target="tpu_custom_call" | custom-call | tf_op jit(solution)/shard_map/gather_rows/pallas_call | solution.py:1282
  83.8 0.7 slice_bitcast_fusion
  84.6 0.7 slice_bitcast_fusion.1
  85.3 0.1 convert_element_type.79
  85.4 0.6 pad_convert_fusion.refs_6_
  86.0 1.3 and_select_fusion.refs_2_
  87.3 116.2 %all_recursions.1 = (bf16[960,128]{1,0:T(8,128)(2,1)}, f32[960,128]{1,0:T(8,128)}, f32[8,1024]{1,0:T(8,128)}, bf16[960,128]{1,0:T(8,128)(2,1)}, bf16[960,128]{1,...) custom-call(bf16[960,128]{1,0:T(8,128)(2,1)} %bitcast.39, ...), custom_call_target="tpu_custom_call" | custom-call | tf_op jit(solution)/shard_map/all_recursions/pallas_call | solution.py:516
  203.5 174.5 %summed_gradients.1 = (bf16[16,960,640]{2,1,0:T(8,128)(2,1)}, f32[8,1024]{1,0:T(8,128)}) custom-call(bf16[960,128]{1,0:T(8,128)(2,1)} %get-tuple-element.63.refs_0_, bf16[960,128]{1,0:T(8,128)(2,1)} %get-tuple-element.64.refs_1_, bf16[960,128]{1,0:T(8,128)(2,1)} %get-tuple-element.65.refs_2_, bf16[960,128]{1,0:T(8,128)(2,1)} %get-tuple-element.66.refs_3_, ...), custom_call_target="tpu_custom_call" | custom-call | tf_op jit(solution)/shard_map/summed_gradients/pallas_call | solution.py:1054
  378.0 21.9 %spread_out.1 = (f32[960,2560]{1,0:T(8,128)}, f32[960,2560]{1,0:T(8,128)}, f32[960,2560]{1,0:T(8,128)}, f32[960,960]{1,0:T(8,128)}, f32[320,960]{1,0:T(8,128)}, ...) custom-call(bf16[16,960,640]{2,1,0:T(8,128)(2,1)} %get-tuple-element, ...), custom_call_target="tpu_custom_call" | custom-call | tf_op jit(solution)/shard_map/spread_out/pallas_call | solution.py:1547
  (8 shorter events, 0.1 us)
